TPU v7x, 128 devices: a whole 4x4x4 slice. The times are simulated.
128 devices in a mesh: dp: 8 (over x, z_lo), tensor: 16 (over z_hi, y, core).
Axes of the slice: x: 4, y: 4, z: 4 (z_hi: 2, z_lo: 2; z = z_hi * 2 + z_lo), core: 2. Of those that a mesh axis runs over, the one named last changes fastest.
Arguments:
- tokens: bfloat16 [8192, 2048], P('dp'), may hold values from -6 to 6
- cotangent: bfloat16 [8192, 2048], P('dp', 'tensor'), may hold values from -6 to 6
- expert_ids: int32 [8192, 6], P('dp'), may hold values from 0 to 15, all different within a row
- slot_order: int32 [8, 1024], P('dp'), may hold values from 0 to 1023, each once within a row
- image_starts: int32 [8, 2], P('dp'), may hold values from 0 to 768, as said below
- norm1_gain: float32 [2048], replicated, may hold values from 0.5 to 1.5
- w_query: bfloat16 [2048, 3072], P(None, 'tensor'), may hold values from -0.125 to 0.125
- w_latent: bfloat16 [2048, 576], P(None, 'tensor'), may hold values from -0.125 to 0.125
- latent_gain: float32 [512], replicated, may hold values from 0.5 to 1.5
- w_expand: bfloat16 [512, 4096], P(None, 'tensor'), may hold values from -0.25 to 0.25
- w_output: bfloat16 [2048, 2048], P('tensor'), may hold values from -0.75 to 0.75
- norm2_gain: float32 [2048], replicated, may hold values from 0.5 to 1.5
- w_router: bfloat16 [2048, 16], replicated, may hold values from -0.0625 to 0.0625
- expert_gate: bfloat16 [16, 2048, 1408], P('tensor', None, 'dp'), may hold values from -0.125 to 0.125
- expert_up: bfloat16 [16, 2048, 1408], P('tensor', None, 'dp'), may hold values from -0.125 to 0.125
- expert_down: bfloat16 [16, 2048, 1408], P('tensor', None, 'dp'), may hold values from -0.875 to 0.875
- shared_gate: bfloat16 [2048, 2816], P(None, 'tensor'), may hold values from -0.125 to 0.125
- shared_up: bfloat16 [2048, 2816], P(None, 'tensor'), may hold values from -0.125 to 0.125
- shared_down: bfloat16 [2816, 2048], P('tensor'), may hold values from -0.15625 to 0.15625
Outputs:
- output: bfloat16 [8192, 2048], P('dp', 'tensor')
- tokens_grad: float32 [8192, 2048], P('dp')
- norm1_gain_grad: float32 [2048], replicated
- w_query_grad: float32 [2048, 3072], P(None, 'tensor')
- w_latent_grad: float32 [2048, 576], P(None, 'tensor')
- latent_gain_grad: float32 [512], replicated
- w_expand_grad: float32 [512, 4096], P(None, 'tensor')
- w_output_grad: float32 [2048, 2048], P('tensor')
- norm2_gain_grad: float32 [2048], replicated
- w_router_grad: float32 [2048, 16], replicated
- expert_gate_grad: float32 [16, 2048, 1408], P('tensor', None, 'dp')
- expert_up_grad: float32 [16, 2048, 1408], P('tensor', None, 'dp')
- expert_down_grad: float32 [16, 2048, 1408], P('tensor', None, 'dp')
- shared_gate_grad: float32 [2048, 2816], P(None, 'tensor')
- shared_up_grad: float32 [2048, 2816], P(None, 'tensor')
- shared_down_grad: float32 [2816, 2048], P('tensor')
Inputs may be any that keep to these rules, and one draw needn't show every extreme that they name: `expert_ids`: each row names 6 different experts. `slot_order`: each row is a permutation of the 1024 token indices of its group. `image_starts`: each sequence has 2 image spans of 256 tokens, given by their first positions in increasing order, that do not intersect and lie within the sequence.
All inputs are finite; a program needn't handle non-finite values.
Results may differ from a plain program's by a relative error of at most 0.035.
Values may be sent and summed in bfloat16 or wider, within the bound.
No kernel may reach another device: no remote copies, remote signals or barrier semaphores. Data moves between devices by JAX's collectives and lax.ppermute only.
A program may use at most 320 MiB of HBM per device.

v0:
```python
import math

import jax
import jax.numpy as jnp
from jax import lax
from jax.sharding import PartitionSpec as P

D = 2048
NOPE = 128
ROPE = 64
VDIM = 128
LATENT = 512
TOPK = 6
IMG = 256
SPANS = 2
LEN = 1024
SEQ_DP = 1


epsilon = 1e-06
masked_score = -1e30


def filled_up(lines, peers):
    spare = -len(lines) % peers
    return jnp.pad(lines, [(0, spare)] + [(0, 0)] * (lines.ndim - 1))


def sum_by_parts(x, axis):
    lines = x.reshape(-1, *x.shape[1:][-1:])
    padded = filled_up(lines, lax.axis_size(axis))
    own = lax.psum_scatter(padded, axis, scatter_dimension=0, tiled=True)
    whole = lax.all_gather(own, axis, axis=0, tiled=True)
    return whole[: len(lines)].reshape(x.shape)


def in_one(arrays, axis):
    ends = [0]
    for a in arrays:
        ends.append(ends[-1] + a.size)
    total = lax.psum(jnp.concatenate([a.ravel() for a in arrays]), axis)
    return tuple((total[b:e].reshape(a.shape) for a, b, e in zip(arrays, ends, ends[1:])))


def rms_norm(values, gain_vec):
    inverse = lax.rsqrt(jnp.mean(values * values, axis=-1, keepdims=True) + epsilon)
    return (values * inverse * gain_vec, inverse)


def norm_back(values, inverse, gain_vec, incoming):
    weighted = incoming * gain_vec
    inner_mean = jnp.mean(weighted * values, axis=-1, keepdims=True)
    outgoing = inverse * weighted - values * (inverse * inverse * inverse) * inner_mean
    gain_grad = jnp.sum(incoming * values * inverse, axis=0)
    return (outgoing, gain_grad)


def rotary_tables(length):
    position = jnp.arange(length, dtype=jnp.float32)
    frequency = jnp.exp(
        jnp.arange(ROPE // 2, dtype=jnp.float32) * (-2.0 * math.log(10000.0) / ROPE)
    )
    angles = position[:, None] * frequency[None, :]
    return (jnp.cos(angles), jnp.sin(angles))


def rotate(values, cos_table, sin_table):
    half_size = values.shape[-1] // 2
    lower_half = values[..., :half_size]
    upper_half = values[..., half_size:]
    return jnp.concatenate(
        [
            lower_half * cos_table - upper_half * sin_table,
            upper_half * cos_table + lower_half * sin_table,
        ],
        axis=-1,
    )


def unrotate(values, cos_table, sin_table):
    half_size = values.shape[-1] // 2
    lower_half = values[..., :half_size]
    upper_half = values[..., half_size:]
    return jnp.concatenate(
        [
            lower_half * cos_table + upper_half * sin_table,
            upper_half * cos_table - lower_half * sin_table,
        ],
        axis=-1,
    )


def seq_mask(span_starts):
    position = jnp.arange(LEN, dtype=jnp.int32)
    inside = (position[None, :] >= span_starts[:, None]) & (
        position[None, :] < span_starts[:, None] + IMG
    )
    labels = jnp.sum(
        inside.astype(jnp.int32) * (jnp.arange(SPANS, dtype=jnp.int32)[:, None] + 1), axis=0
    )
    causal = position[None, :] <= position[:, None]
    return causal | (labels[:, None] == labels[None, :]) & (labels[:, None] > 0)


def gated(gate_act, up_act):
    return gate_act * jax.nn.sigmoid(gate_act) * up_act


def gated_back(gate_act, up_act, incoming):
    squashed = jax.nn.sigmoid(gate_act)
    return (
        incoming * up_act * squashed * (1.0 + gate_act * (1.0 - squashed)),
        incoming * gate_act * squashed,
    )


def attend_forward(pieces):
    query_rows, key_rows, values, span_starts = pieces
    scores = jnp.einsum(
        "qhd,khd->hqk", query_rows, key_rows, preferred_element_type=jnp.float32
    ) * (NOPE + ROPE) ** (-0.5)
    scores = jnp.where(seq_mask(span_starts)[None], scores, masked_score)
    largest = jnp.max(scores, axis=-1, keepdims=True)
    raised = jnp.exp(scores - largest)
    row_total = jnp.sum(raised, axis=-1, keepdims=True)
    attn_probs = raised / row_total
    mixed_rows = jnp.einsum(
        "hqk,khd->qhd", attn_probs.astype(jnp.bfloat16), values, preferred_element_type=jnp.float32
    )
    return (mixed_rows.astype(jnp.bfloat16), largest[..., 0] + jnp.log(row_total[..., 0]))


def attend_back(pieces):
    query_rows, key_rows, values, lse_rows, mixed_grad, span_starts = pieces
    scale_soft = (NOPE + ROPE) ** (-0.5)
    scores = (
        jnp.einsum("qhd,khd->hqk", query_rows, key_rows, preferred_element_type=jnp.float32)
        * scale_soft
    )
    scores = jnp.where(seq_mask(span_starts)[None], scores, masked_score)
    attn_probs = jnp.exp(scores - lse_rows[..., None])
    prob_grad = jnp.einsum("qhd,khd->hqk", mixed_grad, values, preferred_element_type=jnp.float32)
    row_inner = jnp.sum(prob_grad * attn_probs, axis=-1, keepdims=True)
    score_grad = (attn_probs * (prob_grad - row_inner)).astype(jnp.bfloat16)
    query_grad = (
        jnp.einsum("hqk,khd->qhd", score_grad, key_rows, preferred_element_type=jnp.float32)
        * scale_soft
    )
    key_grad = (
        jnp.einsum("hqk,qhd->khd", score_grad, query_rows, preferred_element_type=jnp.float32)
        * scale_soft
    )
    value_grad = jnp.einsum(
        "hqk,qhd->khd",
        attn_probs.astype(jnp.bfloat16),
        mixed_grad,
        preferred_element_type=jnp.float32,
    )
    return (query_grad, key_grad, value_grad)


def local(
    tokens,
    cotangent,
    expert_ids,
    slot_order,
    image_starts,
    norm1_gain,
    w_query,
    w_latent,
    latent_gain,
    w_expand,
    w_output,
    norm2_gain,
    w_router,
    expert_gate,
    expert_up,
    expert_down,
    shared_gate,
    shared_up,
    shared_down,
):
    row_count = tokens.shape[0]
    head_count = w_output.shape[0] // VDIM
    expert_count = w_router.shape[1]
    local_experts = expert_gate.shape[0]
    capacity = (5 * TOPK * row_count + 4 * expert_count - 1) // (4 * expert_count)
    width_part = cotangent.shape[1]
    tensor_rank = lax.axis_index("tensor")
    cos_table, sin_table = rotary_tables(LEN)
    cos_rows = jnp.tile(cos_table, (SEQ_DP, 1))
    sin_rows = jnp.tile(sin_table, (SEQ_DP, 1))
    resid = tokens.astype(jnp.float32)
    normed1, inverse1 = rms_norm(resid, norm1_gain)
    normed1 = normed1.astype(jnp.bfloat16)
    query_raw = jnp.dot(normed1, w_query, preferred_element_type=jnp.float32).reshape(
        row_count, head_count, NOPE + ROPE
    )
    latent_piece = jnp.dot(normed1, w_latent, preferred_element_type=jnp.float32).astype(
        jnp.bfloat16
    )
    latent = lax.all_gather(latent_piece, "tensor", axis=1, tiled=True)
    compressed_in = latent[:, :LATENT].astype(jnp.float32)
    compressed, inverse_latent = rms_norm(compressed_in, latent_gain)
    compressed = compressed.astype(jnp.bfloat16)
    expanded = (
        jnp.dot(compressed, w_expand, preferred_element_type=jnp.float32)
        .astype(jnp.bfloat16)
        .reshape(row_count, head_count, NOPE + VDIM)
    )
    query_rows = jnp.concatenate(
        [
            query_raw[..., :NOPE],
            rotate(query_raw[..., NOPE:], cos_rows[:, None, :], sin_rows[:, None, :]),
        ],
        axis=-1,
    ).astype(jnp.bfloat16)
    key_rope = rotate(latent[:, LATENT:].astype(jnp.float32), cos_rows, sin_rows).astype(
        jnp.bfloat16
    )
    key_rows = jnp.concatenate([expanded[..., :NOPE], key_rope[:, None, :]], axis=-1)
    values = expanded[..., NOPE:]
    query_seq = query_rows.reshape(SEQ_DP, LEN, head_count, NOPE + ROPE)
    key_seq = key_rows.reshape(SEQ_DP, LEN, head_count, NOPE + ROPE)
    value_seq = values.reshape(SEQ_DP, LEN, head_count, VDIM)
    mixed_rows, lse_rows = lax.map(attend_forward, (query_seq, key_seq, value_seq, image_starts))
    mixed_flat = mixed_rows.reshape(row_count, head_count * VDIM)
    attention = sum_by_parts(
        jnp.dot(mixed_flat, w_output, preferred_element_type=jnp.float32).astype(jnp.bfloat16),
        "tensor",
    ).astype(jnp.float32)
    hidden_res = resid + attention
    normed2, inverse2 = rms_norm(hidden_res, norm2_gain)
    normed2 = normed2.astype(jnp.bfloat16)
    logits = jnp.dot(normed2, w_router, preferred_element_type=jnp.float32)
    router_probs = jax.nn.softmax(logits, axis=-1)
    chosen = jnp.any(
        expert_ids[:, :, None] == jnp.arange(expert_count, dtype=jnp.int32)[None, None, :], axis=1
    ).astype(jnp.int32)
    priority = slot_order[0]
    ranked = chosen[priority]
    before = jnp.cumsum(ranked, axis=0) - ranked
    slot_rank = jnp.zeros_like(chosen).at[priority].set(before)
    first_expert = tensor_rank * local_experts
    own_rank = lax.dynamic_slice_in_dim(slot_rank, first_expert, local_experts, 1)
    own_chosen = lax.dynamic_slice_in_dim(chosen, first_expert, local_experts, 1)
    own_probs = lax.dynamic_slice_in_dim(router_probs, first_expert, local_experts, 1)
    kept_mask = (own_chosen > 0) & (own_rank < capacity)
    target = jnp.where(kept_mask, own_rank, capacity)
    token_index = jnp.arange(row_count, dtype=jnp.int32)[:, None]
    expert_index = jnp.broadcast_to(
        jnp.arange(local_experts, dtype=jnp.int32)[None, :], (row_count, local_experts)
    )
    slot_table = (
        jnp.full((local_experts, capacity + 1), row_count, jnp.int32)
        .at[expert_index, target]
        .set(token_index)[:, :capacity]
    )
    flat_table = slot_table.reshape(-1)
    padded_in = jnp.concatenate([normed2, jnp.zeros((1, D), jnp.bfloat16)], axis=0)
    slot_inputs = padded_in[slot_table]
    padded_probs = jnp.concatenate([own_probs, jnp.zeros((1, local_experts), jnp.float32)], axis=0)
    slot_gates = padded_probs[slot_table, jnp.arange(local_experts, dtype=jnp.int32)[:, None]]
    gate_full, up_full, down_full = (
        lax.all_gather(expert_gate, "dp", axis=2, tiled=True),
        lax.all_gather(expert_up, "dp", axis=2, tiled=True),
        lax.all_gather(expert_down, "dp", axis=2, tiled=True),
    )
    gate_act = jnp.einsum(
        "esd,edf->esf", slot_inputs, gate_full, preferred_element_type=jnp.float32
    )
    up_act = jnp.einsum("esd,edf->esf", slot_inputs, up_full, preferred_element_type=jnp.float32)
    expert_hidden = gated(gate_act, up_act).astype(jnp.bfloat16)
    slot_terms = jnp.einsum(
        "esf,edf->esd", expert_hidden, down_full, preferred_element_type=jnp.float32
    )
    slot_out = slot_terms.astype(jnp.bfloat16)
    weighted_out = (slot_out.astype(jnp.float32) * slot_gates[:, :, None]).reshape(-1, D)
    routed = jnp.zeros((row_count + 1, D), jnp.float32).at[flat_table].add(weighted_out)[:row_count]
    shared_gate_act = jnp.dot(normed2, shared_gate, preferred_element_type=jnp.float32)
    shared_up_act = jnp.dot(normed2, shared_up, preferred_element_type=jnp.float32)
    shared_hidden = gated(shared_gate_act, shared_up_act).astype(jnp.bfloat16)
    branch = routed + jnp.dot(shared_hidden, shared_down, preferred_element_type=jnp.float32)
    branch_sum = lax.psum_scatter(
        branch.astype(jnp.bfloat16), "tensor", scatter_dimension=1, tiled=True
    ).astype(jnp.float32)
    own_resid = lax.dynamic_slice_in_dim(hidden_res, tensor_rank * width_part, width_part, 1)
    output = (own_resid + branch_sum).astype(jnp.bfloat16)
    out_grad = lax.all_gather(cotangent, "tensor", axis=1, tiled=True)
    grad_rows = out_grad.astype(jnp.float32)
    shared_hidden_grad = jnp.einsum(
        "td,fd->tf", out_grad, shared_down, preferred_element_type=jnp.float32
    )
    shared_gate_grad_act, shared_up_grad_act = gated_back(
        shared_gate_act, shared_up_act, shared_hidden_grad
    )
    shared_gate_grad_act = shared_gate_grad_act.astype(jnp.bfloat16)
    shared_up_grad_act = shared_up_grad_act.astype(jnp.bfloat16)
    shared_down_grad = jnp.einsum(
        "tf,td->fd", shared_hidden, out_grad, preferred_element_type=jnp.float32
    )
    shared_gate_grad = jnp.einsum(
        "td,tf->df", normed2, shared_gate_grad_act, preferred_element_type=jnp.float32
    )
    shared_up_grad = jnp.einsum(
        "td,tf->df", normed2, shared_up_grad_act, preferred_element_type=jnp.float32
    )
    padded_grad = jnp.concatenate([grad_rows, jnp.zeros((1, D), jnp.float32)], axis=0)
    slot_grad_rows = padded_grad[slot_table]
    gate_grad_slots = jnp.sum(slot_grad_rows * slot_out.astype(jnp.float32), axis=-1)
    slot_out_grad = (slot_grad_rows * slot_gates[:, :, None]).astype(jnp.bfloat16)
    hidden_grad = jnp.einsum(
        "esd,edf->esf", slot_out_grad, down_full, preferred_element_type=jnp.float32
    )
    gate_grad_act, up_grad_act = gated_back(gate_act, up_act, hidden_grad)
    gate_grad_act = gate_grad_act.astype(jnp.bfloat16)
    up_grad_act = up_grad_act.astype(jnp.bfloat16)
    gate_w_grad = jnp.einsum(
        "esd,esf->edf", slot_inputs, gate_grad_act, preferred_element_type=jnp.float32
    )
    up_w_grad = jnp.einsum(
        "esd,esf->edf", slot_inputs, up_grad_act, preferred_element_type=jnp.float32
    )
    down_w_grad = jnp.einsum(
        "esd,esf->edf", slot_out_grad, expert_hidden, preferred_element_type=jnp.float32
    )
    input_terms = jnp.einsum(
        "esf,edf->esd", gate_grad_act, gate_full, preferred_element_type=jnp.float32
    ) + jnp.einsum("esf,edf->esd", up_grad_act, up_full, preferred_element_type=jnp.float32)
    expert_gate_grad, expert_up_grad, expert_down_grad = (
        lax.psum_scatter(
            gate_w_grad.astype(jnp.bfloat16), "dp", scatter_dimension=2, tiled=True
        ).astype(jnp.float32),
        lax.psum_scatter(
            up_w_grad.astype(jnp.bfloat16), "dp", scatter_dimension=2, tiled=True
        ).astype(jnp.float32),
        lax.psum_scatter(
            down_w_grad.astype(jnp.bfloat16), "dp", scatter_dimension=2, tiled=True
        ).astype(jnp.float32),
    )
    normed2_grad = (
        jnp.zeros((row_count + 1, D), jnp.float32)
        .at[flat_table]
        .add(input_terms.reshape(-1, D))[:row_count]
    )
    normed2_grad = normed2_grad + jnp.einsum(
        "tf,df->td", shared_gate_grad_act, shared_gate, preferred_element_type=jnp.float32
    )
    normed2_grad = normed2_grad + jnp.einsum(
        "tf,df->td", shared_up_grad_act, shared_up, preferred_element_type=jnp.float32
    )
    expert_cols = jnp.broadcast_to(
        (first_expert + jnp.arange(local_experts, dtype=jnp.int32))[:, None],
        (local_experts, capacity),
    ).reshape(-1)
    gate_grad_rows = (
        jnp.zeros((row_count + 1, expert_count), jnp.float32)
        .at[flat_table, expert_cols]
        .add(gate_grad_slots.reshape(-1))[:row_count]
    )
    normed2_sum, gate_grads = tuple(
        (
            part.astype(jnp.float32)
            for part in in_one(
                (normed2_grad.astype(jnp.bfloat16), gate_grad_rows.astype(jnp.bfloat16)), "tensor"
            )
        )
    )
    logits_grad = (
        router_probs * (gate_grads - jnp.sum(router_probs * gate_grads, axis=-1, keepdims=True))
    ).astype(jnp.bfloat16)
    router_grad = jnp.einsum("td,te->de", normed2, logits_grad, preferred_element_type=jnp.float32)
    normed2_sum = normed2_sum + jnp.einsum(
        "te,de->td", logits_grad, w_router, preferred_element_type=jnp.float32
    )
    resid_grad_two, norm2_gain_grad = norm_back(hidden_res, inverse2, norm2_gain, normed2_sum)
    hidden_res_grad = grad_rows + resid_grad_two
    attention_grad = hidden_res_grad.astype(jnp.bfloat16)
    output_w_grad = jnp.einsum(
        "tv,td->vd", mixed_flat, attention_grad, preferred_element_type=jnp.float32
    )
    mixed_grad = jnp.einsum(
        "td,vd->tv", attention_grad, w_output, preferred_element_type=jnp.float32
    ).astype(jnp.bfloat16)
    query_grad, key_grad, value_grad = lax.map(
        attend_back,
        (
            query_seq,
            key_seq,
            value_seq,
            lse_rows,
            mixed_grad.reshape(SEQ_DP, LEN, head_count, VDIM),
            image_starts,
        ),
    )
    query_grad = query_grad.reshape(row_count, head_count, NOPE + ROPE)
    key_grad = key_grad.reshape(row_count, head_count, NOPE + ROPE)
    value_grad = value_grad.reshape(row_count, head_count, VDIM)
    query_raw_grad = jnp.concatenate(
        [
            query_grad[..., :NOPE],
            unrotate(query_grad[..., NOPE:], cos_rows[:, None, :], sin_rows[:, None, :]),
        ],
        axis=-1,
    )
    query_raw_grad = query_raw_grad.reshape(row_count, head_count * (NOPE + ROPE)).astype(
        jnp.bfloat16
    )
    query_w_grad = jnp.einsum(
        "td,tq->dq", normed1, query_raw_grad, preferred_element_type=jnp.float32
    )
    normed1_grad = jnp.einsum(
        "tq,dq->td", query_raw_grad, w_query, preferred_element_type=jnp.float32
    )
    expanded_grad = (
        jnp.concatenate([key_grad[..., :NOPE], value_grad], axis=-1)
        .reshape(row_count, head_count * (NOPE + VDIM))
        .astype(jnp.bfloat16)
    )
    expand_w_grad = jnp.einsum(
        "tc,tk->ck", compressed, expanded_grad, preferred_element_type=jnp.float32
    )
    compressed_grad = jnp.einsum(
        "tk,ck->tc", expanded_grad, w_expand, preferred_element_type=jnp.float32
    )
    latent_head_grad, latent_gain_part = norm_back(
        compressed_in, inverse_latent, latent_gain, compressed_grad
    )
    rope_grad = unrotate(jnp.sum(key_grad[..., NOPE:], axis=1), cos_rows, sin_rows)
    latent_grad = lax.psum_scatter(
        jnp.concatenate([latent_head_grad, rope_grad], axis=-1).astype(jnp.bfloat16),
        "tensor",
        scatter_dimension=1,
        tiled=True,
    )
    latent_w_grad = jnp.einsum(
        "td,tl->dl", normed1, latent_grad, preferred_element_type=jnp.float32
    )
    normed1_grad = normed1_grad + jnp.einsum(
        "tl,dl->td", latent_grad, w_latent, preferred_element_type=jnp.float32
    )
    normed1_sum, latent_gain_grad = (
        lax.psum(normed1_grad.astype(jnp.bfloat16), "tensor").astype(jnp.float32),
        lax.psum(latent_gain_part.astype(jnp.bfloat16), "tensor").astype(jnp.float32),
    )
    resid_grad_one, norm1_gain_grad = norm_back(resid, inverse1, norm1_gain, normed1_sum)
    tokens_grad = hidden_res_grad + resid_grad_one
    summed = (
        lax.psum(norm1_gain_grad.astype(jnp.bfloat16), "dp").astype(jnp.float32),
        lax.psum(query_w_grad.astype(jnp.bfloat16), "dp").astype(jnp.float32),
        lax.psum(latent_w_grad.astype(jnp.bfloat16), "dp").astype(jnp.float32),
        lax.psum(latent_gain_grad.astype(jnp.bfloat16), "dp").astype(jnp.float32),
        lax.psum(expand_w_grad.astype(jnp.bfloat16), "dp").astype(jnp.float32),
        lax.psum(output_w_grad.astype(jnp.bfloat16), "dp").astype(jnp.float32),
        lax.psum(norm2_gain_grad.astype(jnp.bfloat16), "dp").astype(jnp.float32),
        lax.psum(router_grad.astype(jnp.bfloat16), "dp").astype(jnp.float32),
        lax.psum(shared_gate_grad.astype(jnp.bfloat16), "dp").astype(jnp.float32),
        lax.psum(shared_up_grad.astype(jnp.bfloat16), "dp").astype(jnp.float32),
        lax.psum(shared_down_grad.astype(jnp.bfloat16), "dp").astype(jnp.float32),
    )
    return (
        output,
        tokens_grad,
        summed[0],
        summed[1],
        summed[2],
        summed[3],
        summed[4],
        summed[5],
        summed[6],
        summed[7],
        expert_gate_grad,
        expert_up_grad,
        expert_down_grad,
        summed[8],
        summed[9],
        summed[10],
    )


def solution(mesh):
    in_specs = (
        P("dp", None),
        P("dp", "tensor"),
        P("dp", None),
        P("dp", None),
        P("dp", None),
        P(),
        P(None, "tensor"),
        P(None, "tensor"),
        P(),
        P(None, "tensor"),
        P("tensor", None),
        P(),
        P(),
        P("tensor", None, "dp"),
        P("tensor", None, "dp"),
        P("tensor", None, "dp"),
        P(None, "tensor"),
        P(None, "tensor"),
        P("tensor", None),
    )
    out_specs = (
        P("dp", "tensor"),
        P("dp", None),
        P(),
        P(None, "tensor"),
        P(None, "tensor"),
        P(),
        P(None, "tensor"),
        P("tensor", None),
        P(),
        P(),
        P("tensor", None, "dp"),
        P("tensor", None, "dp"),
        P("tensor", None, "dp"),
        P(None, "tensor"),
        P(None, "tensor"),
        P("tensor", None),
    )
    return jax.shard_map(local, mesh=mesh, in_specs=in_specs, out_specs=out_specs, check_vma=False)
```

profile of v0, /device:TPU:1, one launch (start us, length us, event | category | flops | bytes accessed | tf_op | source)
XLA Modules:
  0.0 1718.2 jit_solution(17223306693518172735)
XLA Ops:
  20.7 45.2 %all-gather.18.cloned.1.call-done = bf16[16,36,1024]{2,1,0:T(8,128)(2,1)} async-done(((bf16[1,36,1024]{2,1,0:T(8,128)(2,1)}), bf16[16,36,1024]{2,1,0:T(8,128)(2,1)}) %all-gather.18.cloned.1.call-update) | async-done | bytes 1179664 | tf_op jit(solution)/shard_map/all_gather | solution.py:202
  78.9 76.6 %reduce-scatter.16.cloned.1.call-done = bf16[64,2048]{1,0:T(8,128)(2,1)} async-done(((bf16[1024,2048]{1,0:T(8,128)(2,1)}), bf16[64,2048]{1,0:T(8,128)(2,1)}) %reduce-scatter.16.cloned.1.call-update) | async-done | bytes 262160 | tf_op jit(solution)/shard_map/reduce_scatter | solution.py:32
  175.1 42.4 %all-gather.16.cloned.1.call-done = bf16[1024,2048]{1,0:T(8,128)(2,1)} async-done(((bf16[1024,128]{1,0:T(8,128)(2,1)}), bf16[1024,2048]{1,0:T(8,128)(2,1)}) %all-gather.16.cloned.1.call-update) | async-done | bytes 4194320 | tf_op jit(solution)/shard_map/all_gather | solution.py:289
  224.1 8.8 gather_fusion.3
  237.5 37.3 %all-gather.8.cloned.1.call-done = bf16[1024,2048]{1,0:T(8,128)(2,1)} async-done(((bf16[64,2048]{1,0:T(8,128)(2,1)}), bf16[1024,2048]{1,0:T(8,128)(2,1)}) %all-gather.8.cloned.1.call-update) | async-done | bytes 4194320 | tf_op jit(solution)/shard_map/all_gather | solution.py:33
  299.5 12.2 gather_fusion.2
  316.5 77.3 %all-gather.10.cloned.1.call-done = bf16[1,2048,1408]{1,2,0:T(8,128)(2,1)} async-done(((bf16[1,2048,176]{1,2,0:T(8,128)(2,1)}), bf16[1,2048,1408]{1,2,0:T(8,128)(2,1)}) %all-gather.10.cloned.1.call-update) | async-done | bytes 5767184 | tf_op jit(solution)/shard_map/all_gather | solution.py:265
  401.2 114.5 %all-gather.12.cloned.1.call-done = bf16[1,2048,1408]{1,2,0:T(8,128)(2,1)} async-done(((bf16[1,2048,176]{1,2,0:T(8,128)(2,1)}), bf16[1,2048,1408]{1,2,0:T(8,128)(2,1)}) %all-gather.12.cloned.1.call-update) | async-done | bytes 5767184 | tf_op jit(solution)/shard_map/all_gather | solution.py:266
  523.1 114.6 %all-gather.14.cloned.1.call-done = bf16[1,2048,1408]{1,2,0:T(8,128)(2,1)} async-done(((bf16[1,2048,176]{1,2,0:T(8,128)(2,1)}), bf16[1,2048,1408]{1,2,0:T(8,128)(2,1)}) %all-gather.14.cloned.1.call-update) | async-done | bytes 5767184 | tf_op jit(solution)/shard_map/all_gather | solution.py:267
  637.7 11.1 multiply_convert_fusion.3
  652.4 26.0 %scatter_fusion = f32[1025,16]{0,1:T(8,128)S(1)} fusion(f32[1025,16]{0,1:T(8,128)S(1)} %broadcast_in_dim.67, s32[480]{0:T(512)S(1)} %bitcast.207, f32[480]{0:T(512)S(1)} %get-tuple-element.192), kind=kCustom, calls=%fused_computation.7 | custom fusion | flops 480 | bytes 9600 | tf_op jit(solution)/shard_map/scatter-add | solution.py:359
  702.1 13.7 scatter_custom_fusion.2
  724.7 8.9 pad_maximum_fusion
  735.5 10.6 scatter_custom_fusion.1
  770.1 115.0 %all-reduce.13.cloned.1.call-done = bf16[2113536]{0:T(1024)(128)(2,1)} async-done(((bf16[2113536]{0:T(1024)(128)(2,1)}), bf16[2113536]{0:T(1024)(128)(2,1)}) %all-reduce.13.cloned.1.call-update) | async-done | bytes 4227088 | tf_op jit(solution)/shard_map/psum | solution.py:41
  890.4 9.3 reshape.596
  900.9 11.1 multiply_reduce_fusion
  913.5 8.4 subtract_add_fusion
  933.8 42.1 %fusion = bf16[1024,40]{0,1:T(8,128)(2,1)S(1)} fusion(bf16[1024,576]{0,1:T(8,128)(2,1)S(1)} %pad_maximum_fusion.1), kind=kCustom, calls=%all-reduce-scatter | all-reduce-scatter fusion | flops 655361 | bytes 1262080
  1009.5 27.9 %copy.102 = bf16[1,2048,1408]{1,0,2:T(2,128)(2,1)} copy(bf16[1,2048,1408]{2,1,0:T(8,128)(2,1)} %fusion.14) | data formatting | bytes 11534336
  1037.4 10.5 copy.117
  1054.6 27.9 %copy.104 = bf16[1,2048,1408]{1,0,2:T(2,128)(2,1)} copy(bf16[1,2048,1408]{2,1,0:T(8,128)(2,1)} %fusion.15) | data formatting | bytes 11534336
  1082.5 10.5 copy.116
  1102.6 28.0 %copy.106 = bf16[1,2048,1408]{1,0,2:T(2,128)(2,1)} copy(bf16[1,2048,1408]{2,1,0:T(8,128)(2,1)} %fusion.16) | data formatting | bytes 11534336
  1130.5 10.5 copy.115
  1141.1 37.8 %psum.103 = bf16[512]{0:T(512)(128)(2,1)S(1)} all-reduce(bf16[512]{0:T(512)(128)(2,1)S(1)} %get-tuple-element.151), channel_id=1, replica_groups=mesh['dp'=8,'tensor'=16] {'tensor'}, use_global_device_ids=true, to_apply=%region_32.33 | all-reduce | flops 512 | bytes 2048 | tf_op jit(solution)/shard_map/psum | solution.py:444
  1194.5 140.8 %all-reduce.15.cloned.1.call-done = bf16[1024,2048]{1,0:T(8,128)(2,1)} async-done(((bf16[1024,2048]{1,0:T(8,128)(2,1)}), bf16[1024,2048]{1,0:T(8,128)(2,1)}) %all-reduce.15.cloned.1.call-update) | async-done | bytes 4194320 | tf_op jit(solution)/shard_map/psum | solution.py:443
  1340.9 22.3 %all-reduce.7 = (bf16[2048]{0:T(1024)(128)(2,1)S(1)}, bf16[512]{0:T(512)(128)(2,1)S(1)}, bf16[2048]{0:T(1024)(128)(2,1)S(1)}) all-reduce(bf16[2048]{0:T(1024)(128)(2,1)S(1)} %get-tuple-element.149, bf16[512]{0:T(512)(128)(2,1)S(1)} %psum.103, bf16[2048]{0:T(1024)(128)(2,1)S(1)} %get-tuple-element.147), channel_id=1, replica_groups=mesh['dp'=8,'tensor'=16] {'dp'}, use_global_device_ids=true, to_apply=%region_28.29 | all-reduce | flops 4608 | bytes 18432 | tf_op jit(solution)/shard_map/psum | solution.py:449
  1365.1 9.5 fusion.3
  1374.6 85.6 %reduce-scatter.20.cloned.1.call-done = bf16[176,2048]{1,0:T(8,128)(2,1)} async-done(((bf16[1408,2048]{1,0:T(8,128)(2,1)}), bf16[176,2048]{1,0:T(8,128)(2,1)}) %reduce-scatter.20.cloned.1.call-update) | async-done | bytes 720912
  1465.5 117.2 %reduce-scatter.22.cloned.1.call-done = bf16[176,2048]{1,0:T(8,128)(2,1)} async-done(((bf16[1408,2048]{1,0:T(8,128)(2,1)}), bf16[176,2048]{1,0:T(8,128)(2,1)}) %reduce-scatter.22.cloned.1.call-update) | async-done | bytes 720912
  1588.0 118.0 %reduce-scatter.24.cloned.1.call-done = bf16[176,2048]{1,0:T(8,128)(2,1)} async-done(((bf16[1408,2048]{1,0:T(8,128)(2,1)}), bf16[176,2048]{1,0:T(8,128)(2,1)}) %reduce-scatter.24.cloned.1.call-update) | async-done | bytes 720912
  (336 shorter events, 270.2 us)
Async XLA Ops:
  7.2 58.7 %all-gather.18.cloned.1.call-start = ((), (), s32[]{:S(2)}) async-start(), calls=%async_computation.13 | async-start | bytes 1392640 | tf_op jit(solution)/shard_map/all_gather | solution.py:202
  16.1 139.3 %reduce-scatter.16.cloned.1.call-start = ((), (), s32[]{:S(2)}) async-start(), calls=%async_computation.5 | async-start | bytes 4456448 | tf_op jit(solution)/shard_map/reduce_scatter | solution.py:32
  16.2 51.5 %copy-start.61 = (f32[32]{0:T(128)}, f32[32]{0:T(128)S(1)}, u32[]{:S(2)}) copy-start(f32[32]{0:T(128)S(1)} %multiply_exponential_fusion) | copy-start | bytes 388
  16.3 52.6 %copy-start.64 = (f32[512]{0:T(512)S(1)}, f32[512]{0:T(512)}, u32[]{:S(2)}) copy-start(f32[512]{0:T(512)} %param.27) | copy-start | bytes 6148
  16.3 52.5 %copy-start.71 = (bf16[512,256]{1,0:T(8,128)(2,1)S(1)}, bf16[512,256]{1,0:T(8,128)(2,1)}, u32[]{:S(2)}) copy-start(bf16[512,256]{1,0:T(8,128)(2,1)} %param.28) | copy-start | bytes 786436
  20.7 48.8 %copy-start.52 = (bf16[1024,32]{0,1:T(8,128)(2,1)}, bf16[1024,32]{0,1:T(8,128)(2,1)S(1)}, u32[]{:S(2)}) copy-start(bf16[1024,32]{0,1:T(8,128)(2,1)S(1)} %get-tuple-element.176) | copy-start | bytes 196612
  20.7 48.8 %copy-start.54 = (bf16[1024,32]{0,1:T(8,128)(2,1)}, bf16[1024,32]{0,1:T(8,128)(2,1)S(1)}, u32[]{:S(2)}) copy-start(bf16[1024,32]{0,1:T(8,128)(2,1)S(1)} %get-tuple-element.177) | copy-start | bytes 196612
  20.7 50.3 %copy-start.36 = (bf16[1024,128]{0,1:T(8,128)(2,1)}, bf16[1024,128]{0,1:T(8,128)(2,1)S(1)}, u32[]{:S(2)}) copy-start(bf16[1024,128]{0,1:T(8,128)(2,1)S(1)} %fusion.84) | copy-start | bytes 786436
  78.0 79.6 %copy-start.56 = (s32[1024,6]{0,1:T(8,128)S(1)}, s32[1024,6]{0,1:T(8,128)}, u32[]{:S(2)}) copy-start(s32[1024,6]{0,1:T(8,128)} %param.21) | copy-start | bytes 73732
  78.0 80.0 %copy-start.63 = (s32[1,1024]{1,0:T(1,128)S(1)}, s32[1,1024]{1,0:T(1,128)}, u32[]{:S(2)}) copy-start(s32[1,1024]{1,0:T(1,128)} %param.22) | copy-start | bytes 12292
  78.1 139.5 %all-gather.16.cloned.1.call-start = ((), (), s32[]{:S(2)}) async-start(), calls=%async_computation.10 | async-start | bytes 4456448 | tf_op jit(solution)/shard_map/all_gather | solution.py:289
  78.8 195.9 %all-gather.8.cloned.1.call-start = ((), (), s32[]{:S(2)}) async-start(), calls=%async_computation.6 | async-start | bytes 4456448 | tf_op jit(solution)/shard_map/all_gather | solution.py:33
  155.5 238.3 %all-gather.10.cloned.1.call-start = ((), (), s32[]{:S(2)}) async-start(), calls=%async_computation.7 | async-start | bytes 6488064 | tf_op jit(solution)/shard_map/all_gather | solution.py:265
  156.0 359.6 %all-gather.12.cloned.1.call-start = ((), (), s32[]{:S(2)}) async-start(), calls=%async_computation.8 | async-start | bytes 6488064 | tf_op jit(solution)/shard_map/all_gather | solution.py:266
  156.6 481.1 %all-gather.14.cloned.1.call-start = ((), (), s32[]{:S(2)}) async-start(), calls=%async_computation.9 | async-start | bytes 6488064 | tf_op jit(solution)/shard_map/all_gather | solution.py:267
  157.4 727.8 %all-reduce.13.cloned.1.call-start = ((), (), s32[]{:S(2)}) async-start(), calls=%async_computation.11 | async-start | bytes 8454144 | tf_op jit(solution)/shard_map/psum | solution.py:41
  237.5 42.3 %copy-start.42 = (f32[2048]{0:T(1024)S(1)}, f32[2048]{0:T(1024)}, u32[]{:S(2)}) copy-start(f32[2048]{0:T(1024)} %param.30) | copy-start | bytes 24580
  295.3 220.4 %copy-start.21 = (bf16[480,2048]{1,0:T(8,128)(2,1)}, bf16[480,2048]{1,0:T(8,128)(2,1)S(1)}, u32[]{:S(2)}) copy-start(bf16[480,2048]{1,0:T(8,128)(2,1)S(1)} %gather_fusion.1) | copy-start | bytes 5898244
  684.3 12.6 slice-start
  733.6 445.2 %reduce-scatter.18.cloned.1.call-start = ((), (), s32[]{:S(2)}) async-start(), calls=%async_computation.14 | async-start | bytes 4456448
  765.7 416.1 %all-reduce.17.cloned.1.call-start = ((), (), s32[]{:S(2)}) async-start(), calls=%async_computation.18 | async-start | bytes 7929856 | tf_op jit(solution)/shard_map/psum | solution.py:450
  932.6 46.3 %copy-start.49 = (bf16[1024,1,32]{0,2,1:T(8,128)(2,1)S(1)}, bf16[1024,1,32]{0,2,1:T(8,128)(2,1)}, u32[]{:S(2)}) copy-start(bf16[1024,1,32]{0,2,1:T(8,128)(2,1)} %copy-done.48) | copy-start | bytes 196612
  932.6 46.3 %copy-start.51 = (bf16[1024,1,32]{0,2,1:T(8,128)(2,1)S(1)}, bf16[1024,1,32]{0,2,1:T(8,128)(2,1)}, u32[]{:S(2)}) copy-start(bf16[1024,1,32]{0,2,1:T(8,128)(2,1)} %copy-done.50) | copy-start | bytes 196612
  976.0 16.6 collective-permute-start
  981.3 11.2 collective-permute-start.1
  996.6 338.7 %all-reduce.15.cloned.1.call-start = ((), (), s32[]{:S(2)}) async-start(), calls=%async_computation.12 | async-start | bytes 8388608 | tf_op jit(solution)/shard_map/psum | solution.py:443
  1001.3 458.9 %reduce-scatter.20.cloned.1.call-start = ((), (), s32[]{:S(2)}) async-start(), calls=%async_computation.15 | async-start | bytes 6488064
  1047.9 534.8 %reduce-scatter.22.cloned.1.call-start = ((), (), s32[]{:S(2)}) async-start(), calls=%async_computation.16 | async-start | bytes 6488064
  1093.0 612.9 %reduce-scatter.24.cloned.1.call-start = ((), (), s32[]{:S(2)}) async-start(), calls=%async_computation.17 | async-start | bytes 6488064
  1187.9 147.4 %copy-start.44 = (f32[2048]{0:T(1024)S(1)}, f32[2048]{0:T(1024)}, u32[]{:S(2)}) copy-start(f32[2048]{0:T(1024)} %param.24) | copy-start | bytes 24580
  1187.9 147.4 %copy-start.46 = (f32[1024]{0:T(1024)S(1)}, f32[1024]{0:T(1024)}, u32[]{:S(2)}) copy-start(f32[1024]{0:T(1024)} %copy-done.45) | copy-start | bytes 12292
  1194.5 170.6 %copy-start.57 = (f32[1024]{0:T(1024)S(1)}, f32[1024]{0:T(1024)}, u32[]{:S(2)}) copy-start(f32[1024]{0:T(1024)} %get-tuple-element.182) | copy-start | bytes 12292
  (63 other events, 290.6 us)
Sparse Core Ops, SparseCore 0:
  16.2 49.6 all-gather.17
  78.2 77.1 reduce-scatter.15
  158.0 59.5 all-gather.15
  220.1 54.5 all-gather.7
  276.3 117.4 all-gather.9
  395.4 120.2 all-gather.11
  517.4 120.2 all-gather.13
  733.7 151.3 all-reduce.12
  889.7 81.8 reduce-scatter.17
  996.7 183.7 all-reduce.16
  1183.2 152.0 all-reduce.14
  1337.7 122.4 reduce-scatter.19
  1462.7 119.9 reduce-scatter.21
  1585.1 120.8 reduce-scatter.23
where the time goes:
time: 1730 us; the launch traced here: 1720 us
  waiting for transfers between devices  1090 us (63%)
  local copies, waits for them, and re-layouts  216 us (12%)
  matrix products  161 us (9%)
  other arithmetic  129 us (7%)
  blocking collectives  102 us (6%)
    unnamed x20, waiting for transfers between devices  323 us
    unnamed x181, local copies, waits for them, and re-layouts  161 us
    psum x1, waiting for transfers between devices, local(): lax.psum(normed1_grad.astype(jnp.bfloat16), 'tensor').astype(jnp.float32)  141 us
    psum x1, waiting for transfers between devices, in_one(): total = lax.psum(jnp.concatenate([a.ravel() for a in arrays]), axis)  115 us
    all_gather x1, waiting for transfers between devices, local(): lax.all_gather(expert_down, 'dp', axis=2, tiled=True)  115 us
    all_gather x1, waiting for transfers between devices, local(): lax.all_gather(expert_up, 'dp', axis=2, tiled=True)  114 us
    all_gather x1, waiting for transfers between devices, local(): lax.all_gather(expert_gate, 'dp', axis=2, tiled=True)  77.3 us
    reduce_scatter x1, waiting for transfers between devices, sum_by_parts(): own = lax.psum_scatter(padded, axis, scatter_dimension=0, tiled=True)  76.6 us
  transfers between devices with their start and end apart: 16, of which 12 were waited for; matrix products, arithmetic and copies ran while one was open for 24% of the time, Pallas kernels for 0%

commit v1 on v0

v1 whole, which is shorter than its diff:
```python
import functools
import math

import jax
import jax.numpy as jnp
from jax import lax
from jax.experimental import pallas as pl
from jax.experimental.pallas import tpu as pltpu
from jax.sharding import PartitionSpec as P

D = 2048
NOPE = 128
ROPE = 64
VDIM = 128
LATENT = 512
TOPK = 6
EXPERTS = 16
IMG = 256
SPANS = 2
LEN = 1024
CAP = 480
FS = 176
LW = 36
LP = 48
LX = 640
RB = 64
PW = D + 128
BF = jnp.bfloat16
F32 = jnp.float32
EPS = 1e-06
MASKED = -1e30
SCALE = (NOPE + ROPE) ** (-0.5)
MB = 1024 * 1024

NN = (((1,), (0,)), ((), ()))
NT = (((1,), (1,)), ((), ()))
TN = (((0,), (0,)), ((), ()))


def dot(a, b, dims=NN):
    return lax.dot_general(a, b, dims, preferred_element_type=F32)


VM = pl.BlockSpec(memory_space=pltpu.VMEM)
SM = pl.BlockSpec(memory_space=pltpu.SMEM)


def whole(kernel, outs, ins, limit, flops=0):
    arrays = [i[0] if isinstance(i, tuple) else i for i in ins]
    specs = [i[1] if isinstance(i, tuple) else VM for i in ins]
    moved = sum(a.size * a.dtype.itemsize for a in arrays)
    moved += sum(math.prod(o.shape) * o.dtype.itemsize for o in outs)
    return pl.pallas_call(
        kernel,
        out_shape=outs,
        in_specs=specs,
        out_specs=[VM] * len(outs),
        compiler_params=pltpu.CompilerParams(vmem_limit_bytes=limit * MB),
        cost_estimate=pl.CostEstimate(flops=flops, bytes_accessed=moved, transcendentals=0),
    )(*arrays)


def sds(shape, dtype):
    return jax.ShapeDtypeStruct(shape, dtype)


def recv_t(a, zh=0, y=0, c=0):
    pairs = []
    for i in range(16):
        z, r, k = i // 8, i // 2 % 4, i % 2
        pairs.append((((z + zh) % 2) * 8 + ((r + y) % 4) * 2 + (k + c) % 2, i))
    return lax.ppermute(a, "tensor", pairs)


def recv_d(a, x=0, z=0):
    pairs = []
    for i in range(8):
        pairs.append((((i // 2 + x) % 4) * 2 + (i % 2 + z) % 2, i))
    return lax.ppermute(a, "dp", pairs)


def gather_t(a, axis=0):
    z0 = recv_t(a, zh=1)
    y1 = recv_t(a, y=1)
    y3 = recv_t(a, y=-1)
    y2 = recv_t(a, y=2)
    z1 = recv_t(z0, y=1)
    z3 = recv_t(z0, y=-1)
    z2 = recv_t(y2, zh=1)
    half = jnp.concatenate([a, y1, y2, y3, z0, z1, z2, z3], axis=axis)
    return half, recv_t(half, c=1)


def split_sum(keep, got, starts):
    width = keep.shape[1]

    def kernel(s, a, b, *outs):
        for i, o in enumerate(outs):
            rows = pl.ds(pl.multiple_of(s[i], RB), RB)
            o[...] = (a[rows, :].astype(F32) + b[rows, :].astype(F32)).astype(BF)

    return whole(kernel, [sds((RB, width), BF)] * 8, [(starts, SM), keep, got], 24)


def scatter_t(send, keep, starts):
    got = recv_t(send, c=1)
    b = split_sum(keep, got, starts)
    r11 = recv_t(b[5], y=-1)
    r13 = recv_t(b[7], y=1)
    r12 = recv_t(b[6], zh=1)
    s1 = recv_t(b[1], y=-1)
    s3 = recv_t(b[3], y=1)
    s2 = recv_t(b[2] + r12, y=2)
    sz = recv_t((b[4].astype(F32) + r11.astype(F32) + r13.astype(F32)).astype(BF), zh=1)
    return b[0], s1, s2, s3, sz


def sum_dp(rows, dr):
    x, z = dr // 2, dr % 2
    part = [lax.dynamic_slice_in_dim(rows, ((x + i) % 4) * 128, 128, 0) for i in range(4)]
    got = [recv_d(part[i], x=-i) for i in (1, 2, 3)]
    total = part[0].astype(F32) + sum(g.astype(F32) for g in got)
    total = total.astype(BF)
    send = lax.dynamic_slice_in_dim(total, (1 - z) * 64, 64, 0)
    keep = lax.dynamic_slice_in_dim(total, z * 64, 64, 0)
    own = (keep.astype(F32) + recv_d(send, z=1).astype(F32)).astype(BF)
    other = recv_d(own, z=1)
    mine = jnp.where(
        z == 0, jnp.concatenate([own, other], 0), jnp.concatenate([other, own], 0)
    )
    parts = [mine] + [recv_d(mine, x=i) for i in (1, 2, 3)]
    out = jnp.zeros((512, D), BF)
    for i, p in enumerate(parts):
        out = lax.dynamic_update_slice_in_dim(out, p, ((x + i) % 4) * 128, 0)
    return out


def sum_all(v):
    v = v + recv_t(v, zh=1)
    v = v + recv_t(v, c=1)
    pairs = [(i, (i // 8) * 8 + ((i // 2 % 4) ^ 1) * 2 + i % 2) for i in range(16)]
    v = v + lax.ppermute(v, "tensor", pairs)
    v = v + recv_t(v, y=2)
    v = v + recv_d(v, z=1)
    pairs = [(i, ((i // 2) ^ 1) * 2 + i % 2) for i in range(8)]
    v = v + lax.ppermute(v, "dp", pairs)
    return v + recv_d(v, x=2)


def rotary_tables(length):
    position = jnp.arange(length, dtype=F32)
    frequency = jnp.exp(jnp.arange(ROPE // 2, dtype=F32) * (-2.0 * math.log(10000.0) / ROPE))
    angles = position[:, None] * frequency[None, :]
    return jnp.cos(angles), jnp.sin(angles)


def rotate(v, cos, sin):
    a, b = v[:, : ROPE // 2], v[:, ROPE // 2 :]
    return jnp.concatenate([a * cos - b * sin, b * cos + a * sin], axis=-1)


def unrotate(v, cos, sin):
    a, b = v[:, : ROPE // 2], v[:, ROPE // 2 :]
    return jnp.concatenate([a * cos + b * sin, b * cos - a * sin], axis=-1)


QB = 256


def probs_of(starts, first, qn, qr, kn, kr):
    scores = (dot(qn, kn, NT) + dot(qr, kr, NT)) * SCALE
    i = first + lax.broadcasted_iota(jnp.int32, (QB, 1), 0)
    j = lax.broadcasted_iota(jnp.int32, (1, LEN), 1)
    allowed = j <= i
    for n in range(SPANS):
        s = starts[0, n]
        row_in = (i >= s) & (i < s + IMG)
        col_in = (j >= s) & (j < s + IMG)
        allowed = allowed | (row_in & col_in)
    scores = jnp.where(allowed, scores, MASKED)
    raised = jnp.exp(scores - jnp.max(scores, axis=-1, keepdims=True))
    return raised / jnp.sum(raised, axis=-1, keepdims=True)


def attend(starts, qn, qr, kn, kr, v):
    def kernel(s, qn, qr, kn, kr, v, o):
        p = probs_of(s, pl.program_id(0) * QB, qn[...], qr[...], kn[...], kr[...])
        o[...] = dot(p.astype(BF), v[...]).astype(BF)

    rows = lambda w: pl.BlockSpec((QB, w), lambda i: (i, 0))
    full = lambda w: pl.BlockSpec((LEN, w), lambda i: (0, 0))
    return pl.pallas_call(
        kernel,
        grid=(LEN // QB,),
        out_shape=sds((LEN, VDIM), BF),
        in_specs=[SM, rows(NOPE), rows(ROPE), full(NOPE), full(ROPE), full(VDIM)],
        out_specs=rows(VDIM),
        compiler_params=pltpu.CompilerParams(vmem_limit_bytes=32 * MB),
        cost_estimate=pl.CostEstimate(
            flops=2 * LEN * LEN * 320, bytes_accessed=2 * MB, transcendentals=LEN * LEN
        ),
    )(starts, qn, qr, kn, kr, v)


def attend_back(starts, qn, qr, kn, kr, v, mg):
    def kernel(s, qn, qr, kn, kr, v, mg, dqn, dqr, dkn, dkr, dv):
        step = pl.program_id(0)

        @pl.when(step == 0)
        def _():
            dkn[...] = jnp.zeros_like(dkn)
            dkr[...] = jnp.zeros_like(dkr)
            dv[...] = jnp.zeros_like(dv)

        p = probs_of(s, step * QB, qn[...], qr[...], kn[...], kr[...])
        m = mg[...]
        pg = dot(m, v[...], NT)
        sg = (p * (pg - jnp.sum(pg * p, axis=-1, keepdims=True))).astype(BF)
        dqn[...] = dot(sg, kn[...]) * SCALE
        dqr[...] = dot(sg, kr[...]) * SCALE
        dkn[...] += dot(sg, qn[...], TN) * SCALE
        dkr[...] += dot(sg, qr[...], TN) * SCALE
        dv[...] += dot(p.astype(BF), m, TN)

    rows = lambda w: pl.BlockSpec((QB, w), lambda i: (i, 0))
    full = lambda w: pl.BlockSpec((LEN, w), lambda i: (0, 0))
    return pl.pallas_call(
        kernel,
        grid=(LEN // QB,),
        out_shape=[sds((LEN, w), F32) for w in (NOPE, ROPE, NOPE, ROPE, VDIM)],
        in_specs=[SM, rows(NOPE), rows(ROPE), full(NOPE), full(ROPE), full(VDIM), rows(VDIM)],
        out_specs=[rows(NOPE), rows(ROPE), full(NOPE), full(ROPE), full(VDIM)],
        compiler_params=pltpu.CompilerParams(vmem_limit_bytes=40 * MB),
        cost_estimate=pl.CostEstimate(
            flops=2 * LEN * LEN * 960, bytes_accessed=4 * MB, transcendentals=LEN * LEN
        ),
    )(starts, qn, qr, kn, kr, v, mg)


def project(mixed, other, w_half, w_other, tokens, gain, w_router):
    rows_at = 256

    def kernel(m1, m2, w1, w2, x, gain, wr, hid, nrm, inv, probs):
        h = x[...].astype(F32) + (dot(m1[...], w1[...]) + dot(m2[...], w2[...]))
        r = lax.rsqrt(jnp.mean(h * h, axis=-1, keepdims=True) + EPS)
        n = (h * r * gain[...]).astype(BF)
        hid[...] = h
        nrm[...] = n
        inv[...] = r
        logits = dot(n, wr[...])
        e = jnp.exp(logits - jnp.max(logits, axis=-1, keepdims=True))
        probs[...] = e / jnp.sum(e, axis=-1, keepdims=True)

    rows = lambda w: pl.BlockSpec((rows_at, w), lambda i: (i, 0))
    once = lambda a: pl.BlockSpec(a.shape, lambda i: (0, 0), pipeline_mode=pl.Buffered(1))
    return pl.pallas_call(
        kernel,
        grid=(LEN // rows_at,),
        out_shape=[sds((LEN, D), F32), sds((LEN, D), BF), sds((LEN, 1), F32), sds((LEN, EXPERTS), F32)],
        in_specs=[rows(D // 2), rows(D // 2), once(w_half), once(w_other), rows(D), once(gain), once(w_router)],
        out_specs=[rows(D), rows(D), rows(1), rows(EXPERTS)],
        compiler_params=pltpu.CompilerParams(vmem_limit_bytes=48 * MB),
        cost_estimate=pl.CostEstimate(flops=2 * LEN * D * D, bytes_accessed=30 * MB, transcendentals=0),
    )(mixed, other, w_half, w_other, tokens, gain, w_router)


def dispatch(rank_row, probs_row, normed2, grad):
    cols = 512

    def kernel(rank, probs, n, g, x, dy, dyg, gates):
        hit = lax.broadcasted_iota(jnp.int32, (CAP, 1), 0) == rank[...]
        gate = jnp.sum(jnp.where(hit, probs[...], 0.0), axis=-1, keepdims=True)
        pick = jnp.where(hit, 1.0, 0.0).astype(BF)
        x[...] = dot(pick, n[...]).astype(BF)
        got = dot(pick, g[...])
        dyg[...] = got.astype(BF)
        dy[...] = (got * gate).astype(BF)
        gates[...] = gate

    part = pl.BlockSpec((LEN, cols), lambda i: (0, i))
    slot = pl.BlockSpec((CAP, cols), lambda i: (0, i))
    row = pl.BlockSpec((1, LEN), lambda i: (0, 0))
    return pl.pallas_call(
        kernel,
        grid=(D // cols,),
        out_shape=[sds((CAP, D), BF)] * 3 + [sds((CAP, 1), F32)],
        in_specs=[row, row, part, part],
        out_specs=[slot, slot, slot, pl.BlockSpec((CAP, 1), lambda i: (0, 0))],
        compiler_params=pltpu.CompilerParams(vmem_limit_bytes=40 * MB),
        cost_estimate=pl.CostEstimate(flops=4 * LEN * CAP * D, bytes_accessed=16 * MB, transcendentals=0),
    )(rank_row, probs_row, normed2, grad)


def ffn_chunk(x, dy, gu, dn, dgu, ddn):
    act = dot(gu[...], x, NT)
    g, u = act[:FS], act[FS:]
    sg = jax.nn.sigmoid(g)
    h = (g * sg * u).astype(BF)
    dh = dot(dn[...], dy, NT)
    dg = (dh * u * sg * (1.0 + g * (1.0 - sg))).astype(BF)
    du = (dh * g * sg).astype(BF)
    da = jnp.concatenate([dg, du], axis=0)
    ddn[...] = dot(h, dy).astype(BF)
    dgu[...] = dot(da, x).astype(BF)
    return dot(h, dn[...], TN), dot(da, gu[...], TN)


def chunk_outs(n):
    return [sds((2 * FS, D), BF), sds((FS, D), BF)] * n


FLOPS = 2 * 9 * FS * D


def experts_first(x, dy, chunks):
    n = len(chunks)

    def kernel(x, dy, *refs):
        w, outs, (out, dx) = refs[: 2 * n], refs[2 * n : 4 * n], refs[4 * n :]
        xv, dyv = x[...], dy[...]
        for i in range(n):
            o, d = ffn_chunk(xv, dyv, *w[2 * i : 2 * i + 2], *outs[2 * i : 2 * i + 2])
            if i == 0:
                out[...] = o
                dx[...] = d
            else:
                out[...] += o
                dx[...] += d

    flat = [a for c in chunks for a in c]
    res = whole(kernel, chunk_outs(n) + [sds((CAP, D), F32)] * 2, [x, dy] + flat, 56, n * FLOPS * CAP)
    return [(res[2 * i], res[2 * i + 1]) for i in range(n)], res[2 * n], res[2 * n + 1]


def experts_last(x, dy, dyg, chunks, out, dx, me):
    n = len(chunks)

    def kernel(me, x, dy, dyg, out0, dx0, *refs):
        w, outs, (out, dx) = refs[: 2 * n], refs[2 * n : 4 * n], refs[4 * n :]
        xv, dyv = x[...], dy[...]
        sum_o, sum_d = out0[...], dx0[...]
        for i in range(n):
            o, d = ffn_chunk(xv, dyv, *w[2 * i : 2 * i + 2], *outs[2 * i : 2 * i + 2])
            sum_o, sum_d = sum_o + o, sum_d + d
        so = sum_o.astype(BF)
        out[...] = so
        dx[:, :D] = sum_d.astype(BF)
        gg = jnp.sum(so.astype(F32) * dyg[...].astype(F32), axis=-1, keepdims=True)
        lane = lax.broadcasted_iota(jnp.int32, (1, 128), 1)
        dx[:, D:] = jnp.where(lane == me[0], gg, 0.0).astype(BF)

    flat = [a for c in chunks for a in c]
    outs = chunk_outs(n) + [sds((CAP, D), BF), sds((CAP, PW), BF)]
    res = whole(kernel, outs, [(me, SM), x, dy, dyg, out, dx] + flat, 60, n * FLOPS * CAP)
    return [(res[2 * i], res[2 * i + 1]) for i in range(n)], res[2 * n], res[2 * n + 1]


def shared_ffn(x, dy, gu, dn):
    def kernel(x, dy, gu, dn, dgu, ddn, out, dx):
        o, d = ffn_chunk(x[...], dy[...], gu, dn, dgu, ddn)
        out[...] = o.astype(BF)
        dx[...] = d.astype(BF)

    outs = chunk_outs(1) + [sds((LEN, D), BF)] * 2
    return whole(kernel, outs, [x, dy, gu, dn], 58, FLOPS * LEN)


def combine_grad(which, rank_col, dx, shared_dx):
    rows_at = 256

    def kernel(which, rank, dx, sd, o):
        hit = rank[...] == lax.broadcasted_iota(jnp.int32, (1, CAP), 1)
        pick = jnp.where(hit, 1.0, 0.0).astype(BF)
        t = dot(pick, dx[...])
        o[:, :D] = (t[:, :D] + sd[...].astype(F32)).astype(BF)
        o[:, D:] = t[:, D:].astype(BF)

    at = lambda w: pl.BlockSpec((rows_at, w), lambda i, which: (which[0] * 2 + i, 0))
    return pl.pallas_call(
        kernel,
        grid_spec=pltpu.PrefetchScalarGridSpec(
            num_scalar_prefetch=1,
            grid=(2,),
            in_specs=[at(1), pl.BlockSpec((CAP, PW), lambda i, which: (0, 0)), at(D)],
            out_specs=pl.BlockSpec((rows_at, PW), lambda i, which: (i, 0)),
        ),
        out_shape=sds((LEN // 2, PW), BF),
        compiler_params=pltpu.CompilerParams(vmem_limit_bytes=40 * MB),
        cost_estimate=pl.CostEstimate(flops=LEN * CAP * PW, bytes_accessed=7 * MB, transcendentals=0),
    )(which, rank_col, dx, shared_dx)


def combine_out(rank_col, probs_col, slot_out, shared_out):
    rows_at = 256

    def kernel(rank, probs, so, sh, o):
        hit = rank[...] == lax.broadcasted_iota(jnp.int32, (1, CAP), 1)
        pick = jnp.where(hit, 1.0, 0.0).astype(BF)
        o[...] = (dot(pick, so[...]) * probs[...] + sh[...].astype(F32)).astype(BF)

    at = lambda w: pl.BlockSpec((rows_at, w), lambda i: (i, 0))
    return pl.pallas_call(
        kernel,
        grid=(LEN // rows_at,),
        out_shape=sds((LEN, D), BF),
        in_specs=[at(1), at(1), pl.BlockSpec((CAP, D), lambda i: (0, 0)), at(D)],
        out_specs=at(D),
        compiler_params=pltpu.CompilerParams(vmem_limit_bytes=40 * MB),
        cost_estimate=pl.CostEstimate(flops=2 * LEN * CAP * D, bytes_accessed=10 * MB, transcendentals=0),
    )(rank_col, probs_col, slot_out, shared_out)


def norm_back(v, inv, gain, incoming):
    weighted = incoming * gain
    inner = jnp.mean(weighted * v, axis=-1, keepdims=True)
    return inv * weighted - v * (inv * inv * inv) * inner, jnp.sum(incoming * v * inv, axis=0, keepdims=True)


def rows_two(terms, hidden, inv, probs, grad, gain, w_router_t):
    def kernel(a, b, c, d, e, h, inv, p, g, gain, wr, hg, pay, gg):
        t = a[...].astype(F32) + b[...].astype(F32) + c[...].astype(F32)
        t = t + d[...].astype(F32) + e[...].astype(F32)
        gates = t[:, D : D + EXPERTS]
        pv = p[...]
        lg = (pv * (gates - jnp.sum(pv * gates, axis=-1, keepdims=True))).astype(BF)
        n2 = t[:, :D] + dot(lg, wr[...])
        r, gain_grad = norm_back(h[...], inv[...], gain[...], n2)
        r = r + g[...].astype(F32)
        hg[...] = r
        pay[:, :D] = r.astype(BF)
        pay[:, D:] = jnp.concatenate([lg, jnp.zeros((RB, 128 - EXPERTS), BF)], axis=1)
        gg[...] = gain_grad

    outs = [sds((RB, D), F32), sds((RB, PW), BF), sds((1, D), F32)]
    return whole(kernel, outs, [*terms, hidden, inv, probs, grad, gain, w_router_t], 24)


def rows_one(terms, lat, w_lat, x, inv, hg, gain):
    def kernel(a, b, c, d, e, lat, wl, x, inv, hg, gain, o, gg):
        t = a[...].astype(F32) + b[...].astype(F32) + c[...].astype(F32)
        t = t + d[...].astype(F32) + e[...].astype(F32)
        t = t + dot(lat[...], wl[...])
        r, gain_grad = norm_back(x[...].astype(F32), inv[...], gain[...], t)
        o[...] = (hg[...] + r).astype(BF)
        gg[...] = gain_grad

    outs = [sds((RB, D), BF), sds((1, D), F32)]
    return whole(kernel, outs, [*terms, lat, w_lat, x, inv, hg, gain], 24, 2 * RB * LX * D)


def mixed_back(starts, half, other, w_out):
    def kernel(s, a, b, w, o):
        for n, ref in enumerate((a, b)):
            t = dot(ref[:, :D], w[...], NT).astype(BF)
            for i in range(8):
                rows = pl.ds(pl.multiple_of(s[n * 8 + i], RB), RB)
                o[rows, :] = t[i * RB : (i + 1) * RB]

    return whole(kernel, [sds((LEN, VDIM), BF)], [(starts, SM), half, other, w_out], 32, 2 * LEN * D * VDIM)[0]


def output_grads(starts, half, other, mixed, normed2):
    def kernel(s, a, b, m, n2, wo, wr):
        sum_o = jnp.zeros((VDIM, D), F32)
        sum_r = jnp.zeros((EXPERTS, D), F32)
        for n, ref in enumerate((a, b)):
            at = [pl.ds(pl.multiple_of(s[n * 8 + i], RB), RB) for i in range(8)]
            mix = jnp.concatenate([m[r, :] for r in at], axis=0)
            sum_o = sum_o + dot(mix, ref[:, :D], TN)
            for i, r in enumerate(at):
                lg = ref[i * RB : (i + 1) * RB, D:]
                sum_r = sum_r + dot(lg, n2[r, :], TN)[:EXPERTS]
        wo[...] = sum_o.astype(BF)
        wr[...] = sum_r.astype(BF)

    outs = [sds((VDIM, D), BF), sds((EXPERTS, D), BF)]
    return whole(kernel, outs, [(starts, SM), half, other, mixed, normed2], 40, 2 * LEN * D * 256)


def latent_w_grad(starts, half, other, normed1, pick):
    def kernel(s, a, b, n1, pick, o):
        total = jnp.zeros((LP, D), F32)
        for n, ref in enumerate((a, b)):
            rows = jnp.concatenate(
                [n1[pl.ds(pl.multiple_of(s[n * 8 + i], RB), RB), :] for i in range(8)], axis=0
            )
            own = dot(pick[...], ref[...], NT).astype(BF)
            total = total + dot(own, rows)
        o[...] = total.astype(BF)

    outs = [sds((LP, D), BF)]
    return whole(kernel, outs, [(starts, SM), half, other, normed1, pick], 32, 2 * LEN * LX * 256)[0]


def spread(starts, half, other):
    def kernel(s, a, b, o):
        for n, ref in enumerate((a, b)):
            for i in range(8):
                rows = pl.ds(pl.multiple_of(s[n * 8 + i], RB), RB)
                o[rows, :] = ref[i * RB : (i + 1) * RB].astype(F32)

    return whole(kernel, [sds((LEN, D), F32)], [(starts, SM), half, other], 32)[0]


def local(
    tokens,
    cotangent,
    expert_ids,
    slot_order,
    image_starts,
    norm1_gain,
    w_query,
    w_latent,
    latent_gain,
    w_expand,
    w_output,
    norm2_gain,
    w_router,
    expert_gate,
    expert_up,
    expert_down,
    shared_gate,
    shared_up,
    shared_down,
):
    tr = lax.axis_index("tensor")
    dr = lax.axis_index("dp")
    zh, yy, cc = tr // 8, tr // 2 % 4, tr % 2
    peers = [
        ((zh + z) % 2, (yy + y) % 4, (cc + c) % 2) for c in range(2) for z in range(2) for y in range(4)
    ]
    starts16 = jnp.stack([(c * 8 + z * 4 + y) * RB for z, y, c in peers]).astype(jnp.int32)
    starts8 = jnp.stack([(z * 4 + y) * RB for z, y, c in peers[:8]]).astype(jnp.int32)
    ranks16 = jnp.stack([z * 8 + y * 2 + c for z, y, c in peers]).astype(jnp.int32)
    own_row = (cc * 8 + zh * 4 + yy) * RB
    own_rows = lambda a: lax.dynamic_slice_in_dim(a, own_row, RB, 0)
    me = jnp.full((1,), tr, jnp.int32)

    lat_t = jnp.pad(w_latent.T, [(0, LP - LW), (0, 0)])
    lat_half, lat_other = gather_t(lat_t)
    own = (
        jnp.concatenate([expert_gate[0].T, expert_up[0].T], axis=0),
        expert_down[0].T,
    )
    move = lambda pair, **k: tuple(recv_d(a, **k) for a in pair)
    ap, am, zz = move(own, x=1), move(own, x=-1), move(own, z=1)
    a2 = move(own, x=2)
    b2 = move(zz, x=2)
    bp = (recv_d(ap[0], z=1), recv_d(zz[1], x=1))
    bm = (recv_d(am[0], z=1), recv_d(zz[1], x=-1))
    wo_half, wo_other = gather_t(w_output)
    out_grad = lax.all_gather(cotangent, "tensor", axis=1, tiled=True)

    chosen = jnp.any(expert_ids == tr, axis=1)
    order = slot_order[0]
    token = jnp.arange(LEN, dtype=jnp.int32)
    place = jnp.sum(jnp.where(order[:, None] == token[None, :], token[:, None], 0), axis=0)
    before = (place[:, None] < place[None, :]) & chosen[:, None]
    rank = jnp.sum(before.astype(jnp.int32), axis=0)
    rank = jnp.where(chosen, rank, -1)
    rank_row, rank_col = rank[None, :], rank[:, None]

    resid = tokens.astype(F32)
    inv1 = lax.rsqrt(jnp.mean(resid * resid, axis=-1, keepdims=True) + EPS)
    normed1 = (resid * inv1 * norm1_gain).astype(BF)
    cos, sin = rotary_tables(LEN)
    query = dot(normed1, w_query)
    qn = query[:, :NOPE].astype(BF)
    qr = rotate(query[:, NOPE:], cos, sin).astype(BF)
    column = jnp.arange(LP, dtype=jnp.int32)
    target = jnp.where(column[None, :] < LW, ranks16[:, None] * LW + column[None, :], -1).reshape(-1)
    lat_place = (jnp.arange(LX, dtype=jnp.int32)[:, None] == target[None, :]).astype(BF)
    w_lat = (
        dot(lat_place[:, : 8 * LP], lat_half) + dot(lat_place[:, 8 * LP :], lat_other)
    ).astype(BF)
    latent = dot(normed1, w_lat, NT).astype(BF)
    lat_in = latent[:, :LATENT].astype(F32)
    inv_lat = lax.rsqrt(jnp.mean(lat_in * lat_in, axis=-1, keepdims=True) + EPS)
    compressed = (lat_in * inv_lat * latent_gain).astype(BF)
    expanded = dot(compressed, w_expand).astype(BF)
    kn, v = expanded[:, :NOPE], expanded[:, NOPE:]
    kr = rotate(latent[:, LATENT : LATENT + ROPE].astype(F32), cos, sin).astype(BF)
    mixed = attend(image_starts, qn, qr, kn, kr, v)
    mix_half, mix_other = gather_t(mixed, axis=1)
    hidden, normed2, inv2, probs = project(
        mix_half, mix_other, wo_half, wo_other, tokens, norm2_gain[None, :], w_router
    )
    probs_col = lax.dynamic_slice_in_dim(probs, tr, 1, 1)

    x, dy, dyg, _ = dispatch(rank_row, probs_col.reshape(1, LEN), normed2, out_grad)
    near, part_out, part_dx = experts_first(x, dy, [own, ap, am, zz])
    sh_gu = jnp.concatenate([shared_gate.T, shared_up.T], axis=0)
    s_dgu, s_ddn, s_out, s_dx = shared_ffn(normed2, out_grad, sh_gu, shared_down)
    far, slot_out, dx = experts_last(x, dy, dyg, [bp, bm, b2, a2], part_out, part_dx, me)
    half_of = lambda k: jnp.full((1,), k, jnp.int32)
    n2_send = combine_grad(half_of(1 - cc), rank_col, dx, s_dx)
    n2_keep = combine_grad(half_of(cc), rank_col, dx, s_dx)
    n2_terms = scatter_t(n2_send, n2_keep, starts8)

    g_own, g_ap, g_am, g_z = near
    g_bp, g_bm, g_b2, g_a2 = far
    got_b2 = move(g_b2, x=2)
    got_a2 = move(g_a2, x=2)
    ap_gu = g_ap[0] + recv_d(g_bp[0], z=1)
    am_gu = g_am[0] + recv_d(g_bm[0], z=1)
    z_gu = g_z[0] + got_b2[0]
    z_dn = (
        g_z[1].astype(F32)
        + got_b2[1].astype(F32)
        + recv_d(g_bp[1], x=-1).astype(F32)
        + recv_d(g_bm[1], x=1).astype(F32)
    ).astype(BF)
    terms = [g_own, got_a2, move((ap_gu, g_ap[1]), x=-1), move((am_gu, g_am[1]), x=1), move((z_gu, z_dn), z=1)]
    gu_sum = sum(t[0].astype(F32) for t in terms)
    dn_sum = sum(t[1].astype(F32) for t in terms)
    expert_gate_grad = gu_sum[:FS].T[None]
    expert_up_grad = gu_sum[FS:].T[None]
    expert_down_grad = dn_sum.T[None]

    branch = combine_out(rank_col, probs_col, slot_out, s_out)
    branch_sum = lax.psum_scatter(branch, "tensor", scatter_dimension=1, tiled=True)
    own_cols = lax.dynamic_slice_in_dim(hidden, tr * 128, 128, 1)
    output = (own_cols + branch_sum.astype(F32)).astype(BF)
    s_dgu, s_ddn = lax.psum((s_dgu, s_ddn), "dp")

    hid_grad, payload, gain2 = rows_two(
        n2_terms,
        own_rows(hidden),
        own_rows(inv2),
        own_rows(probs),
        own_rows(out_grad),
        norm2_gain[None, :],
        w_router.T,
    )
    pay_half, pay_other = gather_t(payload)
    mixed_grad = mixed_back(starts16, pay_half, pay_other, w_output)

    dqn, dqr, dkn, dkr, dv = attend_back(image_starts, qn, qr, kn, kr, v, mixed_grad)
    query_grad = jnp.concatenate([dqn, unrotate(dqr, cos, sin)], axis=1).astype(BF)
    expanded_grad = jnp.concatenate([dkn, dv], axis=1).astype(BF)
    comp_grad = dot(expanded_grad, w_expand, NT)
    lat_head, gain_lat = norm_back(lat_in, inv_lat, latent_gain, comp_grad)
    lat_part = jnp.concatenate(
        [lat_head, unrotate(dkr, cos, sin), jnp.zeros((LEN, LX - LATENT - ROPE), F32)], axis=1
    ).astype(BF)
    half_rows = lambda a, k: lax.dynamic_slice_in_dim(a, k * (LEN // 2), LEN // 2, 0)
    lat_terms = scatter_t(half_rows(lat_part, 1 - cc), half_rows(lat_part, cc), starts8)
    n1_send = dot(half_rows(query_grad, 1 - cc), w_query, NT).astype(BF)
    n1_keep = dot(half_rows(query_grad, cc), w_query, NT).astype(BF)
    n1_terms = scatter_t(n1_send, n1_keep, starts8)
    lat_rows = sum(t.astype(F32) for t in lat_terms).astype(BF)
    lg_half, lg_other = gather_t(lat_rows)
    tok_rows, gain1 = rows_one(
        n1_terms, lat_rows, w_lat, own_rows(tokens), own_rows(inv1), hid_grad, norm1_gain[None, :]
    )
    tok_half, tok_other = gather_t(tok_rows)
    tokens_grad = spread(starts16, tok_half, tok_other)

    w_out_g, w_router_g = output_grads(starts16, pay_half, pay_other, mixed, normed2)
    w_query_g = dot(query_grad, normed1, TN).astype(BF)
    w_expand_g = dot(compressed, expanded_grad, TN).astype(BF).reshape(64, D)
    pick = (
        (jnp.arange(LX, dtype=jnp.int32)[None, :] == tr * LW + column[:, None]) & (column[:, None] < LW)
    ).astype(BF)
    w_lat_g = latent_w_grad(starts16, lg_half, lg_other, normed1, pick)
    rows = jnp.concatenate(
        [w_query_g, w_out_g, w_expand_g, w_lat_g, w_router_g, jnp.zeros((64, D), BF)], axis=0
    )
    rows = sum_dp(rows, dr).astype(F32)
    gains = jnp.concatenate([gain1.reshape(16, 128), gain2.reshape(16, 128), gain_lat.reshape(4, 128), jnp.zeros((4, 128), F32)], axis=0)
    gains = sum_all(gains)
    return (
        output,
        tokens_grad,
        gains[:16].reshape(D),
        rows[:192].T,
        rows[384 : 384 + LW].T,
        gains[32:36].reshape(LATENT),
        rows[320:384].reshape(LATENT, 256),
        rows[192:320],
        gains[16:32].reshape(D),
        rows[432:448].T,
        expert_gate_grad,
        expert_up_grad,
        expert_down_grad,
        s_dgu[:FS].astype(F32).T,
        s_dgu[FS:].astype(F32).T,
        s_ddn.astype(F32),
    )


def solution(mesh):
    in_specs = (
        P("dp", None),
        P("dp", "tensor"),
        P("dp", None),
        P("dp", None),
        P("dp", None),
        P(),
        P(None, "tensor"),
        P(None, "tensor"),
        P(),
        P(None, "tensor"),
        P("tensor", None),
        P(),
        P(),
        P("tensor", None, "dp"),
        P("tensor", None, "dp"),
        P("tensor", None, "dp"),
        P(None, "tensor"),
        P(None, "tensor"),
        P("tensor", None),
    )
    out_specs = (
        P("dp", "tensor"),
        P("dp", None),
        P(),
        P(None, "tensor"),
        P(None, "tensor"),
        P(),
        P(None, "tensor"),
        P("tensor", None),
        P(),
        P(),
        P("tensor", None, "dp"),
        P("tensor", None, "dp"),
        P("tensor", None, "dp"),
        P(None, "tensor"),
        P(None, "tensor"),
        P("tensor", None),
    )
    return jax.shard_map(local, mesh=mesh, in_specs=in_specs, out_specs=out_specs, check_vma=False)
```

time: 1730 us -> 844 us (0.49)
  waiting for transfers between devices: 1090 us -> 315 us
  starting transfers between devices: 5.86 us -> 206 us
  matrix products: 161 us -> 15.5 us
  Pallas kernels: 0 us -> 137 us
  local copies, waits for them, and re-layouts: 216 us -> 96.1 us
  blocking collectives: 102 us -> 0 us
  other arithmetic: 129 us -> 50.7 us
    all_gather x5 -> x0, waiting for transfers between devices: 389 us -> none  [the longest x1 115 us: local(): lax.all_gather(expert_down, 'dp', axis=2, tiled=True)]
    unnamed x20 -> x4, waiting for transfers between devices: 323 us -> 0.05 us
    ppermute x0 -> x115, waiting for transfers between devices: none -> 315 us  [the longest x38 160 us: recv_d(): return lax.ppermute(a, 'dp', pairs)]
    psum x3 -> x1, waiting for transfers between devices: 256 us -> 0.01 us  [local(): s_dgu, s_ddn = lax.psum((s_dgu, s_ddn), 'dp')]
    ppermute x0 -> x115, starting transfers between devices: none -> 205 us  [the longest x75 155 us: recv_t(): return lax.ppermute(a, 'tensor', pairs)]
    dot_general x39 -> x10, matrix products: 161 us -> 15.5 us  [dot(): return lax.dot_general(a, b, dims, preferred_element_type=F32)]
    pallas_call x0 -> x19, Pallas kernels: none -> 137 us  [the longest x12 89.1 us: whole(): pl.pallas_call(kernel, out_shape=outs, in_specs=specs, out_specs=[VM] * l...]
    unnamed x181 -> x254, local copies, waits for them, and re-layouts: 161 us -> 68.1 us
  transfers between devices with their start and end apart: 16 -> 118, of which waited for: 12 -> 45; matrix products, arithmetic and copies ran while one was open for 24% -> 15% of each run, Pallas kernels for 0% -> 12%
where the time goes in v1:
time: 844 us; the launch traced here: 835 us
  waiting for transfers between devices  315 us (37%)
  starting transfers between devices  206 us (24%)
  Pallas kernels  137 us (16%)
  local copies, waits for them, and re-layouts  96.1 us (11%)
  other arithmetic  50.7 us (6%)
  between operations  15.7 us (2%)
  matrix products  15.5 us (2%)
    ppermute x38, waiting for transfers between devices, recv_d(): return lax.ppermute(a, 'dp', pairs)  160 us
    ppermute x75, starting transfers between devices, recv_t(): return lax.ppermute(a, 'tensor', pairs)  155 us
    ppermute x75, waiting for transfers between devices, recv_t(): return lax.ppermute(a, 'tensor', pairs)  155 us
    pallas_call x12, Pallas kernels, whole(): pl.pallas_call(kernel, out_shape=outs, in_specs=specs, out_specs=[VM] * l...  89.1 us
    unnamed x254, local copies, waits for them, and re-layouts  68.1 us
    ppermute x38, starting transfers between devices, recv_d(): return lax.ppermute(a, 'dp', pairs)  49.1 us
    pallas_call x1, Pallas kernels, project(): pl.pallas_call(kernel, grid=(LEN // rows_at,), out_shape=[sds((LEN, D), F...  17.3 us
  transfers between devices with their start and end apart: 118, of which 45 were waited for; matrix products, arithmetic and copies ran while one was open for 15% of the time, Pallas kernels for 12%

profile of v1, /device:TPU:1, one launch (start us, length us, event | category | flops | bytes accessed | tf_op | source)
XLA Modules:
  0.0 835.2 jit_solution(11076915815784591804)
XLA Ops:
  39.4 23.0 %collective-permute-done.4 = bf16[48,2048]{1,0:T(8,128)(2,1)S(1)} collective-permute-done((bf16[48,2048]{1,0:T(8,128)(2,1)}, bf16[48,2048]{1,0:T(8,128)(2,1)S(1)}, u32[]{:S(2)}, u32[]{:S(2)}) %collective-permute-start.4) | collective-permute-done | bytes 196640 | tf_op jit(solution)/shard_map/ppermute | solution.py:72
  64.9 9.3 %collective-permute-done.5 = bf16[48,2048]{1,0:T(8,128)(2,1)S(1)} collective-permute-done((bf16[48,2048]{1,0:T(8,128)(2,1)}, bf16[48,2048]{1,0:T(8,128)(2,1)S(1)}, u32[]{:S(2)}, u32[]{:S(2)}) %collective-permute-start.5) | collective-permute-done | bytes 196640 | tf_op jit(solution)/shard_map/ppermute | solution.py:72
  76.2 5.4 collective-permute-done.6
  94.1 7.8 collective-permute-done.20
  117.0 6.2 shard_map.306.m
  153.5 14.9 %collective-permute-done.29.refs_7_ = bf16[176,2048]{1,0:T(8,128)(2,1)} collective-permute-done((bf16[176,2048]{1,0:T(8,128)(2,1)}, bf16[176,2048]{1,0:T(8,128)(2,1)}, u32[]{:S(2)}, u32[]{:S(2)}) %collective-permute-start.29) | collective-permute-done | bytes 720928 | tf_op jit(solution)/shard_map/ppermute | solution.py:79
  178.3 8.9 %collective-permute-done.37.refs_7_ = bf16[176,2048]{1,0:T(8,128)(2,1)} collective-permute-done((bf16[176,2048]{1,0:T(8,128)(2,1)}, bf16[176,2048]{1,0:T(8,128)(2,1)}, u32[]{:S(2)}, u32[]{:S(2)}) %collective-permute-start.37) | collective-permute-done | bytes 720928 | tf_op jit(solution)/shard_map/ppermute | solution.py:79
  191.3 17.3 %shard_map.307 = (f32[1024,2048]{1,0:T(8,128)}, bf16[1024,2048]{1,0:T(8,128)(2,1)}, f32[1024,1]{1,0:T(8,128)S(1)}, f32[1024,16]{1,0:T(8,128)S(1)}) custom-call(bf16[1024,1024]{1,0:T(8,128)(2,1)} %constant_dynamic-update-slice_fusion.8.m1, bf16[1024,1024]{1,0:T(8,128)(2,1)} %collective-permute-done.15.m2, ...), custom_call_target="tpu_custom_call" | custom-call | flops 8589934592 | bytes 31457280 | tf_op jit(solution)/shard_map/pallas_call | solution.py:256
  215.6 6.7 shard_map.308
  238.9 23.3 %shard_map.309 = (bf16[352,2048]{1,0:T(8,128)(2,1)}, bf16[176,2048]{1,0:T(8,128)(2,1)}, bf16[352,2048]{1,0:T(8,128)(2,1)}, bf16[176,2048]{1,0:T(8,128)(2,1)}, bf...) custom-call(bf16[480,2048]{1,0:T(8,128)(2,1)} %copy-done.56, ...), custom_call_target="tpu_custom_call" | custom-call | flops 12457082880 | bytes 29097984 | tf_op jit(solution)/shard_map/pallas_call | solution.py:53
  262.2 14.7 %shard_map.311 = (bf16[352,2048]{1,0:T(8,128)(2,1)}, bf16[176,2048]{1,0:T(8,128)(2,1)}, bf16[1024,2048]{1,0:T(8,128)(2,1)}, bf16[1024,2048]{1,0:T(8,128)(2,1)}) custom-call(bf16[1024,2048]{1,0:T(8,128)(2,1)} %get-tuple-element.85.n.x.n2, bf16[1024,2048]{1,0:T(8,128)(2,1)} %all-gather.2.cloned.1.call-done.g.dy, bf16[352,2048]{1,0:T(8,128)(2,1)} %pad_maximum_fusion.1.gu, ...), custom_call_target="tpu_custom_call" | custom-call | flops 6643777536 | bytes 21102592 | tf_op jit(solution)/shard_map/pallas_call | solution.py:53
  279.8 8.9 %collective-permute-done.32.refs_2_ = bf16[352,2048]{1,0:T(8,128)(2,1)} collective-permute-done((bf16[352,2048]{1,0:T(8,128)(2,1)}, bf16[352,2048]{1,0:T(8,128)(2,1)}, u32[]{:S(2)}, u32[]{:S(2)}) %collective-permute-start.32) | collective-permute-done | bytes 1441824 | tf_op jit(solution)/shard_map/ppermute | solution.py:79
  288.7 22.1 %collective-permute-done.34.refs_4_ = bf16[352,2048]{1,0:T(8,128)(2,1)} collective-permute-done((bf16[352,2048]{1,0:T(8,128)(2,1)}, bf16[352,2048]{1,0:T(8,128)(2,1)}, u32[]{:S(2)}, u32[]{:S(2)}) %collective-permute-start.34) | collective-permute-done | bytes 1441824 | tf_op jit(solution)/shard_map/ppermute | solution.py:79
  310.8 25.7 %shard_map.310 = (bf16[352,2048]{1,0:T(8,128)(2,1)}, bf16[176,2048]{1,0:T(8,128)(2,1)}, bf16[352,2048]{1,0:T(8,128)(2,1)}, bf16[176,2048]{1,0:T(8,128)(2,1)}, bf...) custom-call(s32[1]{0:T(128)} %bitcast.20.me, ...), custom_call_target="tpu_custom_call" | custom-call | flops 12457082880 | bytes 35119108 | tf_op jit(solution)/shard_map/pallas_call | solution.py:53
  361.7 25.2 %collective-permute-start.40 = (bf16[64,2176]{1,0:T(8,128)(2,1)S(1)}, bf16[64,2176]{1,0:T(8,128)(2,1)S(1)}, u32[]{:S(2)}, u32[]{:S(2)}) collective-permute-start(bf16[64,2176]{1,0:T(8,128)(2,1)S(1)} %get-tuple-element.98), channel_id=1, source_target_pairs={{8,0},{9,1},{10,2},{11,3},{12,4},{13,5},{14,6},{15,7},{0,8},{1,9},... | collective-permute-start | bytes 835592 | tf_op jit(solution)/shard_map/ppermute | solution.py:72
  426.0 10.3 %collective-permute-done.49 = bf16[64,2176]{1,0:T(8,128)(2,1)S(1)} collective-permute-done((bf16[64,2176]{1,0:T(8,128)(2,1)S(1)}, bf16[64,2176]{1,0:T(8,128)(2,1)S(1)}, u32[]{:S(2)}, u32[]{:S(2)}) %collective-permute-start.49) | collective-permute-done | bytes 278560 | tf_op jit(solution)/shard_map/ppermute | solution.py:72
  436.3 8.7 %collective-permute-start.50 = (bf16[64,2176]{1,0:T(8,128)(2,1)S(1)}, bf16[64,2176]{1,0:T(8,128)(2,1)S(1)}, u32[]{:S(2)}, u32[]{:S(2)}) collective-permute-start(bf16[64,2176]{1,0:T(8,128)(2,1)S(1)} %collective-permute-done.49), channel_id=1, source_target_pairs={{2,0},{3,1},{4,2},{5,3},{6,4},{7,5},{0,6},{1,7},{10,8},{11,9},{12,... | collective-permute-start | bytes 835592 | tf_op jit(solution)/shard_map/ppermute | solution.py:72
  462.6 14.3 %collective-permute-start.53 = (bf16[512,2176]{1,0:T(8,128)(2,1)}, bf16[512,2176]{1,0:T(8,128)(2,1)}, u32[]{:S(2)}, u32[]{:S(2)}) collective-permute-start(bf16[512,2176]{1,0:T(8,128)(2,1)} %constant_dynamic-update-slice_fusion.24.a), channel_id=1, source_target_pairs={{1,0},{0,1},{3,2},{2,3},{5,4},{4,5},{7,6},{6,7},{9,8},{8,9},{11,10... | collective-permute-start | bytes 6684680 | tf_op jit(solution)/shard_map/ppermute | solution.py:72
  481.4 13.8 %collective-permute-done.102 = bf16[352,2048]{1,0:T(8,128)(2,1)} collective-permute-done((bf16[352,2048]{1,0:T(8,128)(2,1)}, bf16[352,2048]{1,0:T(8,128)(2,1)}, u32[]{:S(2)}, u32[]{:S(2)}) %collective-permute-start.102) | collective-permute-done | bytes 1441824 | tf_op jit(solution)/shard_map/ppermute | solution.py:79
  495.2 38.5 %collective-permute-done.104 = bf16[352,2048]{1,0:T(8,128)(2,1)} collective-permute-done((bf16[352,2048]{1,0:T(8,128)(2,1)}, bf16[352,2048]{1,0:T(8,128)(2,1)}, u32[]{:S(2)}, u32[]{:S(2)}) %collective-permute-start.104) | collective-permute-done | bytes 1441824 | tf_op jit(solution)/shard_map/ppermute | solution.py:79
  543.0 6.4 copy.90
  559.2 22.9 %collective-permute-done.114 = bf16[176,2048]{1,0:T(8,128)(2,1)} collective-permute-done((bf16[176,2048]{1,0:T(8,128)(2,1)}, bf16[176,2048]{1,0:T(8,128)(2,1)}, u32[]{:S(2)}, u32[]{:S(2)}) %collective-permute-start.114) | collective-permute-done | bytes 720928 | tf_op jit(solution)/shard_map/ppermute | solution.py:79
  589.4 9.4 %shard_map.318 = (f32[1024,128]{1,0:T(8,128)S(1)}, f32[1024,64]{1,0:T(8,128)S(1)}, f32[1024,128]{1,0:T(8,128)S(1)}, f32[1024,64]{1,0:T(8,128)S(1)}, f32[1024,128]{1,0:T(8,128)S(1)}) custom-call(s32[1,2]{1,0:T(1,128)S(1)} %copy-done.55, bf16[1024,128]{1,0:T(8,128)(2,1)S(1)} %copy-done.35, bf16[1024,64]{1,0:T(8,128)(2,1)S(1)} %copy-done.39, ...), custom_call_target="tpu_custom_call" | custom-call | flops 2013265920 | bytes 4194304 | tf_op jit(solution)/shard_map/pallas_call | solution.py:227
  642.0 5.8 shard_map.323
  669.7 4.2 collective-permute-done.91
  673.9 4.4 collective-permute-start.92
  685.8 33.4 %collective-permute-done.56 = bf16[64,2048]{1,0:T(8,128)(2,1)S(1)} collective-permute-done((bf16[64,2048]{1,0:T(8,128)(2,1)S(1)}, bf16[64,2048]{1,0:T(8,128)(2,1)S(1)}, u32[]{:S(2)}, u32[]{:S(2)}) %collective-permute-start.56) | collective-permute-done | bytes 262176 | tf_op jit(solution)/shard_map/ppermute | solution.py:72
  721.1 5.1 collective-permute-done.60
  745.0 8.5 %collective-permute-done.94 = bf16[128,2048]{1,0:T(8,128)(2,1)S(1)} collective-permute-done((bf16[128,2048]{1,0:T(8,128)(2,1)S(1)}, bf16[128,2048]{1,0:T(8,128)(2,1)S(1)}, u32[]{:S(2)}, u32[]{:S(2)}) %collective-permute-start.94) | collective-permute-done | bytes 524320 | tf_op jit(solution)/shard_map/ppermute | solution.py:79
  791.8 6.9 collective-permute-done.74
  798.7 7.1 collective-permute-done.76
  822.9 5.5 shard_map.322
  (592 shorter events, 394.9 us)
Async XLA Ops:
  7.2 204.0 %all-gather.2.cloned.1.call-start = ((), (), s32[]{:S(2)}) async-start(), calls=%async_computation.1 | async-start | bytes 4456448 | tf_op jit(solution)/shard_map/all_gather | solution.py:552
  17.1 66.9 %collective-permute-start.19 = (bf16[128,2048]{1,0:T(8,128)(2,1)}, bf16[128,2048]{1,0:T(8,128)(2,1)}, u32[]{:S(2)}, u32[]{:S(2)}) collective-permute-start(bf16[128,2048]{1,0:T(8,128)(2,1)} %w.1), channel_id=1, source_target_pairs={{8,0},{9,1},{10,2},{11,3},{12,4},{13,5},{14,6},{15,7},{0,8},{1,9},... | collective-permute-start | bytes 1572872 | tf_op jit(solution)/shard_map/ppermute | solution.py:72
  17.2 590.6 %all-reduce.4.cloned.1.call-start = ((), (), s32[]{:S(2)}) async-start(), calls=%async_computation.3 | async-start | bytes 4325376 | tf_op jit(solution)/shard_map/psum | solution.py:624
  28.7 56.8 %collective-permute-start.17 = (bf16[128,2048]{1,0:T(8,128)(2,1)S(1)}, bf16[128,2048]{1,0:T(8,128)(2,1)S(1)}, u32[]{:S(2)}, u32[]{:S(2)}) collective-permute-start(bf16[128,2048]{1,0:T(8,128)(2,1)S(1)} %copy-done.19), channel_id=1, source_target_pairs={{4,0},{5,1},{6,2},{7,3},{0,4},{1,5},{2,6},{3,7},{12,8},{13,9},{14,... | collective-permute-start | bytes 1572872 | tf_op jit(solution)/shard_map/ppermute | solution.py:72
  31.7 53.8 %collective-permute-start.16 = (bf16[128,2048]{1,0:T(8,128)(2,1)S(1)}, bf16[128,2048]{1,0:T(8,128)(2,1)S(1)}, u32[]{:S(2)}, u32[]{:S(2)}) collective-permute-start(bf16[128,2048]{1,0:T(8,128)(2,1)S(1)} %copy-done.19), channel_id=1, source_target_pairs={{2,0},{3,1},{4,2},{5,3},{6,4},{7,5},{0,6},{1,7},{10,8},{11,9},{12,... | collective-permute-start | bytes 1572872 | tf_op jit(solution)/shard_map/ppermute | solution.py:72
  34.8 56.6 %collective-permute-start.18 = (bf16[128,2048]{1,0:T(8,128)(2,1)S(1)}, bf16[128,2048]{1,0:T(8,128)(2,1)S(1)}, u32[]{:S(2)}, u32[]{:S(2)}) collective-permute-start(bf16[128,2048]{1,0:T(8,128)(2,1)S(1)} %copy-done.19), channel_id=1, source_target_pairs={{6,0},{7,1},{0,2},{1,3},{2,4},{3,5},{4,6},{5,7},{14,8},{15,9},{8,1... | collective-permute-start | bytes 1572872 | tf_op jit(solution)/shard_map/ppermute | solution.py:72
  104.4 86.9 %collective-permute-start.23 = (bf16[1024,2048]{1,0:T(8,128)(2,1)}, bf16[1024,2048]{1,0:T(8,128)(2,1)}, u32[]{:S(2)}, u32[]{:S(2)}) collective-permute-start(bf16[1024,2048]{1,0:T(8,128)(2,1)} %constant_dynamic-update-slice_fusion.16.w1), channel_id=1, source_target_pairs={{1,0},{0,1},{3,2},{2,3},{5,4},{4,5},{7,6},{6,7},{9,8},{8,9},{11,10... | collective-permute-start | bytes 12582920 | tf_op jit(solution)/shard_map/ppermute | solution.py:72
  176.7 49.5 %collective-permute-start.24 = (bf16[352,2048]{1,0:T(8,128)(2,1)}, bf16[352,2048]{1,0:T(8,128)(2,1)}, u32[]{:S(2)}, u32[]{:S(2)}) collective-permute-start(bf16[352,2048]{1,0:T(8,128)(2,1)} %pad_maximum_fusion.refs_0_), channel_id=1, source_target_pairs={{32,0},{48,16},{64,32},{80,48},{96,64},{112,80},{0,96},{16,112},{3... | collective-permute-start | bytes 4325384 | tf_op jit(solution)/shard_map/ppermute | solution.py:79
  177.7 50.2 %collective-permute-start.26 = (bf16[352,2048]{1,0:T(8,128)(2,1)}, bf16[352,2048]{1,0:T(8,128)(2,1)}, u32[]{:S(2)}, u32[]{:S(2)}) collective-permute-start(bf16[352,2048]{1,0:T(8,128)(2,1)} %pad_maximum_fusion.refs_0_), channel_id=1, source_target_pairs={{96,0},{112,16},{0,32},{16,48},{32,64},{48,80},{64,96},{80,112},{9... | collective-permute-start | bytes 4325384 | tf_op jit(solution)/shard_map/ppermute | solution.py:79
  188.9 45.4 %collective-permute-start.31 = (bf16[176,2048]{1,0:T(8,128)(2,1)}, bf16[176,2048]{1,0:T(8,128)(2,1)}, u32[]{:S(2)}, u32[]{:S(2)}) collective-permute-start(bf16[176,2048]{1,0:T(8,128)(2,1)} %collective-permute-done.29.refs_7_), channel_id=1, source_target_pairs={{32,0},{48,16},{64,32},{80,48},{96,64},{112,80},{0,96},{16,112},{3... | collective-permute-start | bytes 2162696 | tf_op jit(solution)/shard_map/ppermute | solution.py:79
  191.3 44.5 %collective-permute-start.33 = (bf16[176,2048]{1,0:T(8,128)(2,1)}, bf16[176,2048]{1,0:T(8,128)(2,1)}, u32[]{:S(2)}, u32[]{:S(2)}) collective-permute-start(bf16[176,2048]{1,0:T(8,128)(2,1)} %collective-permute-done.29.refs_7_), channel_id=1, source_target_pairs={{96,0},{112,16},{0,32},{16,48},{32,64},{48,80},{64,96},{80,112},{9... | collective-permute-start | bytes 2162696 | tf_op jit(solution)/shard_map/ppermute | solution.py:79
  226.2 53.6 %collective-permute-start.36 = (bf16[352,2048]{1,0:T(8,128)(2,1)}, bf16[352,2048]{1,0:T(8,128)(2,1)S(1)}, u32[]{:S(2)}, u32[]{:S(2)}) collective-permute-start(bf16[352,2048]{1,0:T(8,128)(2,1)} %pad_maximum_fusion.refs_0_), channel_id=1, source_target_pairs={{64,0},{80,16},{96,32},{112,48},{0,64},{16,80},{32,96},{48,112},{6... | collective-permute-start | bytes 4325384 | tf_op jit(solution)/shard_map/ppermute | solution.py:79
  227.8 51.9 %collective-permute-start.35 = (bf16[176,2048]{1,0:T(8,128)(2,1)}, bf16[176,2048]{1,0:T(8,128)(2,1)S(1)}, u32[]{:S(2)}, u32[]{:S(2)}) collective-permute-start(bf16[176,2048]{1,0:T(8,128)(2,1)} %collective-permute-done.29.refs_7_), channel_id=1, source_target_pairs={{64,0},{80,16},{96,32},{112,48},{0,64},{16,80},{32,96},{48,112},{6... | collective-permute-start | bytes 2162696 | tf_op jit(solution)/shard_map/ppermute | solution.py:79
  229.2 50.6 %collective-permute-start.30 = (bf16[352,2048]{1,0:T(8,128)(2,1)}, bf16[352,2048]{1,0:T(8,128)(2,1)}, u32[]{:S(2)}, u32[]{:S(2)}) collective-permute-start(bf16[352,2048]{1,0:T(8,128)(2,1)} %collective-permute-done.24.refs_2_), channel_id=1, source_target_pairs={{16,0},{0,16},{48,32},{32,48},{80,64},{64,80},{112,96},{96,112},{1... | collective-permute-start | bytes 4325384 | tf_op jit(solution)/shard_map/ppermute | solution.py:79
  234.4 54.4 %collective-permute-start.32 = (bf16[352,2048]{1,0:T(8,128)(2,1)}, bf16[352,2048]{1,0:T(8,128)(2,1)}, u32[]{:S(2)}, u32[]{:S(2)}) collective-permute-start(bf16[352,2048]{1,0:T(8,128)(2,1)} %collective-permute-done.26.refs_4_), channel_id=1, source_target_pairs={{16,0},{0,16},{48,32},{32,48},{80,64},{64,80},{112,96},{96,112},{1... | collective-permute-start | bytes 4325384 | tf_op jit(solution)/shard_map/ppermute | solution.py:79
  235.8 75.0 %collective-permute-start.34 = (bf16[352,2048]{1,0:T(8,128)(2,1)}, bf16[352,2048]{1,0:T(8,128)(2,1)}, u32[]{:S(2)}, u32[]{:S(2)}) collective-permute-start(bf16[352,2048]{1,0:T(8,128)(2,1)} %collective-permute-done.28.refs_6_), channel_id=1, source_target_pairs={{64,0},{80,16},{96,32},{112,48},{0,64},{16,80},{32,96},{48,112},{6... | collective-permute-start | bytes 4325384 | tf_op jit(solution)/shard_map/ppermute | solution.py:79
  397.4 52.6 %collective-permute-start.111 = (bf16[176,2048]{1,0:T(8,128)(2,1)}, bf16[176,2048]{1,0:T(8,128)(2,1)}, u32[]{:S(2)}, u32[]{:S(2)}) collective-permute-start(bf16[176,2048]{1,0:T(8,128)(2,1)} %get-tuple-element.145), channel_id=1, source_target_pairs={{64,0},{80,16},{96,32},{112,48},{0,64},{16,80},{32,96},{48,112},{6... | collective-permute-start | bytes 2162696 | tf_op jit(solution)/shard_map/ppermute | solution.py:79
  400.7 358.9 %reduce-scatter.4.cloned.1.call-start = ((), (), s32[]{:S(2)}) async-start(), calls=%async_computation.2 | async-start | bytes 4456448
  401.7 60.0 %collective-permute-start.112 = (bf16[176,2048]{1,0:T(8,128)(2,1)}, bf16[176,2048]{1,0:T(8,128)(2,1)S(1)}, u32[]{:S(2)}, u32[]{:S(2)}) collective-permute-start(bf16[176,2048]{1,0:T(8,128)(2,1)} %get-tuple-element.146), channel_id=1, source_target_pairs={{96,0},{112,16},{0,32},{16,48},{32,64},{48,80},{64,96},{80,112},{9... | collective-permute-start | bytes 2162696 | tf_op jit(solution)/shard_map/ppermute | solution.py:79
  401.8 76.1 %collective-permute-start.113 = (bf16[176,2048]{1,0:T(8,128)(2,1)}, bf16[176,2048]{1,0:T(8,128)(2,1)}, u32[]{:S(2)}, u32[]{:S(2)}) collective-permute-start(bf16[176,2048]{1,0:T(8,128)(2,1)} %get-tuple-element.147), channel_id=1, source_target_pairs={{32,0},{48,16},{64,32},{80,48},{96,64},{112,80},{0,96},{16,112},{3... | collective-permute-start | bytes 2162696 | tf_op jit(solution)/shard_map/ppermute | solution.py:79
  450.0 45.2 %collective-permute-start.102 = (bf16[352,2048]{1,0:T(8,128)(2,1)}, bf16[352,2048]{1,0:T(8,128)(2,1)}, u32[]{:S(2)}, u32[]{:S(2)}) collective-permute-start(bf16[352,2048]{1,0:T(8,128)(2,1)} %get-tuple-element.135), channel_id=1, source_target_pairs={{16,0},{0,16},{48,32},{32,48},{80,64},{64,80},{112,96},{96,112},{1... | collective-permute-start | bytes 4325384 | tf_op jit(solution)/shard_map/ppermute | solution.py:79
  454.2 79.5 %collective-permute-start.104 = (bf16[352,2048]{1,0:T(8,128)(2,1)}, bf16[352,2048]{1,0:T(8,128)(2,1)}, u32[]{:S(2)}, u32[]{:S(2)}) collective-permute-start(bf16[352,2048]{1,0:T(8,128)(2,1)} %get-tuple-element.137), channel_id=1, source_target_pairs={{16,0},{0,16},{48,32},{32,48},{80,64},{64,80},{112,96},{96,112},{1... | collective-permute-start | bytes 4325384 | tf_op jit(solution)/shard_map/ppermute | solution.py:79
  456.2 77.5 %collective-permute-start.106 = (bf16[352,2048]{1,0:T(8,128)(2,1)}, bf16[352,2048]{1,0:T(8,128)(2,1)}, u32[]{:S(2)}, u32[]{:S(2)}) collective-permute-start(bf16[352,2048]{1,0:T(8,128)(2,1)} %get-tuple-element.139), channel_id=1, source_target_pairs={{64,0},{80,16},{96,32},{112,48},{0,64},{16,80},{32,96},{48,112},{6... | collective-permute-start | bytes 4325384 | tf_op jit(solution)/shard_map/ppermute | solution.py:79
  462.6 123.0 %collective-permute-start.53 = (bf16[512,2176]{1,0:T(8,128)(2,1)}, bf16[512,2176]{1,0:T(8,128)(2,1)}, u32[]{:S(2)}, u32[]{:S(2)}) collective-permute-start(bf16[512,2176]{1,0:T(8,128)(2,1)} %constant_dynamic-update-slice_fusion.24.a), channel_id=1, source_target_pairs={{1,0},{0,1},{3,2},{2,3},{5,4},{4,5},{7,6},{6,7},{9,8},{8,9},{11,10... | collective-permute-start | bytes 6684680 | tf_op jit(solution)/shard_map/ppermute | solution.py:72
  477.9 81.3 %collective-permute-start.108 = (bf16[176,2048]{1,0:T(8,128)(2,1)}, bf16[176,2048]{1,0:T(8,128)(2,1)}, u32[]{:S(2)}, u32[]{:S(2)}) collective-permute-start(bf16[176,2048]{1,0:T(8,128)(2,1)} %get-tuple-element.141), channel_id=1, source_target_pairs={{64,0},{80,16},{96,32},{112,48},{0,64},{16,80},{32,96},{48,112},{6... | collective-permute-start | bytes 2162696 | tf_op jit(solution)/shard_map/ppermute | solution.py:79
  495.2 64.0 %collective-permute-start.109 = (bf16[176,2048]{1,0:T(8,128)(2,1)}, bf16[176,2048]{1,0:T(8,128)(2,1)}, u32[]{:S(2)}, u32[]{:S(2)}) collective-permute-start(bf16[176,2048]{1,0:T(8,128)(2,1)} %get-tuple-element.142), channel_id=1, source_target_pairs={{96,0},{112,16},{0,32},{16,48},{32,64},{48,80},{64,96},{80,112},{9... | collective-permute-start | bytes 2162696 | tf_op jit(solution)/shard_map/ppermute | solution.py:79
  533.7 48.4 %collective-permute-start.114 = (bf16[176,2048]{1,0:T(8,128)(2,1)}, bf16[176,2048]{1,0:T(8,128)(2,1)}, u32[]{:S(2)}, u32[]{:S(2)}) collective-permute-start(bf16[176,2048]{1,0:T(8,128)(2,1)} %add_convert_fusion.1), channel_id=1, source_target_pairs={{16,0},{0,16},{48,32},{32,48},{80,64},{64,80},{112,96},{96,112},{1... | collective-permute-start | bytes 2162696 | tf_op jit(solution)/shard_map/ppermute | solution.py:79
  559.2 126.3 %collective-permute-start.101 = (bf16[352,2048]{1,0:T(8,128)(2,1)}, bf16[352,2048]{1,0:T(8,128)(2,1)}, u32[]{:S(2)}, u32[]{:S(2)}) collective-permute-start(bf16[352,2048]{1,0:T(8,128)(2,1)} %get-tuple-element.133), channel_id=1, source_target_pairs={{64,0},{80,16},{96,32},{112,48},{0,64},{16,80},{32,96},{48,112},{6... | collective-permute-start | bytes 4325384 | tf_op jit(solution)/shard_map/ppermute | solution.py:79
  634.6 93.7 %collective-permute-start.103 = (bf16[352,2048]{1,0:T(8,128)(2,1)}, bf16[352,2048]{1,0:T(8,128)(2,1)S(1)}, u32[]{:S(2)}, u32[]{:S(2)}) collective-permute-start(bf16[352,2048]{1,0:T(8,128)(2,1)} %add.688), channel_id=1, source_target_pairs={{96,0},{112,16},{0,32},{16,48},{32,64},{48,80},{64,96},{80,112},{9... | collective-permute-start | bytes 4325384 | tf_op jit(solution)/shard_map/ppermute | solution.py:79
  634.6 47.8 %collective-permute-start.54 = (bf16[512,2048]{1,0:T(8,128)(2,1)}, bf16[512,2048]{1,0:T(8,128)(2,1)S(1)}, u32[]{:S(2)}, u32[]{:S(2)}) collective-permute-start(bf16[512,2048]{1,0:T(8,128)(2,1)} %convolution_convert_fusion), channel_id=1, source_target_pairs={{1,0},{0,1},{3,2},{2,3},{5,4},{4,5},{7,6},{6,7},{9,8},{8,9},{11,10... | collective-permute-start | bytes 6291464 | tf_op jit(solution)/shard_map/ppermute | solution.py:72
  655.8 75.3 %collective-permute-start.105 = (bf16[352,2048]{1,0:T(8,128)(2,1)}, bf16[352,2048]{1,0:T(8,128)(2,1)S(1)}, u32[]{:S(2)}, u32[]{:S(2)}) collective-permute-start(bf16[352,2048]{1,0:T(8,128)(2,1)} %add.690), channel_id=1, source_target_pairs={{32,0},{48,16},{64,32},{80,48},{96,64},{112,80},{0,96},{16,112},{3... | collective-permute-start | bytes 4325384 | tf_op jit(solution)/shard_map/ppermute | solution.py:79
  680.0 52.3 %collective-permute-start.107 = (bf16[352,2048]{1,0:T(8,128)(2,1)S(1)}, bf16[352,2048]{1,0:T(8,128)(2,1)S(1)}, u32[]{:S(2)}, u32[]{:S(2)}) collective-permute-start(bf16[352,2048]{1,0:T(8,128)(2,1)S(1)} %copy-done.73), channel_id=1, source_target_pairs={{16,0},{0,16},{48,32},{32,48},{80,64},{64,80},{112,96},{96,112},{1... | collective-permute-start | bytes 4325384 | tf_op jit(solution)/shard_map/ppermute | solution.py:79
  (188 other events, 2456.7 us)
Sparse Core Ops, SparseCore 0:
  17.3 82.3 all-gather.1
  400.8 197.8 all-reduce.3
  602.8 85.3 reduce-scatter.3

commit v2 on v1

v2 whole, which is shorter than its diff:
```python
import functools
import math

import jax
import jax.numpy as jnp
from jax import lax
from jax.experimental import pallas as pl
from jax.experimental.pallas import tpu as pltpu
from jax.sharding import PartitionSpec as P

D = 2048
NOPE = 128
ROPE = 64
VDIM = 128
LATENT = 512
TOPK = 6
EXPERTS = 16
IMG = 256
SPANS = 2
LEN = 1024
CAP = 480
FS = 176
LW = 36
LW48 = 48
LP = 80
LX = 640
RB = 128
PW = D + 128
QW = D + LX
FA = 3 * FS
BF = jnp.bfloat16
F32 = jnp.float32
EPS = 1e-06
MASKED = -1e30
SCALE = (NOPE + ROPE) ** (-0.5)
MB = 1024 * 1024

NN = (((1,), (0,)), ((), ()))
NT = (((1,), (1,)), ((), ()))
TN = (((0,), (0,)), ((), ()))


def dot(a, b, dims=NN):
    return lax.dot_general(a, b, dims, preferred_element_type=F32)


VM = pl.BlockSpec(memory_space=pltpu.VMEM)
SM = pl.BlockSpec(memory_space=pltpu.SMEM)


def whole(kernel, outs, ins, limit, flops=0):
    arrays = [i[0] if isinstance(i, tuple) else i for i in ins]
    specs = [i[1] if isinstance(i, tuple) else VM for i in ins]
    return pl.pallas_call(
        kernel,
        out_shape=outs,
        in_specs=specs,
        out_specs=[VM] * len(outs),
        compiler_params=pltpu.CompilerParams(vmem_limit_bytes=limit * MB),
        cost_estimate=LIGHT,
    )(*arrays)


LIGHT = pl.CostEstimate(flops=1, bytes_accessed=1, transcendentals=0)


def sds(shape, dtype):
    return jax.ShapeDtypeStruct(shape, dtype)


def recv_t(a, zh=0, y=0, c=0):
    pairs = []
    for i in range(16):
        z, r, k = i // 8, i // 2 % 4, i % 2
        pairs.append((((z + zh) % 2) * 8 + ((r + y) % 4) * 2 + (k + c) % 2, i))
    return lax.ppermute(a, "tensor", pairs)


def recv_d(a, x=0, z=0):
    pairs = []
    for i in range(8):
        pairs.append((((i // 2 + x) % 4) * 2 + (i % 2 + z) % 2, i))
    return lax.ppermute(a, "dp", pairs)


def from_y(a):
    y1, y3 = recv_t(a, y=1), recv_t(a, y=-1)
    across, y1, y3 = sync(a, y1, y3)
    return [y1, recv_t(across, y=2), y3]


def to_y(b):
    y1, y3 = recv_t(b[1], y=-1), recv_t(b[3], y=1)
    across, y1, y3 = sync(b[2], y1, y3)
    return [y1, recv_t(across, y=2), y3]


def cat(*arrays):
    return jnp.concatenate(arrays, axis=0)


def split_sum(keep, got, starts):
    width = keep.shape[1]

    def kernel(s, a, b, *outs):
        for i, o in enumerate(outs):
            rows = pl.ds(pl.multiple_of(s[i], RB), RB)
            o[...] = (a[rows, :].astype(F32) + b[rows, :].astype(F32)).astype(BF)

    return whole(kernel, [sds((RB, width), BF)] * 4, [(starts, SM), keep, got], 16)


def add(*terms):
    return sum(t.astype(F32) for t in terms).astype(BF)


def swap_x(a):
    return lax.ppermute(a, "dp", [(i, ((i // 2) ^ 1) * 2 + i % 2) for i in range(8)])


def halves(a, k):
    n = a.shape[1] // 2
    return lax.dynamic_slice_in_dim(a, k * n, n, 1), lax.dynamic_slice_in_dim(a, (1 - k) * n, n, 1)


def sum_d(v, turn):
    if turn == 0:
        got = recv_d(v, z=1)
    elif turn == 1:
        got = swap_x(v)
    else:
        got = recv_d(v, x=2)
    return (v.astype(F32) + got.astype(F32)).astype(v.dtype)


def sync(*arrays):
    return lax.optimization_barrier(arrays)


def rotary_tables(length):
    position = jnp.arange(length, dtype=F32)
    frequency = jnp.exp(jnp.arange(ROPE // 2, dtype=F32) * (-2.0 * math.log(10000.0) / ROPE))
    angles = position[:, None] * frequency[None, :]
    return jnp.cos(angles), jnp.sin(angles)


def rotate(v, cos, sin):
    a, b = v[:, : ROPE // 2], v[:, ROPE // 2 :]
    return jnp.concatenate([a * cos - b * sin, b * cos + a * sin], axis=-1)


def unrotate(v, cos, sin):
    a, b = v[:, : ROPE // 2], v[:, ROPE // 2 :]
    return jnp.concatenate([a * cos + b * sin, b * cos - a * sin], axis=-1)


QB = 256


def probs_of(starts, first, qn, qr, kn, kr):
    scores = (dot(qn, kn, NT) + dot(qr, kr, NT)) * SCALE
    i = first + lax.broadcasted_iota(jnp.int32, (QB, 1), 0)
    j = lax.broadcasted_iota(jnp.int32, (1, LEN), 1)
    allowed = j <= i
    for n in range(SPANS):
        s = starts[0, n]
        row_in = (i >= s) & (i < s + IMG)
        col_in = (j >= s) & (j < s + IMG)
        allowed = allowed | (row_in & col_in)
    scores = jnp.where(allowed, scores, MASKED)
    raised = jnp.exp(scores - jnp.max(scores, axis=-1, keepdims=True))
    return raised / jnp.sum(raised, axis=-1, keepdims=True)


def attend(starts, qn, qr, kn, kr, v):
    def kernel(s, qn, qr, kn, kr, v, o):
        p = probs_of(s, pl.program_id(0) * QB, qn[...], qr[...], kn[...], kr[...])
        o[...] = dot(p.astype(BF), v[...]).astype(BF)

    rows = lambda w: pl.BlockSpec((QB, w), lambda i: (i, 0))
    full = lambda w: pl.BlockSpec((LEN, w), lambda i: (0, 0))
    return pl.pallas_call(
        kernel,
        grid=(LEN // QB,),
        out_shape=sds((LEN, VDIM), BF),
        in_specs=[SM, rows(NOPE), rows(ROPE), full(NOPE), full(ROPE), full(VDIM)],
        out_specs=rows(VDIM),
        compiler_params=pltpu.CompilerParams(vmem_limit_bytes=14 * MB),
        cost_estimate=LIGHT,
    )(starts, qn, qr, kn, kr, v)


def half_turn(v):
    return jnp.concatenate([v[:, ROPE // 2 :], v[:, : ROPE // 2]], axis=1)


def attend_back(starts, qn, qr, kn, kr, v, mg, cos2, sin2):
    def kernel(s, qn, qr, kn, kr, v, mg, cos, sin, qg, eg, rg, dkn, dkr, dv):
        step = pl.program_id(0)

        @pl.when(step == 0)
        def _():
            dkn[...] = jnp.zeros_like(dkn)
            dkr[...] = jnp.zeros_like(dkr)
            dv[...] = jnp.zeros_like(dv)

        p = probs_of(s, step * QB, qn[...], qr[...], kn[...], kr[...])
        m = mg[...]
        pg = dot(m, v[...], NT)
        sg = (p * (pg - jnp.sum(pg * p, axis=-1, keepdims=True))).astype(BF)
        qg[:, :NOPE] = (dot(sg, kn[...]) * SCALE).astype(BF)
        dqr = dot(sg, kr[...]) * SCALE
        rows = pl.ds(step * QB, QB)
        qg[:, NOPE:] = (dqr * cos[rows, :] - half_turn(dqr) * sin[rows, :]).astype(BF)
        dkn[...] += dot(sg, qn[...], TN) * SCALE
        dkr[...] += dot(sg, qr[...], TN) * SCALE
        dv[...] += dot(p.astype(BF), m, TN)

        @pl.when(step == LEN // QB - 1)
        def _():
            eg[:, :NOPE] = dkn[...].astype(BF)
            eg[:, NOPE:] = dv[...].astype(BF)
            d = dkr[...]
            rg[...] = (d * cos[...] - half_turn(d) * sin[...]).astype(BF)

    rows = lambda w: pl.BlockSpec((QB, w), lambda i: (i, 0))
    full = lambda w: pl.BlockSpec((LEN, w), lambda i: (0, 0))
    return pl.pallas_call(
        kernel,
        grid=(LEN // QB,),
        out_shape=[sds((LEN, w), BF) for w in (NOPE + ROPE, NOPE + VDIM, ROPE)],
        in_specs=[SM, rows(NOPE), rows(ROPE), full(NOPE), full(ROPE), full(VDIM), rows(VDIM), full(ROPE), full(ROPE)],
        out_specs=[rows(NOPE + ROPE), full(NOPE + VDIM), full(ROPE)],
        scratch_shapes=[pltpu.VMEM((LEN, w), F32) for w in (NOPE, ROPE, VDIM)],
        compiler_params=pltpu.CompilerParams(vmem_limit_bytes=18 * MB),
        cost_estimate=LIGHT,
    )(starts, qn, qr, kn, kr, v, mg, cos2, sin2)


def keys(normed1, place, lat_half, lat_other, gain, w_expand, cos2, sin2):
    n = lat_half.shape[0]

    def kernel(n1, place, a, b, gain, we, cos, sin, wl, lat, inv, comp, kn, kr, v):
        @pl.when(pl.program_id(0) == 0)
        def _():
            wl[...] = (dot(place[:, :n], a[...]) + dot(place[:, n:], b[...])).astype(BF)

        t = dot(n1[...], wl[...], NT).astype(BF)
        lat[...] = t
        t = t.astype(F32)
        c = t[:, :LATENT]
        r = lax.rsqrt(jnp.mean(c * c, axis=-1, keepdims=True) + EPS)
        c = (c * r * gain[...]).astype(BF)
        inv[...] = r
        comp[...] = c
        e = dot(c, we[...]).astype(BF)
        kn[...] = e[:, :NOPE]
        v[...] = e[:, NOPE:]
        d = t[:, LATENT : LATENT + ROPE]
        kr[...] = (d * cos[...] + half_turn(d) * sin[...]).astype(BF)

    rows = lambda w: pl.BlockSpec((QB, w), lambda i: (i, 0))
    full = lambda a: pl.BlockSpec(a.shape, lambda i: (0, 0))
    outs = [(LX, BF), (1, F32), (LATENT, BF), (NOPE, BF), (ROPE, BF), (VDIM, BF)]
    return pl.pallas_call(
        kernel,
        grid=(LEN // QB,),
        out_shape=[sds((LX, D), BF)] + [sds((LEN, w), t) for w, t in outs],
        in_specs=[rows(D), full(place), full(lat_half), full(lat_other), full(gain), full(w_expand), rows(ROPE), rows(ROPE)],
        out_specs=[pl.BlockSpec((LX, D), lambda i: (0, 0))] + [rows(w) for w, _ in outs],
        compiler_params=pltpu.CompilerParams(vmem_limit_bytes=26 * MB),
        cost_estimate=LIGHT,
    )(normed1, place, lat_half, lat_other, gain, w_expand, cos2, sin2)


def attention_part(which, mixed, w_out):
    def kernel(which, m, w, o):
        o[...] = dot(m[...], w[...]).astype(BF)

    return pl.pallas_call(
        kernel,
        grid_spec=pltpu.PrefetchScalarGridSpec(
            num_scalar_prefetch=1,
            grid=(2,),
            in_specs=[
                pl.BlockSpec((QB, VDIM), lambda i, which: (which[0] * 2 + i, 0)),
                pl.BlockSpec((VDIM, D), lambda i, which: (0, 0)),
            ],
            out_specs=pl.BlockSpec((QB, D), lambda i, which: (i, 0)),
        ),
        out_shape=sds((LEN // 2, D), BF),
        compiler_params=pltpu.CompilerParams(vmem_limit_bytes=16 * MB),
        cost_estimate=LIGHT,
    )(which, mixed, w_out)


def softmax(logits):
    e = jnp.exp(logits - jnp.max(logits, axis=-1, keepdims=True))
    return e / jnp.sum(e, axis=-1, keepdims=True)


def total_of(refs):
    t = refs[0][...].astype(F32)
    for r in refs[1:]:
        t = t + r[...].astype(F32)
    return t


def rows_mid(terms, x, gain, w_router):
    def kernel(a, b, x, gain, wr, hid, nrm, inv, probs):
        h = x[...].astype(F32) + total_of((a, b))
        r = lax.rsqrt(jnp.mean(h * h, axis=-1, keepdims=True) + EPS)
        n = (h * r * gain[...]).astype(BF)
        hid[...] = h
        nrm[...] = n
        inv[...] = r
        probs[...] = softmax(dot(n, wr[...]))

    outs = [sds((RB, D), F32), sds((RB, D), BF), sds((RB, 1), F32), sds((RB, EXPERTS), F32)]
    return whole(kernel, outs, [*terms, x, gain, w_router], 16)


def experts_front(starts, me, half, other, w_router, w_router_t, rank_row, grad, gu, dn):
    def kernel(s, me, a, b, wr, wrt, rank, g, gu, dn, n2, col, x, dy, dyg, dw, out, dx):
        lane = lax.broadcasted_iota(jnp.int32, (1, EXPERTS), 1)
        for n, ref in enumerate((a, b)):
            p = softmax(dot(ref[...], wr[...]))
            p = jnp.sum(jnp.where(lane == me[0], p, 0.0), axis=-1, keepdims=True)
            for i in range(4):
                rows = pl.ds(pl.multiple_of(s[n * 4 + i], RB), RB)
                n2[rows, :] = ref[i * RB : (i + 1) * RB]
                col[rows, :] = p[i * RB : (i + 1) * RB]
        nv, gv = n2[...], g[...]
        t = dot(wrt[...], nv, NT)
        t = jnp.exp(t - jnp.max(t, axis=0, keepdims=True))
        t = t / jnp.sum(t, axis=0, keepdims=True)
        mine = lax.broadcasted_iota(jnp.int32, (EXPERTS, 1), 0) == me[0]
        row = jnp.sum(jnp.where(mine, t, 0.0), axis=0, keepdims=True)
        hit = lax.broadcasted_iota(jnp.int32, (CAP, 1), 0) == rank[...]
        gate = jnp.sum(jnp.where(hit, row, 0.0), axis=-1, keepdims=True)
        pick = jnp.where(hit, 1.0, 0.0).astype(BF)
        x[...] = dot(pick, nv).astype(BF)
        got = dot(pick, gv)
        dyg[...] = got.astype(BF)
        dy[...] = (got * gate).astype(BF)
        h, da = ffn_back(nv, gv, gu[...], dn[...])
        dw[: 2 * FS] = dot(da, nv).astype(BF)
        dw[2 * FS :] = dot(h, gv).astype(BF)
        out[...] = dot(h, dn[...], TN).astype(BF)
        dx[...] = dot(da, gu[...], TN).astype(BF)

    outs = [sds((LEN, D), BF), sds((LEN, 1), F32)] + [sds((CAP, D), BF)] * 3
    outs += [sds((FA, D), BF)] + [sds((LEN, D), BF)] * 2
    ins = [(starts, SM), (me, SM), half, other, w_router, w_router_t, rank_row, grad, gu, dn]
    return whole(kernel, outs, ins, 56)


ANY = pl.BlockSpec(memory_space=pl.ANY)
FLOPS = 2 * 9 * FS * D


def ffn_back(x, dy, gu, dn):
    act = dot(gu, x, NT)
    g, u = act[:FS], act[FS:]
    sg = jax.nn.sigmoid(g)
    h = (g * sg * u).astype(BF)
    dh = dot(dn, dy, NT)
    dg = (dh * u * sg * (1.0 + g * (1.0 - sg))).astype(BF)
    du = (dh * g * sg).astype(BF)
    return h, jnp.concatenate([dg, du], axis=0)


def experts(x, dy, chunks, last=None):
    n = len(chunks)
    n_in = 2 if last is None else 6
    pieces = [(i, first, a) for i, c in enumerate(chunks) for first, a in zip((0, 2 * FS), c)]
    m = len(pieces)

    def kernel(*refs):
        if last is None:
            x, dy = refs[:2]
        else:
            me, x, dy, dyg, out0, dx0 = refs[:6]
        w, outs, (out, dx) = refs[n_in : n_in + m], refs[n_in + m : n_in + 2 * m], refs[n_in + 2 * m : n_in + 2 * m + 2]
        wgu, wdn, hs, das, grads, sem_in, sem_out = refs[n_in + 2 * m + 2 :]
        loads = [[] for _ in range(n)]
        for k, (i, first, a) in enumerate(pieces):
            for part, (size, ref) in enumerate(((2 * FS, wgu), (FS, wdn))):
                at = 2 * FS * part - first
                if 0 <= at < a.shape[0]:
                    src = w[k].at[pl.ds(at, size)]
                    loads[i].append(
                        pltpu.make_async_copy(src, ref.at[pl.ds(size * i, size)], sem_in.at[2 * i + part])
                    )
        for c in loads:
            for d in c:
                d.start()
        xv, dyv = x[...], dy[...]
        stores = []
        for i in range(n):
            for c in loads[i]:
                c.wait()
            h, da = ffn_back(xv, dyv, wgu[2 * FS * i : 2 * FS * (i + 1)], wdn[FS * i : FS * (i + 1)])
            hs[FS * i : FS * (i + 1)] = h
            das[2 * FS * i : 2 * FS * (i + 1)] = da
            grads[i, : 2 * FS] = dot(da, xv).astype(BF)
            grads[i, 2 * FS :] = dot(h, dyv).astype(BF)
            for k, (o, first, a) in enumerate(pieces):
                if o == i:
                    src = grads.at[i, pl.ds(first, a.shape[0])]
                    stores.append(pltpu.make_async_copy(src, outs[k], sem_out.at[k]))
                    stores[-1].start()
        sum_o = dot(hs[...], wdn[...], TN)
        sum_d = dot(das[...], wgu[...], TN)
        if last is None:
            out[...] = sum_o
            dx[...] = sum_d
        else:
            so = (out0[...] + sum_o).astype(BF)
            out[...] = so
            dx[:, :D] = (dx0[...] + sum_d).astype(BF)
            gg = jnp.sum(so.astype(F32) * dyg[...].astype(F32), axis=-1, keepdims=True)
            lane = lax.broadcasted_iota(jnp.int32, (1, 128), 1)
            dx[:, D:] = jnp.where(lane == me[0], gg, 0.0).astype(BF)
        for c in stores:
            c.wait()

    if last is None:
        arrays, specs = [x, dy], [VM] * 2
        ends = [sds((CAP, D), F32)] * 2
    else:
        dyg, out, dx, me = last
        arrays, specs = [me, x, dy, dyg, out, dx], [SM] + [VM] * 5
        ends = [sds((CAP, D), BF), sds((CAP, PW), BF)]
    res = pl.pallas_call(
        kernel,
        out_shape=[sds(a.shape, BF) for _, _, a in pieces] + ends,
        in_specs=specs + [ANY] * m,
        out_specs=[ANY] * m + [VM] * 2,
        scratch_shapes=[
            pltpu.VMEM((2 * FS * n, D), BF),
            pltpu.VMEM((FS * n, D), BF),
            pltpu.VMEM((FS * n, CAP), BF),
            pltpu.VMEM((2 * FS * n, CAP), BF),
            pltpu.VMEM((n, FA, D), BF),
            pltpu.SemaphoreType.DMA((2 * n,)),
            pltpu.SemaphoreType.DMA((m,)),
        ],
        compiler_params=pltpu.CompilerParams(vmem_limit_bytes=52 * MB),
        cost_estimate=LIGHT,
    )(*arrays, *[a for _, _, a in pieces])
    return res[:m], res[m], res[m + 1]


def combine_grad(which, rank_col, dx, shared_dx):
    rows_at = 256

    def kernel(which, rank, dx, sd, o):
        hit = rank[...] == lax.broadcasted_iota(jnp.int32, (1, CAP), 1)
        pick = jnp.where(hit, 1.0, 0.0).astype(BF)
        t = dot(pick, dx[...])
        o[:, :D] = (t[:, :D] + sd[...].astype(F32)).astype(BF)
        o[:, D:] = t[:, D:].astype(BF)

    at = lambda w: pl.BlockSpec((rows_at, w), lambda i, which: (which[0] * 2 + i, 0))
    return pl.pallas_call(
        kernel,
        grid_spec=pltpu.PrefetchScalarGridSpec(
            num_scalar_prefetch=1,
            grid=(2,),
            in_specs=[at(1), pl.BlockSpec((CAP, PW), lambda i, which: (0, 0)), at(D)],
            out_specs=pl.BlockSpec((rows_at, PW), lambda i, which: (i, 0)),
        ),
        out_shape=sds((LEN // 2, PW), BF),
        compiler_params=pltpu.CompilerParams(vmem_limit_bytes=40 * MB),
        cost_estimate=LIGHT,
    )(which, rank_col, dx, shared_dx)


def combine_out(rank_col, probs_col, slot_out, shared_out, mixed, w_out):
    rows_at = 256

    def kernel(rank, probs, so, sh, m, w, o):
        hit = rank[...] == lax.broadcasted_iota(jnp.int32, (1, CAP), 1)
        pick = jnp.where(hit, 1.0, 0.0).astype(BF)
        t = dot(pick, so[...]) * probs[...] + sh[...].astype(F32)
        t = (t + dot(m[...], w[...])).astype(BF)
        for i in range(D // 128):
            o[i] = t[:, 128 * i : 128 * (i + 1)]

    at = lambda w: pl.BlockSpec((rows_at, w), lambda i: (i, 0))
    return pl.pallas_call(
        kernel,
        grid=(LEN // rows_at,),
        out_shape=sds((D // 128, LEN, 128), BF),
        in_specs=[
            at(1),
            at(1),
            pl.BlockSpec((CAP, D), lambda i: (0, 0)),
            at(D),
            at(VDIM),
            pl.BlockSpec((VDIM, D), lambda i: (0, 0)),
        ],
        out_specs=pl.BlockSpec((D // 128, rows_at, 128), lambda i: (0, i, 0)),
        compiler_params=pltpu.CompilerParams(vmem_limit_bytes=24 * MB),
        cost_estimate=LIGHT,
    )(rank_col, probs_col, slot_out, shared_out, mixed, w_out)


def normed1_part(which, query_grad, expanded_grad, rope_grad, w_query, w_expand):
    rows_at = 256

    def kernel(which, q, e, r, wq, we, o):
        o[:, :D] = dot(q[...], wq[...]).astype(BF)
        o[:, D : D + LATENT] = dot(e[...], we[...], NT).astype(BF)
        o[:, D + LATENT :] = jnp.concatenate([r[...], jnp.zeros((rows_at, LX - LATENT - ROPE), BF)], axis=1)

    at = lambda w: pl.BlockSpec((rows_at, w), lambda i, which: (which[0] * 2 + i, 0))
    full = lambda a: pl.BlockSpec(a.shape, lambda i, which: (0, 0))
    return pl.pallas_call(
        kernel,
        grid_spec=pltpu.PrefetchScalarGridSpec(
            num_scalar_prefetch=1,
            grid=(2,),
            in_specs=[at(NOPE + ROPE), at(NOPE + VDIM), at(ROPE), full(w_query), full(w_expand)],
            out_specs=pl.BlockSpec((rows_at, QW), lambda i, which: (i, 0)),
        ),
        out_shape=sds((LEN // 2, QW), BF),
        compiler_params=pltpu.CompilerParams(vmem_limit_bytes=14 * MB),
        cost_estimate=LIGHT,
    )(which, query_grad, expanded_grad, rope_grad, w_query, w_expand)


def norm_back(v, inv, gain, incoming):
    weighted = incoming * gain
    inner = jnp.mean(weighted * v, axis=-1, keepdims=True)
    return inv * weighted - v * (inv * inv * inv) * inner, jnp.sum(incoming * v * inv, axis=0, keepdims=True)


def rows_two(terms, hidden, inv, probs, grad, gain, w_router_t):
    def kernel(a, b, h, inv, p, g, gain, wr, hg, pay, gg):
        t = total_of((a, b))
        gates = t[:, D : D + EXPERTS]
        pv = p[...]
        lg = (pv * (gates - jnp.sum(pv * gates, axis=-1, keepdims=True))).astype(BF)
        n2 = t[:, :D] + dot(lg, wr[...])
        r, gain_grad = norm_back(h[...], inv[...], gain[...], n2)
        r = r + g[...].astype(F32)
        hg[...] = r
        pay[:, :D] = r.astype(BF)
        pay[:, D:] = jnp.concatenate([lg, jnp.zeros((RB, 128 - EXPERTS), BF)], axis=1)
        gg[...] = gain_grad

    outs = [sds((RB, D), F32), sds((RB, PW), BF), sds((1, D), F32)]
    return whole(kernel, outs, [*terms, hidden, inv, probs, grad, gain, w_router_t], 16)


GAINS = 2 * D + LATENT
FREE = LX - LATENT - ROPE


def rows_one(terms, w_lat, x, inv, hg, gain, latent, inv_lat, gain_lat, gain_two):
    def kernel(a, b, wl, x, inv, hg, gain, lat, inv_lat, gain_lat, two, o):
        t = total_of((a, b))
        head, g_lat = norm_back(lat[:, :LATENT].astype(F32), inv_lat[...], gain_lat[...], t[:, D : D + LATENT])
        lg = jnp.concatenate([head, t[:, D + LATENT :]], axis=1).astype(BF)
        t = t[:, :D] + dot(lg, wl[...])
        r, g_one = norm_back(x[...].astype(F32), inv[...], gain[...], t)
        o[:, :D] = (hg[...] + r).astype(BF)
        o[:, D : D + LATENT] = lg[:, :LATENT]
        g = jnp.concatenate([g_one, two[...], g_lat], axis=1)
        g = [g[:, FREE * i : FREE * (i + 1)] for i in range(GAINS // FREE)]
        g = jnp.concatenate(g + [jnp.zeros((RB - len(g), FREE), F32)], axis=0)
        o[:, D + LATENT :] = jnp.concatenate([lg[:, LATENT : LATENT + ROPE], g.astype(BF)], axis=1)

    ins = [*terms, w_lat, x, inv, hg, gain, latent, inv_lat, gain_lat, gain_two]
    return whole(kernel, [sds((RB, QW), BF)], ins, 20)[0]


def mixed_back(starts, half, other, w_out):
    def kernel(s, a, b, w, o):
        for n, ref in enumerate((a, b)):
            t = dot(ref[:, :D], w[...], NT).astype(BF)
            for i in range(4):
                rows = pl.ds(pl.multiple_of(s[n * 4 + i], RB), RB)
                o[rows, :] = t[i * RB : (i + 1) * RB]

    return whole(kernel, [sds((LEN, VDIM), BF)], [(starts, SM), half, other, w_out], 16, 2 * LEN * D * VDIM)[0]


def output_grads(starts, half, other, mixed, normed2):
    def kernel(s, a, b, m, n2, wo, wr):
        sum_o = jnp.zeros((VDIM, D), F32)
        sum_r = jnp.zeros((EXPERTS, D), F32)
        for n, ref in enumerate((a, b)):
            at = [pl.ds(pl.multiple_of(s[n * 4 + i], RB), RB) for i in range(4)]
            mix = jnp.concatenate([m[r, :] for r in at], axis=0)
            sum_o = sum_o + dot(mix, ref[:, :D], TN)
            for i, r in enumerate(at):
                lg = ref[i * RB : (i + 1) * RB, D:]
                sum_r = sum_r + dot(lg, n2[r, :], TN)[:EXPERTS]
        wo[...] = sum_o.astype(BF)
        wr[...] = sum_r.astype(BF)

    outs = [sds((VDIM, D), BF), sds((EXPERTS, D), BF)]
    return whole(kernel, outs, [(starts, SM), half, other, mixed, normed2], 24, 2 * LEN * D * 256)


def column_blocks(offsets, blocks):
    for i, ref in enumerate(blocks):
        for j in range(2):
            off = pl.multiple_of(offsets[2 * i + j], 256)
            yield off, lambda a, b, ref=ref, j=j: ref[a:b, 256 * j : 256 * (j + 1)].astype(F32)


def finish_rest(offsets, blocks):
    def kernel(off, *refs):
        wq, wo, we, wr = refs[4:]
        for at, block in column_blocks(off, refs[:4]):
            cols = pl.ds(at, 256)
            wq[:, cols] = block(0, 192)
            wo[:, cols] = block(192, 320)
            we[pl.ds(pl.multiple_of(at // 4, 64), 64), :] = block(320, 384)
            wr[:, cols] = block(384, 400)

    outs = [sds((192, D), F32), sds((VDIM, D), F32), sds((LATENT, 256), F32), sds((EXPERTS, D), F32)]
    return whole(kernel, outs, [(offsets, SM), *blocks], 16)


def finish_shared(offsets, near, far):
    def kernel(off, a, b, gate, up, down):
        refs = [r.at[:, 512 * i : 512 * (i + 1)] for r in (a, b) for i in range(2)]
        for at, block in column_blocks(off, refs):
            cols = pl.ds(at, 256)
            gate[:, cols] = block(0, FS)
            up[:, cols] = block(FS, 2 * FS)
            down[:, cols] = block(2 * FS, 3 * FS)

    return whole(kernel, [sds((FS, D), F32)] * 3, [(offsets, SM), near, far], 16)


def finish_experts(gu, dn):
    def kernel(*refs):
        gu, dn, (gate, up, down) = refs[:5], refs[5:10], refs[10:]
        t = total_of(gu)
        gate[...] = t[:FS]
        up[...] = t[FS:]
        down[...] = total_of(dn)

    return whole(kernel, [sds((FS, D), F32)] * 3, [*gu, *dn], 24)


def latent_w_grad(starts, half, other, normed1, pick):
    def kernel(s, a, b, n1, pick, o, gains, parts):
        total = jnp.zeros((LW48, D), F32)
        for n, ref in enumerate((a, b)):
            at = [pl.multiple_of(s[n * 4 + i], RB) for i in range(4)]
            rows = jnp.concatenate([n1[pl.ds(r, RB), :] for r in at], axis=0)
            own = dot(pick[...], ref[:, D:], NT).astype(BF)
            total = total + dot(own, rows)
            for i, r in enumerate(at):
                parts[pl.ds(r, RB), :] = ref[i * RB : (i + 1) * RB, QW - 128 :].astype(F32)
        o[...] = total.astype(BF)
        g = parts[:RB]
        for i in range(1, LEN // RB):
            g = g + parts[i * RB : (i + 1) * RB]
        gains[...] = g

    return pl.pallas_call(
        kernel,
        out_shape=[sds((LW48, D), BF), sds((RB, 128), F32)],
        in_specs=[SM, VM, VM, VM, VM],
        out_specs=[VM, VM],
        scratch_shapes=[pltpu.VMEM((LEN, 128), F32)],
        compiler_params=pltpu.CompilerParams(vmem_limit_bytes=24 * MB),
        cost_estimate=LIGHT,
    )(starts, half, other, normed1, pick)


def spread(starts, half, other):
    def kernel(s, a, b, o):
        for n, ref in enumerate((a, b)):
            for i in range(4):
                rows = pl.ds(pl.multiple_of(s[n * 4 + i], RB), RB)
                o[rows, :] = ref[i * RB : (i + 1) * RB, :D].astype(F32)

    return whole(kernel, [sds((LEN, D), F32)], [(starts, SM), half, other], 24)[0]


def local(
    tokens,
    cotangent,
    expert_ids,
    slot_order,
    image_starts,
    norm1_gain,
    w_query,
    w_latent,
    latent_gain,
    w_expand,
    w_output,
    norm2_gain,
    w_router,
    expert_gate,
    expert_up,
    expert_down,
    shared_gate,
    shared_up,
    shared_down,
):
    tr = lax.axis_index("tensor")
    dr = lax.axis_index("dp")
    zh, yy, cc = tr // 8, tr // 2 % 4, tr % 2
    peers = [((yy + y) % 4, (cc + c) % 2) for c in range(2) for y in range(4)]
    starts8 = jnp.stack([(c * 4 + y) * RB for y, c in peers]).astype(jnp.int32)
    starts4 = jnp.stack([y * RB for y, c in peers[:4]]).astype(jnp.int32)
    own_row = (cc * 4 + yy) * RB
    own_rows = lambda a: lax.dynamic_slice_in_dim(a, own_row, RB, 0)
    me = jnp.full((1,), tr, jnp.int32)

    half_at = lambda k: jnp.full((1,), k, jnp.int32)
    half_rows = lambda a, k: lax.dynamic_slice_in_dim(a, k * (LEN // 2), LEN // 2, 0)

    x, z = dr // 2, dr % 2

    lat_t = w_latent.T
    lat_z = recv_t(lat_t, zh=1)
    own_gu = cat(expert_gate[0].T, expert_up[0].T)
    own_dn = expert_down[0].T
    resid = tokens.astype(F32)
    inv1 = lax.rsqrt(jnp.mean(resid * resid, axis=-1, keepdims=True) + EPS)
    normed1 = (resid * inv1 * norm1_gain).astype(BF)
    lat_z, lat_t, own_gu, own_dn, normed1 = sync(lat_z, lat_t, own_gu, own_dn, normed1)

    lat = jnp.pad(cat(lat_t, lat_z), [(0, LP - 2 * LW), (0, 0)])
    lat_y = from_y(lat)
    ap_dn, zz_dn = recv_d(own_dn, x=1), recv_d(own_dn, z=1)
    chosen = jnp.any(expert_ids == tr, axis=1)
    order = slot_order[0]
    token = jnp.arange(LEN, dtype=jnp.int32)
    place = jnp.sum(jnp.where(order[:, None] == token[None, :], token[:, None], 0), axis=0)
    before = (place[:, None] < place[None, :]) & chosen[:, None]
    rank = jnp.sum(before.astype(jnp.int32), axis=0)
    rank = jnp.where(chosen, rank, -1)
    rank_row, rank_col = rank[None, :], rank[:, None]
    cos, sin = rotary_tables(LEN)
    cos2, sin2 = jnp.concatenate([cos, cos], axis=1), jnp.concatenate([-sin, sin], axis=1)
    w_query_t = w_query.T
    query = dot(normed1, w_query_t, NT)
    qn = query[:, :NOPE].astype(BF)
    qr = rotate(query[:, NOPE:], cos, sin).astype(BF)
    column = jnp.arange(LP, dtype=jnp.int32)
    owner = jnp.stack([(zh + column // LW) % 2 * 8 + y * 2 + c for y, c in peers])
    target = jnp.where(column < 2 * LW, owner * LW + column % LW, -1).reshape(-1)
    lat_place = (jnp.arange(LX, dtype=jnp.int32)[:, None] == target[None, :]).astype(BF)
    lat, *lat_y, ap_dn, zz_dn, qn, qr, rank_row, rank_col, cotangent, own_gu, own_dn, lat_place, cos2, sin2 = sync(
        lat, *lat_y, ap_dn, zz_dn, qn, qr, rank_row, rank_col, cotangent, own_gu, own_dn, lat_place, cos2, sin2
    )

    lat_half = cat(lat, *lat_y)
    lat_other = recv_t(lat_half, c=1)
    zz_gu, ap_gu, am_gu = recv_d(own_gu, z=1), recv_d(own_gu, x=1), recv_d(own_gu, x=-1)
    out_grad = lax.all_gather(cotangent, "tensor", axis=1, tiled=True)
    sh_gu = cat(shared_gate.T, shared_up.T)
    lat_half, lat_other, sh_gu = sync(lat_half, lat_other, sh_gu)

    w_lat, latent, inv_lat, compressed, kn, kr, v = keys(
        normed1, lat_place, lat_half, lat_other, latent_gain[None, :], w_expand, cos2, sin2
    )
    mixed = attend(image_starts, qn, qr, kn, kr, v)
    at_send = attention_part(half_at(1 - cc), mixed, w_output)
    at_send, zz_gu, ap_gu, am_gu, own_dn, own_gu = sync(at_send, zz_gu, ap_gu, am_gu, own_dn, own_gu)
    at_got = recv_t(at_send, c=1)
    at_keep = attention_part(half_at(cc), mixed, w_output)
    bp_gu, am_dn = recv_d(ap_gu, z=1), recv_d(own_dn, x=-1)
    at_got, at_keep, own_gu = sync(at_got, at_keep, own_gu)

    at_b = split_sum(at_keep, at_got, starts4)
    at_y = to_y(at_b)
    a2_gu = recv_d(own_gu, x=2)
    *at_y, bp_gu, am_dn, ap_dn, own_dn, am_gu = sync(*at_y, bp_gu, am_dn, ap_dn, own_dn, am_gu)
    at_sum = add(at_b[0], *at_y)
    at_other = recv_t(at_sum, zh=1)
    at_sum, at_other, ap_dn, am_gu, own_dn = sync(at_sum, at_other, ap_dn, am_gu, own_dn)
    hidden, rows2, inv2, probs = rows_mid((at_sum, at_other), own_rows(tokens), norm2_gain[None, :], w_router)
    n2_y = from_y(rows2)
    bp_dn, bm_gu = recv_d(ap_dn, z=1), recv_d(am_gu, z=1)
    rows2, *n2_y, bp_dn, a2_gu, own_dn, am_dn, zz_gu, zz_dn = sync(
        rows2, *n2_y, bp_dn, a2_gu, own_dn, am_dn, zz_gu, zz_dn
    )
    n2_half = cat(rows2, *n2_y)
    n2_other = recv_t(n2_half, c=1)
    a2_dn, bm_dn = recv_d(own_dn, x=2), recv_d(am_dn, z=1)
    b2_gu = recv_d(zz_gu, x=2)
    w_router_t = w_router.T
    n2_half, n2_other, out_grad, rank_row, w_router_t = sync(n2_half, n2_other, out_grad, rank_row, w_router_t)

    normed2, probs_col, slots, dy, dyg, sh_sum, s_out, s_dx = experts_front(
        starts8, me, n2_half, n2_other, w_router, w_router_t, rank_row, out_grad, sh_gu, shared_down
    )
    slots, dy, a2_dn, bm_gu, zz_dn, own_gu = sync(slots, dy, a2_dn, bm_gu, zz_dn, own_gu)
    b2_dn = recv_d(zz_dn, x=2)
    near, part_out, part_dx = experts(
        slots, dy, [(own_gu, own_dn), (ap_gu, ap_dn), (am_gu, am_dn), (zz_gu, zz_dn)]
    )
    sh_half, sh_send = halves(sh_sum, x // 2)
    part_out, part_dx, bm_dn, b2_gu, b2_dn, sh_half, sh_send = sync(
        part_out, part_dx, bm_dn, b2_gu, b2_dn, sh_half, sh_send
    )
    sh_got = recv_d(sh_send, x=2)
    far, slot_out, dx = experts(
        slots,
        dy,
        [(a2_gu, a2_dn), (bp_gu, bp_dn), (b2_gu, b2_dn), (bm_gu, bm_dn)],
        (dyg, part_out, part_dx, me),
    )
    g_own_gu, g_own_dn, g_ap_gu, g_ap_dn, g_am_gu, g_am_dn, g_z_gu, g_z_dn = near
    g_a2_gu, g_a2_dn, g_bp_gu, g_bp_dn, g_b2_gu, g_b2_dn, g_bm_gu, g_bm_dn = far
    dx, sh_half, sh_got, g_b2_gu, g_bp_gu, slot_out = sync(dx, sh_half, sh_got, g_b2_gu, g_bp_gu, slot_out)

    n2_send = combine_grad(half_at(1 - cc), rank_col, dx, s_dx)
    n2_send, g_b2_gu, g_bp_gu, slot_out = sync(n2_send, g_b2_gu, g_bp_gu, slot_out)
    n2_got = recv_t(n2_send, c=1)
    branch = combine_out(rank_col, probs_col, slot_out, s_out, mixed, w_output)
    n2_keep = combine_grad(half_at(cc), rank_col, dx, s_dx)
    r_b2_gu, r_bp_gu = recv_d(g_b2_gu, x=2), recv_d(g_bp_gu, z=1)
    n2_got, n2_keep, branch, sh_half, sh_got = sync(n2_got, n2_keep, branch, sh_half, sh_got)
    branch_sum = lax.psum_scatter(branch.reshape(-1, 128), "tensor", scatter_dimension=0, tiled=True)
    n2_b = split_sum(n2_keep, n2_got, starts4)
    n2_y = to_y(n2_b)
    sh_keep, sh_send = halves(add(sh_half, sh_got), x % 2)
    sh_got = swap_x(sh_send)
    *n2_y, r_b2_gu, r_bp_gu, g_b2_dn, g_bp_dn, g_a2_gu, sh_keep, sh_got = sync(
        *n2_y, r_b2_gu, r_bp_gu, g_b2_dn, g_bp_dn, g_a2_gu, sh_keep, sh_got
    )
    sh_sum = add(sh_keep, sh_got)
    n2_sum = add(n2_b[0], *n2_y)
    n2_other = recv_t(n2_sum, zh=1)
    r_b2_dn = recv_d(g_b2_dn, x=2)
    n2_sum, n2_other, g_bp_dn, g_a2_gu, r_b2_dn, sh_sum, g_bm_gu = sync(
        n2_sum, n2_other, g_bp_dn, g_a2_gu, r_b2_dn, sh_sum, g_bm_gu
    )

    hid_grad, payload, gain2 = rows_two(
        (n2_sum, n2_other), hidden, inv2, probs, own_rows(out_grad), norm2_gain[None, :], w_router_t
    )
    p_y = from_y(payload)
    r_bp_dn, r_a2_gu = recv_d(g_bp_dn, z=1), recv_d(g_a2_gu, x=2)
    sh_keep, sh_send = halves(sh_sum, z)
    sh_z = recv_d(sh_send, z=1)
    z_gu_sum, ap_gu_sum, z_dn_sum = add(g_z_gu, r_b2_gu), add(g_ap_gu, r_bp_gu), add(g_z_dn, r_b2_dn)
    payload, *p_y, r_bp_dn, g_bm_gu, r_a2_gu, g_a2_dn, sh_keep, sh_z, z_gu_sum, ap_gu_sum, z_dn_sum = sync(
        payload, *p_y, r_bp_dn, g_bm_gu, r_a2_gu, g_a2_dn, sh_keep, sh_z, z_gu_sum, ap_gu_sum, z_dn_sum
    )
    pay_half = cat(payload, *p_y)
    pay_other = recv_t(pay_half, c=1)
    sh_own = add(sh_keep, sh_z)
    sh_pair = recv_d(sh_own, z=1)
    r_a2_dn = recv_d(g_a2_dn, x=2)
    pay_half, pay_other, g_bm_gu, sh_own, sh_pair = sync(pay_half, pay_other, g_bm_gu, sh_own, sh_pair)
    r_bm_gu = recv_d(g_bm_gu, z=1)
    mixed_grad = mixed_back(starts8, pay_half, pay_other, w_output)
    sh_pair = jnp.concatenate([sh_own, sh_pair], axis=1)
    sh_next = swap_x(sh_pair)
    w_out_g, w_router_g = output_grads(starts8, pay_half, pay_other, mixed, normed2)

    query_grad, expanded_grad, rope_grad = attend_back(image_starts, qn, qr, kn, kr, v, mixed_grad, cos2, sin2)
    n1_send = normed1_part(half_at(1 - cc), query_grad, expanded_grad, rope_grad, w_query_t, w_expand)
    n1_send, r_a2_dn, r_bm_gu, sh_pair, sh_next, z_gu_sum = sync(n1_send, r_a2_dn, r_bm_gu, sh_pair, sh_next, z_gu_sum)
    n1_got = recv_t(n1_send, c=1)
    n1_keep = normed1_part(half_at(cc), query_grad, expanded_grad, rope_grad, w_query_t, w_expand)
    r_z_gu = recv_d(z_gu_sum, z=1)
    n1_got, n1_keep, query_grad, expanded_grad, ap_gu_sum, g_am_gu, sh_pair, sh_next = sync(
        n1_got, n1_keep, query_grad, expanded_grad, ap_gu_sum, g_am_gu, sh_pair, sh_next
    )
    n1_b = split_sum(n1_keep, n1_got, starts4)
    n1_y1, n1_y3 = recv_t(n1_b[1], y=-1), recv_t(n1_b[3], y=1)
    r_ap_gu = recv_d(ap_gu_sum, x=-1)

    w_query_g = dot(query_grad, normed1, TN).astype(BF)
    w_expand_g = dot(compressed, expanded_grad, TN).astype(BF)
    w_expand_g = jnp.concatenate([w_expand_g[64 * i : 64 * (i + 1)] for i in range(8)], axis=1)
    rest = cat(w_query_g, w_out_g, w_expand_g, w_router_g)
    rest_half, rest_send = halves(rest, x // 2)
    rest_got = recv_d(rest_send, x=2)
    n1_y1, n1_y3, n1_b2, rest_half, g_am_gu, g_ap_dn, sh_pair = sync(
        n1_y1, n1_y3, n1_b[2], rest_half, g_am_gu, g_ap_dn, sh_pair
    )
    n1_y2 = recv_t(n1_b2, y=2)
    am_gu_sum, ap_dn_sum = add(g_am_gu, r_bm_gu), add(g_ap_dn, r_bp_dn)
    r_am_gu = recv_d(am_gu_sum, x=1)
    sh_near = jnp.concatenate([sh_pair, sh_next], axis=1)
    n1_y1, n1_y3, n1_y2, rest_half, rest_got, r_z_gu, r_ap_gu, ap_dn_sum, sh_near = sync(
        n1_y1, n1_y3, n1_y2, rest_half, rest_got, r_z_gu, r_ap_gu, ap_dn_sum, sh_near
    )
    n1_sum = add(n1_b[0], n1_y1, n1_y2, n1_y3)
    n1_other = recv_t(n1_sum, zh=1)
    rest_keep, rest_send = halves(add(rest_half, rest_got), x % 2)
    rest_got = swap_x(rest_send)
    n1_sum, n1_other, rest_keep, rest_got, sh_near = sync(n1_sum, n1_other, rest_keep, rest_got, sh_near)
    sh_far = recv_d(sh_near, x=2)
    tok_rows = rows_one(
        (n1_sum, n1_other),
        w_lat,
        own_rows(tokens),
        own_rows(inv1),
        hid_grad,
        norm1_gain[None, :],
        own_rows(latent),
        own_rows(inv_lat),
        latent_gain[None, :],
        gain2,
    )
    t1, t3 = recv_t(tok_rows, y=1), recv_t(tok_rows, y=-1)
    rest_keep, rest_send = halves(add(rest_keep, rest_got), z)
    rest_got = recv_d(rest_send, z=1)
    tok_rows, t1, t3, rest_keep, rest_got, r_am_gu, g_bm_dn, ap_dn_sum = sync(
        tok_rows, t1, t3, rest_keep, rest_got, r_am_gu, g_bm_dn, ap_dn_sum
    )
    t2 = recv_t(tok_rows, y=2)
    rest_own = add(rest_keep, rest_got)
    rest_pair = recv_d(rest_own, z=1)
    r_bm_dn, r_ap_dn = recv_d(g_bm_dn, z=1), recv_d(ap_dn_sum, x=-1)
    tok_rows, t1, t2, t3, rest_own, rest_pair, sh_far, r_ap_dn = sync(
        tok_rows, t1, t2, t3, rest_own, rest_pair, sh_far, r_ap_dn
    )
    tok_half = cat(tok_rows, t1, t2, t3)
    tok_other = recv_t(tok_half, c=1)
    pair = jnp.concatenate([rest_own, rest_pair], axis=1)
    blocks = [pair] + [recv_d(pair, x=i) for i in (1, 2, 3)]
    tok_half, tok_other, r_bm_dn, g_am_dn, z_dn_sum = sync(tok_half, tok_other, r_bm_dn, g_am_dn, z_dn_sum)
    pick = (
        (jnp.arange(LX, dtype=jnp.int32)[None, :] == tr * LW + column[:LW48, None]) & (column[:LW48, None] < LW)
    ).astype(BF)
    offsets = jnp.stack([((x + i) % 4 * 2 + (z + j) % 2) * 256 for i in range(4) for j in range(2)])
    w_lat_g, gains = latent_w_grad(starts8, tok_half, tok_other, normed1, pick)
    gains = jnp.pad(gains[: GAINS // FREE, 128 - FREE :].reshape(-1), (0, 16 * D - GAINS)).reshape(16, D)
    small = cat(w_lat_g, gains.astype(BF))
    small, z_dn_sum, g_am_dn, r_bm_dn, tok_half = sync(small, z_dn_sum, g_am_dn, r_bm_dn, tok_half)
    small = sum_d(small, 0)
    tokens_grad = spread(starts8, tok_half, tok_other)
    small, tokens_grad, z_dn_sum, g_am_dn, *blocks = sync(small, tokens_grad, z_dn_sum, g_am_dn, *blocks)
    small = sum_d(small, 1)
    r_z_dn, r_am_dn = recv_d(z_dn_sum, z=1), recv_d(add(g_am_dn, r_bm_dn), x=1)
    wq_grad, wo_grad, we_grad, wr_grad = finish_rest(offsets, blocks)
    sh_offsets = jnp.stack([((x ^ i) * 2 + (z + j) % 2) * 256 for i in range(4) for j in range(2)])
    sg_grad, su_grad, sd_grad = finish_shared(sh_offsets, sh_near, sh_far)
    small, sg_grad, su_grad, sd_grad = sync(small, sg_grad, su_grad, sd_grad)
    small = sum_d(small, 2).astype(F32)
    eg_grad, eu_grad, ed_grad = finish_experts(
        (g_own_gu, r_a2_gu, r_ap_gu, r_am_gu, r_z_gu), (g_own_dn, r_a2_dn, r_ap_dn, r_am_dn, r_z_dn)
    )
    gains = small[LW48:].reshape(-1)

    own_cols = lax.dynamic_slice_in_dim(tokens, tr * 128, 128, 1)
    output = (own_cols.astype(F32) + branch_sum.astype(F32)).astype(BF)
    return (
        output,
        tokens_grad,
        gains[:D],
        wq_grad.T,
        small[:LW].T,
        gains[2 * D : GAINS],
        we_grad,
        wo_grad,
        gains[D : 2 * D],
        wr_grad.T,
        eg_grad.T[None],
        eu_grad.T[None],
        ed_grad.T[None],
        sg_grad.T,
        su_grad.T,
        sd_grad,
    )


def solution(mesh):
    in_specs = (
        P("dp", None),
        P("dp", "tensor"),
        P("dp", None),
        P("dp", None),
        P("dp", None),
        P(),
        P(None, "tensor"),
        P(None, "tensor"),
        P(),
        P(None, "tensor"),
        P("tensor", None),
        P(),
        P(),
        P("tensor", None, "dp"),
        P("tensor", None, "dp"),
        P("tensor", None, "dp"),
        P(None, "tensor"),
        P(None, "tensor"),
        P("tensor", None),
    )
    out_specs = (
        P("dp", "tensor"),
        P("dp", None),
        P(),
        P(None, "tensor"),
        P(None, "tensor"),
        P(),
        P(None, "tensor"),
        P("tensor", None),
        P(),
        P(),
        P("tensor", None, "dp"),
        P("tensor", None, "dp"),
        P("tensor", None, "dp"),
        P(None, "tensor"),
        P(None, "tensor"),
        P("tensor", None),
    )
    return jax.shard_map(local, mesh=mesh, in_specs=in_specs, out_specs=out_specs, check_vma=False)
```

time: 844 us -> 652 us (0.77)
  starting transfers between devices: 206 us -> 105 us
  local copies, waits for them, and re-layouts: 96.1 us -> 49.6 us
  waiting for transfers between devices: 315 us -> 285 us
  matrix products: 15.5 us -> 3.03 us
  other arithmetic: 50.7 us -> 41.2 us
    ppermute x75 -> x32, starting transfers between devices: 155 us -> 60.5 us  [recv_t(): return lax.ppermute(a, 'tensor', pairs)]
    ppermute x75 -> x32, waiting for transfers between devices: 155 us -> 107 us  [recv_t(): return lax.ppermute(a, 'tensor', pairs)]
    pallas_call x4 -> x10, Pallas kernels: 36.5 us -> 81.5 us  [the longest x2 48.9 us: experts(): pl.pallas_call(kernel, out_shape=[sds(a.shape, BF) for _, _, a in pieces]...]
    pallas_call x12 -> x13, Pallas kernels: 89.1 us -> 51.9 us  [whole(): pl.pallas_call(kernel, out_shape=outs, in_specs=specs, out_specs=[VM] * l...]
    unnamed x254 -> x222, local copies, waits for them, and re-layouts: 68.1 us -> 32.3 us
    ppermute x2 -> x4, waiting for transfers between devices: 0.01 us -> 26.1 us  [swap_x(): lax.ppermute(a, 'dp', [(i, (i // 2 ^ 1) * 2 + i % 2) for i in range(8)])]
    add x15 -> x5, other arithmetic: 14 us -> 0.11 us  [the longest x4 0.1 us: local(): (zh + column // LW) % 2 * 8 + y * 2 + c]
    dot_general x10 -> x3, matrix products: 15.5 us -> 3.03 us  [dot(): return lax.dot_general(a, b, dims, preferred_element_type=F32)]
  transfers between devices with their start and end apart: 118 -> 78, of which waited for: 45 -> 44; matrix products, arithmetic and copies ran while one was open for 15% -> 11% of each run, Pallas kernels for 12% -> 21%
where the time goes in v2:
time: 652 us; the launch traced here: 643 us
  waiting for transfers between devices  285 us (44%)
  Pallas kernels  143 us (22%)
  starting transfers between devices  105 us (16%)
  local copies, waits for them, and re-layouts  49.6 us (8%)
  other arithmetic  41.2 us (6%)
  between operations  16 us (2%)
    ppermute x40, waiting for transfers between devices, recv_d(): return lax.ppermute(a, 'dp', pairs)  152 us
    ppermute x32, waiting for transfers between devices, recv_t(): return lax.ppermute(a, 'tensor', pairs)  107 us
    ppermute x32, starting transfers between devices, recv_t(): return lax.ppermute(a, 'tensor', pairs)  60.5 us
    pallas_call x13, Pallas kernels, whole(): pl.pallas_call(kernel, out_shape=outs, in_specs=specs, out_specs=[VM] * l...  51.9 us
    pallas_call x2, Pallas kernels, experts(): pl.pallas_call(kernel, out_shape=[sds(a.shape, BF) for _, _, a in pieces]...  48.9 us
    ppermute x40, starting transfers between devices, recv_d(): return lax.ppermute(a, 'dp', pairs)  41.8 us
    unnamed x222, local copies, waits for them, and re-layouts  32.3 us
    ppermute x4, waiting for transfers between devices, swap_x(): lax.ppermute(a, 'dp', [(i, (i // 2 ^ 1) * 2 + i % 2) for i in range(8)])  26.1 us
  transfers between devices with their start and end apart: 78, of which 44 were waited for; matrix products, arithmetic and copies ran while one was open for 11% of the time, Pallas kernels for 21%

profile of v2, /device:TPU:1, one launch (start us, length us, event | category | flops | bytes accessed | tf_op | source)
XLA Modules:
  0.0 643.0 jit_solution(18102722968973565926)
XLA Ops:
  61.5 10.0 %shard_map.306 = (bf16[640,2048]{1,0:T(8,128)(2,1)S(1)}, bf16[1024,640]{1,0:T(8,128)(2,1)S(1)}, f32[1024,1]{1,0:T(8,128)S(1)}, bf16[1024,512]{1,0:T(8,128)(2,1)S...) custom-call(bf16[1024,2048]{1,0:T(8,128)(2,1)S(1)} %copy-done.1, ...), custom_call_target="tpu_custom_call" | custom-call | flops 1 | bytes 1 | tf_op jit(solution)/shard_map/pallas_call | solution.py:265
  71.6 6.2 shard_map.307.m
  90.4 16.3 %collective-permute-done.11 = bf16[128,2048]{1,0:T(8,128)(2,1)S(1)} collective-permute-done((bf16[128,2048]{1,0:T(8,128)(2,1)S(1)}, bf16[128,2048]{1,0:T(8,128)(2,1)S(1)}, u32[]{:S(2)}, u32[]{:S(2)}) %collective-permute-start.11) | collective-permute-done | bytes 524320 | tf_op jit(solution)/shard_map/ppermute | solution.py:76
  108.6 11.6 %collective-permute-done.14.refs_8_ = bf16[352,2048]{1,0:T(8,128)(2,1)} collective-permute-done((bf16[352,2048]{1,0:T(8,128)(2,1)}, bf16[352,2048]{1,0:T(8,128)(2,1)}, u32[]{:S(2)}, u32[]{:S(2)}) %collective-permute-start.14) | collective-permute-done | bytes 1441824 | tf_op jit(solution)/shard_map/ppermute | solution.py:83
  126.6 12.4 %collective-permute-done.16.b = bf16[128,2048]{1,0:T(8,128)(2,1)} collective-permute-done((bf16[128,2048]{1,0:T(8,128)(2,1)}, bf16[128,2048]{1,0:T(8,128)(2,1)}, u32[]{:S(2)}, u32[]{:S(2)}) %collective-permute-start.16) | collective-permute-done | bytes 524320 | tf_op jit(solution)/shard_map/ppermute | solution.py:76
  143.9 9.8 %collective-permute-done.18 = bf16[128,2048]{1,0:T(8,128)(2,1)S(1)} collective-permute-done((bf16[128,2048]{1,0:T(8,128)(2,1)S(1)}, bf16[128,2048]{1,0:T(8,128)(2,1)S(1)}, u32[]{:S(2)}, u32[]{:S(2)}) %collective-permute-start.18) | collective-permute-done | bytes 524320 | tf_op jit(solution)/shard_map/ppermute | solution.py:76
  159.0 7.0 %collective-permute-done.19 = bf16[128,2048]{1,0:T(8,128)(2,1)S(1)} collective-permute-done((bf16[128,2048]{1,0:T(8,128)(2,1)S(1)}, bf16[128,2048]{1,0:T(8,128)(2,1)S(1)}, u32[]{:S(2)}, u32[]{:S(2)}) %collective-permute-start.19) | collective-permute-done | bytes 524320 | tf_op jit(solution)/shard_map/ppermute | solution.py:76
  178.6 21.6 %shard_map.312 = (bf16[1024,2048]{1,0:T(8,128)(2,1)}, f32[1024,1]{1,0:T(8,128)}, bf16[480,2048]{1,0:T(8,128)(2,1)}, bf16[480,2048]{1,0:T(8,128)(2,1)}, bf16[480,...) custom-call(s32[8]{0:T(128)} %stack.116.s, ...), custom_call_target="tpu_custom_call" | custom-call | flops 1 | bytes 1 | tf_op jit(solution)/shard_map/pallas_call | solution.py:54
  200.2 6.4 collective-permute-done.24.refs_12_
  209.0 23.5 %shard_map.313 = (bf16[352,2048]{1,0:T(8,128)(2,1)}, bf16[176,2048]{1,0:T(8,128)(2,1)S(1)}, bf16[352,2048]{1,0:T(8,128)(2,1)}, bf16[176,2048]{1,0:T(8,128)(2,1)S...) custom-call(bf16[480,2048]{1,0:T(8,128)(2,1)} %get-tuple-element.374, ...), custom_call_target="tpu_custom_call" | custom-call | flops 1 | bytes 1 | tf_op jit(solution)/shard_map/pallas_call | solution.py:435
  241.9 25.4 %shard_map.314 = (bf16[352,2048]{1,0:T(8,128)(2,1)}, bf16[176,2048]{1,0:T(8,128)(2,1)S(1)}, bf16[352,2048]{1,0:T(8,128)(2,1)}, bf16[176,2048]{1,0:T(8,128)(2,1)S...) custom-call(s32[1]{0:T(128)} %bitcast.11.me.refs_0_, ...), custom_call_target="tpu_custom_call" | custom-call | flops 1 | bytes 1 | tf_op jit(solution)/shard_map/pallas_call | solution.py:435
  276.7 4.7 shard_map.317
  289.3 10.3 %collective-permute-done.30 = bf16[128,2176]{1,0:T(8,128)(2,1)} collective-permute-done((bf16[128,2176]{1,0:T(8,128)(2,1)}, bf16[128,2176]{1,0:T(8,128)(2,1)}, u32[]{:S(2)}, u32[]{:S(2)}) %collective-permute-start.30) | collective-permute-done | bytes 557088 | tf_op jit(solution)/shard_map/ppermute | solution.py:76
  307.7 9.3 %collective-permute-done.35 = bf16[528,512]{1,0:T(8,128)(2,1)S(1)} collective-permute-done((bf16[528,512]{1,0:T(8,128)(2,1)S(1)}, bf16[528,512]{1,0:T(8,128)(2,1)S(1)}, u32[]{:S(2)}, u32[]{:S(2)}) %collective-permute-start.35) | collective-permute-done | bytes 540704 | tf_op jit(solution)/shard_map/ppermute | solution.py:118
  327.8 9.4 %collective-permute-done.36.b = bf16[128,2176]{1,0:T(8,128)(2,1)} collective-permute-done((bf16[128,2176]{1,0:T(8,128)(2,1)S(1)}, bf16[128,2176]{1,0:T(8,128)(2,1)}, u32[]{:S(2)}, u32[]{:S(2)}) %collective-permute-start.36) | collective-permute-done | bytes 557088 | tf_op jit(solution)/shard_map/ppermute | solution.py:76
  349.8 6.9 %collective-permute-done.39 = bf16[128,2176]{1,0:T(8,128)(2,1)S(1)} collective-permute-done((bf16[128,2176]{1,0:T(8,128)(2,1)S(1)}, bf16[128,2176]{1,0:T(8,128)(2,1)S(1)}, u32[]{:S(2)}, u32[]{:S(2)}) %collective-permute-start.39) | collective-permute-done | bytes 557088 | tf_op jit(solution)/shard_map/ppermute | solution.py:76
  362.7 4.9 collective-permute-done.43
  376.1 6.7 %collective-permute-done.45 = bf16[528,256]{1,0:T(8,128)(2,1)S(1)} collective-permute-done((bf16[528,256]{1,0:T(8,128)(2,1)S(1)}, bf16[528,256]{1,0:T(8,128)(2,1)S(1)}, u32[]{:S(2)}, u32[]{:S(2)}) %collective-permute-start.45) | collective-permute-done | bytes 270368 | tf_op jit(solution)/shard_map/ppermute | solution.py:83
  387.3 10.0 %shard_map.321 = (bf16[1024,192]{1,0:T(8,128)(2,1)S(1)}, bf16[1024,256]{1,0:T(8,128)(2,1)S(1)}, bf16[1024,64]{1,0:T(8,128)(2,1)S(1)}) custom-call(s32[1,2]{1,0:T(1,128)S(1)} %copy-done.68, bf16[1024,128]{1,0:T(8,128)(2,1)S(1)} %copy-done.18, bf16[1024,64]{1,0:T(8,128)(2,1)S(1)} %pad_maximum_fusion.6.qr, bf16[1024,128]{1,0:T(8,128)(2,1)S(1)} %copy-done.36, ...), custom_call_target="tpu_custom_call" | custom-call | flops 1 | bytes 1 | tf_op jit(solution)/shard_map/pallas_call | solution.py:228
  402.3 9.6 %collective-permute-done.48 = bf16[528,512]{1,0:T(8,128)(2,1)S(1)} collective-permute-done((bf16[528,512]{1,0:T(8,128)(2,1)S(1)}, bf16[528,512]{1,0:T(8,128)(2,1)S(1)}, u32[]{:S(2)}, u32[]{:S(2)}) %collective-permute-start.48) | collective-permute-done | bytes 540704 | tf_op jit(solution)/shard_map/ppermute | solution.py:118
  429.9 11.7 %collective-permute-done.50 = bf16[128,2688]{1,0:T(8,128)(2,1)S(1)} collective-permute-done((bf16[128,2688]{1,0:T(8,128)(2,1)S(1)}, bf16[128,2688]{1,0:T(8,128)(2,1)S(1)}, u32[]{:S(2)}, u32[]{:S(2)}) %collective-permute-start.50) | collective-permute-done | bytes 688160 | tf_op jit(solution)/shard_map/ppermute | solution.py:76
  447.6 6.1 collective-permute-done.54.refs_4_
  453.7 24.1 %collective-permute-done.53 = bf16[400,1024]{1,0:T(8,128)(2,1)S(1)} collective-permute-done((bf16[400,1024]{1,0:T(8,128)(2,1)S(1)}, bf16[400,1024]{1,0:T(8,128)(2,1)S(1)}, u32[]{:S(2)}, u32[]{:S(2)}) %collective-permute-start.53) | collective-permute-done | bytes 819232 | tf_op jit(solution)/shard_map/ppermute | solution.py:83
  486.0 7.2 %collective-permute-done.57 = bf16[400,512]{1,0:T(8,128)(2,1)} collective-permute-done((bf16[400,512]{1,0:T(8,128)(2,1)}, bf16[400,512]{1,0:T(8,128)(2,1)}, u32[]{:S(2)}, u32[]{:S(2)}) %collective-permute-start.57) | collective-permute-done | bytes 409632 | tf_op jit(solution)/shard_map/ppermute | solution.py:118
  512.4 5.8 collective-permute-done.59
  519.4 4.9 collective-permute-done.63
  524.3 4.9 collective-permute-done.64.b
  533.4 14.8 %collective-permute-done.65.refs_7_ = bf16[176,2048]{1,0:T(8,128)(2,1)S(1)} collective-permute-done((bf16[176,2048]{1,0:T(8,128)(2,1)S(1)}, bf16[176,2048]{1,0:T(8,128)(2,1)S(1)}, u32[]{:S(2)}, u32[]{:S(2)}) %collective-permute-start.65) | collective-permute-done | bytes 720928 | tf_op jit(solution)/shard_map/ppermute | solution.py:83
  552.2 17.8 %collective-permute-done.67 = bf16[176,2048]{1,0:T(8,128)(2,1)} collective-permute-done((bf16[176,2048]{1,0:T(8,128)(2,1)}, bf16[176,2048]{1,0:T(8,128)(2,1)}, u32[]{:S(2)}, u32[]{:S(2)}) %collective-permute-start.67) | collective-permute-done | bytes 720928 | tf_op jit(solution)/shard_map/ppermute | solution.py:83
  580.9 5.8 shard_map.328
  591.1 5.6 collective-permute-done.70.refs_2_
  617.5 14.0 %collective-permute-done.74.refs_8_ = bf16[176,2048]{1,0:T(8,128)(2,1)S(1)} collective-permute-done((bf16[176,2048]{1,0:T(8,128)(2,1)S(1)}, bf16[176,2048]{1,0:T(8,128)(2,1)S(1)}, u32[]{:S(2)}, u32[]{:S(2)}) %collective-permute-start.74) | collective-permute-done | bytes 720928 | tf_op jit(solution)/shard_map/ppermute | solution.py:83
  (461 shorter events, 282.1 us)
Async XLA Ops:
  7.2 171.4 %all-gather.2.cloned.1.call-start = ((), (), s32[]{:S(2)}) async-start(), calls=%async_computation.1 | async-start | bytes 4456448 | tf_op jit(solution)/shard_map/all_gather | solution.py:763
  44.4 35.5 %collective-permute-start.9 = (bf16[352,2048]{1,0:T(8,128)(2,1)}, bf16[352,2048]{1,0:T(8,128)(2,1)}, u32[]{:S(2)}, u32[]{:S(2)}) collective-permute-start(bf16[352,2048]{1,0:T(8,128)(2,1)} %pad_maximum_fusion.1.refs_2_), channel_id=1, source_target_pairs={{96,0},{112,16},{0,32},{16,48},{32,64},{48,80},{64,96},{80,112},{9... | collective-permute-start | bytes 4325384 | tf_op jit(solution)/shard_map/ppermute | solution.py:83
  45.7 34.2 %collective-permute-start.8 = (bf16[352,2048]{1,0:T(8,128)(2,1)}, bf16[352,2048]{1,0:T(8,128)(2,1)}, u32[]{:S(2)}, u32[]{:S(2)}) collective-permute-start(bf16[352,2048]{1,0:T(8,128)(2,1)} %pad_maximum_fusion.1.refs_2_), channel_id=1, source_target_pairs={{32,0},{48,16},{64,32},{80,48},{96,64},{112,80},{0,96},{16,112},{3... | collective-permute-start | bytes 4325384 | tf_op jit(solution)/shard_map/ppermute | solution.py:83
  47.1 32.7 %collective-permute-start.7 = (bf16[352,2048]{1,0:T(8,128)(2,1)}, bf16[352,2048]{1,0:T(8,128)(2,1)}, u32[]{:S(2)}, u32[]{:S(2)}) collective-permute-start(bf16[352,2048]{1,0:T(8,128)(2,1)} %pad_maximum_fusion.1.refs_2_), channel_id=1, source_target_pairs={{16,0},{0,16},{48,32},{32,48},{80,64},{64,80},{112,96},{96,112},{1... | collective-permute-start | bytes 4325384 | tf_op jit(solution)/shard_map/ppermute | solution.py:83
  81.5 519.6 %reduce-scatter.2.cloned.1.call-start = ((), (), s32[]{:S(2)}) async-start(), calls=%async_computation.2 | async-start | bytes 4456448 | tf_op jit(solution)/shard_map/reduce_scatter | solution.py:828
  81.5 38.6 %collective-permute-start.14 = (bf16[352,2048]{1,0:T(8,128)(2,1)}, bf16[352,2048]{1,0:T(8,128)(2,1)}, u32[]{:S(2)}, u32[]{:S(2)}) collective-permute-start(bf16[352,2048]{1,0:T(8,128)(2,1)} %collective-permute-done.8.refs_4_), channel_id=1, source_target_pairs={{16,0},{0,16},{48,32},{32,48},{80,64},{64,80},{112,96},{96,112},{1... | collective-permute-start | bytes 4325384 | tf_op jit(solution)/shard_map/ppermute | solution.py:83
  87.7 19.1 %collective-permute-start.11 = (bf16[128,2048]{1,0:T(8,128)(2,1)S(1)}, bf16[128,2048]{1,0:T(8,128)(2,1)S(1)}, u32[]{:S(2)}, u32[]{:S(2)}) collective-permute-start(bf16[128,2048]{1,0:T(8,128)(2,1)S(1)} %get-tuple-element.330), channel_id=1, source_target_pairs={{6,0},{7,1},{0,2},{1,3},{2,4},{3,5},{4,6},{5,7},{14,8},{15,9},{8,1... | collective-permute-start | bytes 1572872 | tf_op jit(solution)/shard_map/ppermute | solution.py:76
  125.0 33.0 %collective-permute-start.21 = (bf16[352,2048]{1,0:T(8,128)(2,1)}, bf16[352,2048]{1,0:T(8,128)(2,1)}, u32[]{:S(2)}, u32[]{:S(2)}) collective-permute-start(bf16[352,2048]{1,0:T(8,128)(2,1)} %pad_maximum_fusion.1.refs_2_), channel_id=1, source_target_pairs={{64,0},{80,16},{96,32},{112,48},{0,64},{16,80},{32,96},{48,112},{6... | collective-permute-start | bytes 4325384 | tf_op jit(solution)/shard_map/ppermute | solution.py:83
  173.1 33.5 %collective-permute-start.24 = (bf16[352,2048]{1,0:T(8,128)(2,1)}, bf16[352,2048]{1,0:T(8,128)(2,1)}, u32[]{:S(2)}, u32[]{:S(2)}) collective-permute-start(bf16[352,2048]{1,0:T(8,128)(2,1)} %collective-permute-done.9.refs_6_), channel_id=1, source_target_pairs={{16,0},{0,16},{48,32},{32,48},{80,64},{64,80},{112,96},{96,112},{1... | collective-permute-start | bytes 4325384 | tf_op jit(solution)/shard_map/ppermute | solution.py:83
  173.1 33.5 %collective-permute-start.23 = (bf16[176,2048]{1,0:T(8,128)(2,1)}, bf16[176,2048]{1,0:T(8,128)(2,1)S(1)}, u32[]{:S(2)}, u32[]{:S(2)}) collective-permute-start(bf16[176,2048]{1,0:T(8,128)(2,1)} %bitcast.7.refs_3_), channel_id=1, source_target_pairs={{64,0},{80,16},{96,32},{112,48},{0,64},{16,80},{32,96},{48,112},{6... | collective-permute-start | bytes 2162696 | tf_op jit(solution)/shard_map/ppermute | solution.py:83
  175.8 58.5 %collective-permute-start.26 = (bf16[352,2048]{1,0:T(8,128)(2,1)}, bf16[352,2048]{1,0:T(8,128)(2,1)}, u32[]{:S(2)}, u32[]{:S(2)}) collective-permute-start(bf16[352,2048]{1,0:T(8,128)(2,1)} %collective-permute-done.7.refs_8_), channel_id=1, source_target_pairs={{64,0},{80,16},{96,32},{112,48},{0,64},{16,80},{32,96},{48,112},{6... | collective-permute-start | bytes 4325384 | tf_op jit(solution)/shard_map/ppermute | solution.py:83
  176.7 57.6 %collective-permute-start.25 = (bf16[176,2048]{1,0:T(8,128)(2,1)}, bf16[176,2048]{1,0:T(8,128)(2,1)}, u32[]{:S(2)}, u32[]{:S(2)}) collective-permute-start(bf16[176,2048]{1,0:T(8,128)(2,1)} %copy-done.87), channel_id=1, source_target_pairs={{16,0},{0,16},{48,32},{32,48},{80,64},{64,80},{112,96},{96,112},{1... | collective-permute-start | bytes 2162696 | tf_op jit(solution)/shard_map/ppermute | solution.py:83
  206.6 32.3 %collective-permute-start.27 = (bf16[176,2048]{1,0:T(8,128)(2,1)}, bf16[176,2048]{1,0:T(8,128)(2,1)}, u32[]{:S(2)}, u32[]{:S(2)}) collective-permute-start(bf16[176,2048]{1,0:T(8,128)(2,1)} %collective-permute-done.5.refs_9_), channel_id=1, source_target_pairs={{64,0},{80,16},{96,32},{112,48},{0,64},{16,80},{32,96},{48,112},{6... | collective-permute-start | bytes 2162696 | tf_op jit(solution)/shard_map/ppermute | solution.py:83
  238.9 28.5 %collective-permute-start.28 = (bf16[528,1024]{1,0:T(8,128)(2,1)}, bf16[528,1024]{1,0:T(8,128)(2,1)}, u32[]{:S(2)}, u32[]{:S(2)}) collective-permute-start(bf16[528,1024]{1,0:T(8,128)(2,1)} %get-tuple-element.396), channel_id=1, source_target_pairs={{64,0},{80,16},{96,32},{112,48},{0,64},{16,80},{32,96},{48,112},{6... | collective-permute-start | bytes 3244040 | tf_op jit(solution)/shard_map/ppermute | solution.py:83
  272.7 35.0 %collective-permute-start.33 = (bf16[352,2048]{1,0:T(8,128)(2,1)}, bf16[352,2048]{1,0:T(8,128)(2,1)}, u32[]{:S(2)}, u32[]{:S(2)}) collective-permute-start(bf16[352,2048]{1,0:T(8,128)(2,1)} %get-tuple-element.421), channel_id=1, source_target_pairs={{64,0},{80,16},{96,32},{112,48},{0,64},{16,80},{32,96},{48,112},{6... | collective-permute-start | bytes 4325384 | tf_op jit(solution)/shard_map/ppermute | solution.py:83
  273.2 34.5 %collective-permute-start.34 = (bf16[352,2048]{1,0:T(8,128)(2,1)}, bf16[352,2048]{1,0:T(8,128)(2,1)}, u32[]{:S(2)}, u32[]{:S(2)}) collective-permute-start(bf16[352,2048]{1,0:T(8,128)(2,1)} %get-tuple-element.422), channel_id=1, source_target_pairs={{16,0},{0,16},{48,32},{32,48},{80,64},{64,80},{112,96},{96,112},{1... | collective-permute-start | bytes 4325384 | tf_op jit(solution)/shard_map/ppermute | solution.py:83
  317.0 20.2 %collective-permute-start.37 = (bf16[176,2048]{1,0:T(8,128)(2,1)}, bf16[176,2048]{1,0:T(8,128)(2,1)}, u32[]{:S(2)}, u32[]{:S(2)}) collective-permute-start(bf16[176,2048]{1,0:T(8,128)(2,1)} %get-tuple-element.433), channel_id=1, source_target_pairs={{64,0},{80,16},{96,32},{112,48},{0,64},{16,80},{32,96},{48,112},{6... | collective-permute-start | bytes 2162696 | tf_op jit(solution)/shard_map/ppermute | solution.py:83
  337.2 33.0 %collective-permute-start.42 = (bf16[352,2048]{1,0:T(8,128)(2,1)}, bf16[352,2048]{1,0:T(8,128)(2,1)S(1)}, u32[]{:S(2)}, u32[]{:S(2)}) collective-permute-start(bf16[352,2048]{1,0:T(8,128)(2,1)} %get-tuple-element.448), channel_id=1, source_target_pairs={{64,0},{80,16},{96,32},{112,48},{0,64},{16,80},{32,96},{48,112},{6... | collective-permute-start | bytes 4325384 | tf_op jit(solution)/shard_map/ppermute | solution.py:83
  345.9 21.7 %collective-permute-start.41 = (bf16[176,2048]{1,0:T(8,128)(2,1)S(1)}, bf16[176,2048]{1,0:T(8,128)(2,1)S(1)}, u32[]{:S(2)}, u32[]{:S(2)}) collective-permute-start(bf16[176,2048]{1,0:T(8,128)(2,1)S(1)} %copy-done.74), channel_id=1, source_target_pairs={{16,0},{0,16},{48,32},{32,48},{80,64},{64,80},{112,96},{96,112},{1... | collective-permute-start | bytes 2162696 | tf_op jit(solution)/shard_map/ppermute | solution.py:83
  382.9 32.4 %collective-permute-start.47 = (bf16[352,2048]{1,0:T(8,128)(2,1)S(1)}, bf16[352,2048]{1,0:T(8,128)(2,1)S(1)}, u32[]{:S(2)}, u32[]{:S(2)}) collective-permute-start(bf16[352,2048]{1,0:T(8,128)(2,1)S(1)} %copy-done.97), channel_id=1, source_target_pairs={{16,0},{0,16},{48,32},{32,48},{80,64},{64,80},{112,96},{96,112},{1... | collective-permute-start | bytes 4325384 | tf_op jit(solution)/shard_map/ppermute | solution.py:83
  385.2 26.8 %collective-permute-start.48 = (bf16[528,512]{1,0:T(8,128)(2,1)S(1)}, bf16[528,512]{1,0:T(8,128)(2,1)S(1)}, u32[]{:S(2)}, u32[]{:S(2)}) collective-permute-start(bf16[528,512]{1,0:T(8,128)(2,1)S(1)} %constant_dynamic-update-slice_fusion.12), channel_id=1, source_target_pairs={{0,32},{16,48},{32,0},{48,16},{64,96},{80,112},{96,64},{112,80},{1... | collective-permute-start | bytes 1622024 | tf_op jit(solution)/shard_map/ppermute | solution.py:118
  420.3 33.4 %collective-permute-start.54 = (bf16[352,2048]{1,0:T(8,128)(2,1)S(1)}, bf16[352,2048]{1,0:T(8,128)(2,1)S(1)}, u32[]{:S(2)}, u32[]{:S(2)}) collective-permute-start(bf16[352,2048]{1,0:T(8,128)(2,1)S(1)} %add_convert_fusion.2), channel_id=1, source_target_pairs={{16,0},{0,16},{48,32},{32,48},{80,64},{64,80},{112,96},{96,112},{1... | collective-permute-start | bytes 4325384 | tf_op jit(solution)/shard_map/ppermute | solution.py:83
  427.3 50.5 %collective-permute-start.55 = (bf16[352,2048]{1,0:T(8,128)(2,1)S(1)}, bf16[352,2048]{1,0:T(8,128)(2,1)S(1)}, u32[]{:S(2)}, u32[]{:S(2)}) collective-permute-start(bf16[352,2048]{1,0:T(8,128)(2,1)S(1)} %add_convert_fusion.1), channel_id=1, source_target_pairs={{96,0},{112,16},{0,32},{16,48},{32,64},{48,80},{64,96},{80,112},{9... | collective-permute-start | bytes 4325384 | tf_op jit(solution)/shard_map/ppermute | solution.py:83
  428.3 49.5 %collective-permute-start.53 = (bf16[400,1024]{1,0:T(8,128)(2,1)S(1)}, bf16[400,1024]{1,0:T(8,128)(2,1)S(1)}, u32[]{:S(2)}, u32[]{:S(2)}) collective-permute-start(bf16[400,1024]{1,0:T(8,128)(2,1)S(1)} %get-tuple-element.584), channel_id=1, source_target_pairs={{64,0},{80,16},{96,32},{112,48},{0,64},{16,80},{32,96},{48,112},{6... | collective-permute-start | bytes 2457608 | tf_op jit(solution)/shard_map/ppermute | solution.py:83
  441.6 36.2 %collective-permute-start.52 = (bf16[128,2688]{1,0:T(8,128)(2,1)S(1)}, bf16[128,2688]{1,0:T(8,128)(2,1)S(1)}, u32[]{:S(2)}, u32[]{:S(2)}) collective-permute-start(bf16[128,2688]{1,0:T(8,128)(2,1)S(1)} %get-tuple-element.496), channel_id=1, source_target_pairs={{4,0},{5,1},{6,2},{7,3},{0,4},{1,5},{2,6},{3,7},{12,8},{13,9},{14,... | collective-permute-start | bytes 2064392 | tf_op jit(solution)/shard_map/ppermute | solution.py:76
  445.2 62.5 %collective-permute-start.61 = (bf16[352,2048]{1,0:T(8,128)(2,1)}, bf16[352,2048]{1,0:T(8,128)(2,1)}, u32[]{:S(2)}, u32[]{:S(2)}) collective-permute-start(bf16[352,2048]{1,0:T(8,128)(2,1)} %add_convert_fusion), channel_id=1, source_target_pairs={{32,0},{48,16},{64,32},{80,48},{96,64},{112,80},{0,96},{16,112},{3... | collective-permute-start | bytes 4325384 | tf_op jit(solution)/shard_map/ppermute | solution.py:83
  505.2 23.9 %collective-permute-start.64 = (bf16[528,1024]{1,0:T(8,128)(2,1)S(1)}, bf16[528,1024]{1,0:T(8,128)(2,1)S(1)}, u32[]{:S(2)}, u32[]{:S(2)}) collective-permute-start(bf16[528,1024]{1,0:T(8,128)(2,1)S(1)} %pad_maximum_fusion.3.a), channel_id=1, source_target_pairs={{64,0},{80,16},{96,32},{112,48},{0,64},{16,80},{32,96},{48,112},{6... | collective-permute-start | bytes 3244040 | tf_op jit(solution)/shard_map/ppermute | solution.py:83
  518.3 29.9 %collective-permute-start.65 = (bf16[176,2048]{1,0:T(8,128)(2,1)S(1)}, bf16[176,2048]{1,0:T(8,128)(2,1)S(1)}, u32[]{:S(2)}, u32[]{:S(2)}) collective-permute-start(bf16[176,2048]{1,0:T(8,128)(2,1)S(1)} %copy-done.85), channel_id=1, source_target_pairs={{96,0},{112,16},{0,32},{16,48},{32,64},{48,80},{64,96},{80,112},{9... | collective-permute-start | bytes 2162696 | tf_op jit(solution)/shard_map/ppermute | solution.py:83
  578.0 18.7 %collective-permute-start.70 = (bf16[400,512]{1,0:T(8,128)(2,1)S(1)}, bf16[400,512]{1,0:T(8,128)(2,1)S(1)}, u32[]{:S(2)}, u32[]{:S(2)}) collective-permute-start(bf16[400,512]{1,0:T(8,128)(2,1)S(1)} %constant_dynamic-update-slice_fusion.26.refs_0_), channel_id=1, source_target_pairs={{64,0},{80,16},{96,32},{112,48},{0,64},{16,80},{32,96},{48,112},{6... | collective-permute-start | bytes 1228808 | tf_op jit(solution)/shard_map/ppermute | solution.py:83
  579.4 19.3 %collective-permute-start.69 = (bf16[400,512]{1,0:T(8,128)(2,1)S(1)}, bf16[400,512]{1,0:T(8,128)(2,1)S(1)}, u32[]{:S(2)}, u32[]{:S(2)}) collective-permute-start(bf16[400,512]{1,0:T(8,128)(2,1)S(1)} %constant_dynamic-update-slice_fusion.26.refs_0_), channel_id=1, source_target_pairs={{32,0},{48,16},{64,32},{80,48},{96,64},{112,80},{0,96},{16,112},{3... | collective-permute-start | bytes 1228808 | tf_op jit(solution)/shard_map/ppermute | solution.py:83
  612.1 19.4 %collective-permute-start.74 = (bf16[176,2048]{1,0:T(8,128)(2,1)S(1)}, bf16[176,2048]{1,0:T(8,128)(2,1)S(1)}, u32[]{:S(2)}, u32[]{:S(2)}) collective-permute-start(bf16[176,2048]{1,0:T(8,128)(2,1)S(1)} %add_convert_fusion.5), channel_id=1, source_target_pairs={{32,0},{48,16},{64,32},{80,48},{96,64},{112,80},{0,96},{16,112},{3... | collective-permute-start | bytes 2162696 | tf_op jit(solution)/shard_map/ppermute | solution.py:83
  612.2 19.4 %collective-permute-start.75 = (bf16[176,2048]{1,0:T(8,128)(2,1)}, bf16[176,2048]{1,0:T(8,128)(2,1)S(1)}, u32[]{:S(2)}, u32[]{:S(2)}) collective-permute-start(bf16[176,2048]{1,0:T(8,128)(2,1)} %add_convert_fusion.7), channel_id=1, source_target_pairs={{16,0},{0,16},{48,32},{32,48},{80,64},{64,80},{112,96},{96,112},{1... | collective-permute-start | bytes 2162696 | tf_op jit(solution)/shard_map/ppermute | solution.py:83
  (144 other events, 1582.7 us)
Sparse Core Ops, SparseCore 0:
  81.6 59.7 all-gather.1
  505.3 81.1 reduce-scatter.1

commit v3 on v2

--- a/solution.py
+++ b/solution.py
@@ -81,6 +81,17 @@
     for i in range(8):
         pairs.append((((i // 2 + x) % 4) * 2 + (i % 2 + z) % 2, i))
     return lax.ppermute(a, "dp", pairs)
+
+
+def stack(*arrays):
+    n = arrays[0].shape[0]
+
+    def kernel(*refs):
+        for i, r in enumerate(refs[:-1]):
+            refs[-1][n * i : n * (i + 1)] = r[...]
+
+    shape = (n * len(arrays), arrays[0].shape[1])
+    return whole(kernel, [sds(shape, BF)], list(arrays), 12)[0]
 
 
 def from_y(a):
@@ -629,12 +640,12 @@
 
 def finish_shared(offsets, near, far):
     def kernel(off, a, b, gate, up, down):
-        refs = [r.at[:, 512 * i : 512 * (i + 1)] for r in (a, b) for i in range(2)]
-        for at, block in column_blocks(off, refs):
-            cols = pl.ds(at, 256)
-            gate[:, cols] = block(0, FS)
-            up[:, cols] = block(FS, 2 * FS)
-            down[:, cols] = block(2 * FS, 3 * FS)
+        for i in range(8):
+            ref, cols = (a, b)[i // 4], slice(256 * (i % 4), 256 * (i % 4 + 1))
+            at = pl.ds(pl.multiple_of(off[i], 256), 256)
+            gate[:, at] = ref[:FS, cols].astype(F32)
+            up[:, at] = ref[FS : 2 * FS, cols].astype(F32)
+            down[:, at] = ref[2 * FS :, cols].astype(F32)
 
     return whole(kernel, [sds((FS, D), F32)] * 3, [(offsets, SM), near, far], 16)
 
@@ -723,6 +734,7 @@
 
     x, z = dr // 2, dr % 2
 
+    out_grad = lax.all_gather(cotangent, "tensor", axis=1, tiled=True)
     lat_t = w_latent.T
     lat_z = recv_t(lat_t, zh=1)
     own_gu = cat(expert_gate[0].T, expert_up[0].T)
@@ -753,14 +765,13 @@
     owner = jnp.stack([(zh + column // LW) % 2 * 8 + y * 2 + c for y, c in peers])
     target = jnp.where(column < 2 * LW, owner * LW + column % LW, -1).reshape(-1)
     lat_place = (jnp.arange(LX, dtype=jnp.int32)[:, None] == target[None, :]).astype(BF)
-    lat, *lat_y, ap_dn, zz_dn, qn, qr, rank_row, rank_col, cotangent, own_gu, own_dn, lat_place, cos2, sin2 = sync(
-        lat, *lat_y, ap_dn, zz_dn, qn, qr, rank_row, rank_col, cotangent, own_gu, own_dn, lat_place, cos2, sin2
-    )
-
-    lat_half = cat(lat, *lat_y)
+    lat, *lat_y, ap_dn, zz_dn, qn, qr, rank_row, rank_col, own_gu, own_dn, lat_place, cos2, sin2 = sync(
+        lat, *lat_y, ap_dn, zz_dn, qn, qr, rank_row, rank_col, own_gu, own_dn, lat_place, cos2, sin2
+    )
+
+    lat_half = stack(lat, *lat_y)
     lat_other = recv_t(lat_half, c=1)
     zz_gu, ap_gu, am_gu = recv_d(own_gu, z=1), recv_d(own_gu, x=1), recv_d(own_gu, x=-1)
-    out_grad = lax.all_gather(cotangent, "tensor", axis=1, tiled=True)
     sh_gu = cat(shared_gate.T, shared_up.T)
     lat_half, lat_other, sh_gu = sync(lat_half, lat_other, sh_gu)
 
@@ -776,38 +787,42 @@
     at_got, at_keep, own_gu = sync(at_got, at_keep, own_gu)
 
     at_b = split_sum(at_keep, at_got, starts4)
-    at_y = to_y(at_b)
+    at_y1, at_y3 = recv_t(at_b[1], y=-1), recv_t(at_b[3], y=1)
+    at_y1, at_y3, at_b2, am_dn, own_gu = sync(at_y1, at_y3, at_b[2], am_dn, own_gu)
+    at_y = [at_y1, recv_t(at_b2, y=2), at_y3]
     a2_gu = recv_d(own_gu, x=2)
-    *at_y, bp_gu, am_dn, ap_dn, own_dn, am_gu = sync(*at_y, bp_gu, am_dn, ap_dn, own_dn, am_gu)
+    *at_y, bp_gu, ap_dn, own_dn, am_gu = sync(*at_y, bp_gu, ap_dn, own_dn, am_gu)
     at_sum = add(at_b[0], *at_y)
     at_other = recv_t(at_sum, zh=1)
     at_sum, at_other, ap_dn, am_gu, own_dn = sync(at_sum, at_other, ap_dn, am_gu, own_dn)
     hidden, rows2, inv2, probs = rows_mid((at_sum, at_other), own_rows(tokens), norm2_gain[None, :], w_router)
-    n2_y = from_y(rows2)
-    bp_dn, bm_gu = recv_d(ap_dn, z=1), recv_d(am_gu, z=1)
-    rows2, *n2_y, bp_dn, a2_gu, own_dn, am_dn, zz_gu, zz_dn = sync(
-        rows2, *n2_y, bp_dn, a2_gu, own_dn, am_dn, zz_gu, zz_dn
-    )
-    n2_half = cat(rows2, *n2_y)
+    n2_y1, n2_y3 = recv_t(rows2, y=1), recv_t(rows2, y=-1)
+    bp_dn = recv_d(ap_dn, z=1)
+    rows2, n2_y1, n2_y3, a2_gu, own_dn = sync(rows2, n2_y1, n2_y3, a2_gu, own_dn)
+    n2_y2 = recv_t(rows2, y=2)
+    a2_dn = recv_d(own_dn, x=2)
+    rows2, n2_y1, n2_y2, n2_y3, bp_dn, am_gu, am_dn, zz_gu, zz_dn, a2_dn = sync(
+        rows2, n2_y1, n2_y2, n2_y3, bp_dn, am_gu, am_dn, zz_gu, zz_dn, a2_dn
+    )
+    n2_y = [n2_y1, n2_y2, n2_y3]
+    n2_half = stack(rows2, *n2_y)
     n2_other = recv_t(n2_half, c=1)
-    a2_dn, bm_dn = recv_d(own_dn, x=2), recv_d(am_dn, z=1)
-    b2_gu = recv_d(zz_gu, x=2)
+    bm_gu, bm_dn = recv_d(am_gu, z=1), recv_d(am_dn, z=1)
+    b2_gu, b2_dn = recv_d(zz_gu, x=2), recv_d(zz_dn, x=2)
     w_router_t = w_router.T
     n2_half, n2_other, out_grad, rank_row, w_router_t = sync(n2_half, n2_other, out_grad, rank_row, w_router_t)
 
     normed2, probs_col, slots, dy, dyg, sh_sum, s_out, s_dx = experts_front(
         starts8, me, n2_half, n2_other, w_router, w_router_t, rank_row, out_grad, sh_gu, shared_down
     )
-    slots, dy, a2_dn, bm_gu, zz_dn, own_gu = sync(slots, dy, a2_dn, bm_gu, zz_dn, own_gu)
-    b2_dn = recv_d(zz_dn, x=2)
     near, part_out, part_dx = experts(
         slots, dy, [(own_gu, own_dn), (ap_gu, ap_dn), (am_gu, am_dn), (zz_gu, zz_dn)]
     )
-    sh_half, sh_send = halves(sh_sum, x // 2)
-    part_out, part_dx, bm_dn, b2_gu, b2_dn, sh_half, sh_send = sync(
-        part_out, part_dx, bm_dn, b2_gu, b2_dn, sh_half, sh_send
-    )
-    sh_got = recv_d(sh_send, x=2)
+    sh_half, sh_send = halves(sh_sum, z)
+    part_out, part_dx, bm_gu, bm_dn, b2_gu, b2_dn, sh_half, sh_send = sync(
+        part_out, part_dx, bm_gu, bm_dn, b2_gu, b2_dn, sh_half, sh_send
+    )
+    sh_got = recv_d(sh_send, z=1)
     far, slot_out, dx = experts(
         slots,
         dy,
@@ -821,84 +836,82 @@
     n2_send = combine_grad(half_at(1 - cc), rank_col, dx, s_dx)
     n2_send, g_b2_gu, g_bp_gu, slot_out = sync(n2_send, g_b2_gu, g_bp_gu, slot_out)
     n2_got = recv_t(n2_send, c=1)
-    branch = combine_out(rank_col, probs_col, slot_out, s_out, mixed, w_output)
     n2_keep = combine_grad(half_at(cc), rank_col, dx, s_dx)
     r_b2_gu, r_bp_gu = recv_d(g_b2_gu, x=2), recv_d(g_bp_gu, z=1)
-    n2_got, n2_keep, branch, sh_half, sh_got = sync(n2_got, n2_keep, branch, sh_half, sh_got)
+    n2_got, n2_keep, slot_out, sh_half, sh_got = sync(n2_got, n2_keep, slot_out, sh_half, sh_got)
+    n2_b = split_sum(n2_keep, n2_got, starts4)
+    n2_y1, n2_y3 = recv_t(n2_b[1], y=-1), recv_t(n2_b[3], y=1)
+    sh_keep, sh_send = halves(add(sh_half, sh_got), x // 2)
+    branch = combine_out(rank_col, probs_col, slot_out, s_out, mixed, w_output)
+    n2_y1, n2_y3, n2_b2, sh_keep, sh_send, g_b2_dn, branch = sync(
+        n2_y1, n2_y3, n2_b[2], sh_keep, sh_send, g_b2_dn, branch
+    )
     branch_sum = lax.psum_scatter(branch.reshape(-1, 128), "tensor", scatter_dimension=0, tiled=True)
-    n2_b = split_sum(n2_keep, n2_got, starts4)
-    n2_y = to_y(n2_b)
-    sh_keep, sh_send = halves(add(sh_half, sh_got), x % 2)
-    sh_got = swap_x(sh_send)
-    *n2_y, r_b2_gu, r_bp_gu, g_b2_dn, g_bp_dn, g_a2_gu, sh_keep, sh_got = sync(
-        *n2_y, r_b2_gu, r_bp_gu, g_b2_dn, g_bp_dn, g_a2_gu, sh_keep, sh_got
-    )
-    sh_sum = add(sh_keep, sh_got)
+    n2_y = [n2_y1, recv_t(n2_b2, y=2), n2_y3]
+    r_b2_dn = recv_d(g_b2_dn, x=2)
+    *n2_y, r_b2_gu, r_bp_gu, g_bp_dn, g_a2_gu = sync(*n2_y, r_b2_gu, r_bp_gu, g_bp_dn, g_a2_gu)
     n2_sum = add(n2_b[0], *n2_y)
     n2_other = recv_t(n2_sum, zh=1)
-    r_b2_dn = recv_d(g_b2_dn, x=2)
-    n2_sum, n2_other, g_bp_dn, g_a2_gu, r_b2_dn, sh_sum, g_bm_gu = sync(
-        n2_sum, n2_other, g_bp_dn, g_a2_gu, r_b2_dn, sh_sum, g_bm_gu
+    r_a2_gu = recv_d(g_a2_gu, x=2)
+    r_bm_gu = recv_d(g_bm_gu, z=1)
+    n2_sum, n2_other, r_b2_dn, g_bp_dn, sh_keep, sh_send, r_b2_gu, r_bp_gu, g_z_gu, g_ap_gu, g_z_dn = sync(
+        n2_sum, n2_other, r_b2_dn, g_bp_dn, sh_keep, sh_send, r_b2_gu, r_bp_gu, g_z_gu, g_ap_gu, g_z_dn
     )
 
     hid_grad, payload, gain2 = rows_two(
         (n2_sum, n2_other), hidden, inv2, probs, own_rows(out_grad), norm2_gain[None, :], w_router_t
     )
     p_y = from_y(payload)
-    r_bp_dn, r_a2_gu = recv_d(g_bp_dn, z=1), recv_d(g_a2_gu, x=2)
-    sh_keep, sh_send = halves(sh_sum, z)
-    sh_z = recv_d(sh_send, z=1)
     z_gu_sum, ap_gu_sum, z_dn_sum = add(g_z_gu, r_b2_gu), add(g_ap_gu, r_bp_gu), add(g_z_dn, r_b2_dn)
-    payload, *p_y, r_bp_dn, g_bm_gu, r_a2_gu, g_a2_dn, sh_keep, sh_z, z_gu_sum, ap_gu_sum, z_dn_sum = sync(
-        payload, *p_y, r_bp_dn, g_bm_gu, r_a2_gu, g_a2_dn, sh_keep, sh_z, z_gu_sum, ap_gu_sum, z_dn_sum
-    )
-    pay_half = cat(payload, *p_y)
+    payload, *p_y, r_bm_gu, r_a2_gu, g_a2_dn, g_bp_dn, sh_keep, sh_send, z_gu_sum, ap_gu_sum, z_dn_sum = sync(
+        payload, *p_y, r_bm_gu, r_a2_gu, g_a2_dn, g_bp_dn, sh_keep, sh_send, z_gu_sum, ap_gu_sum, z_dn_sum
+    )
+    r_a2_dn, r_bp_dn, sh_got = recv_d(g_a2_dn, x=2), recv_d(g_bp_dn, z=1), recv_d(sh_send, x=2)
+    pay_half = stack(payload, *p_y)
     pay_other = recv_t(pay_half, c=1)
-    sh_own = add(sh_keep, sh_z)
-    sh_pair = recv_d(sh_own, z=1)
-    r_a2_dn = recv_d(g_a2_dn, x=2)
-    pay_half, pay_other, g_bm_gu, sh_own, sh_pair = sync(pay_half, pay_other, g_bm_gu, sh_own, sh_pair)
-    r_bm_gu = recv_d(g_bm_gu, z=1)
+    pay_half, pay_other = sync(pay_half, pay_other)
     mixed_grad = mixed_back(starts8, pay_half, pay_other, w_output)
-    sh_pair = jnp.concatenate([sh_own, sh_pair], axis=1)
-    sh_next = swap_x(sh_pair)
-    w_out_g, w_router_g = output_grads(starts8, pay_half, pay_other, mixed, normed2)
 
     query_grad, expanded_grad, rope_grad = attend_back(image_starts, qn, qr, kn, kr, v, mixed_grad, cos2, sin2)
     n1_send = normed1_part(half_at(1 - cc), query_grad, expanded_grad, rope_grad, w_query_t, w_expand)
-    n1_send, r_a2_dn, r_bm_gu, sh_pair, sh_next, z_gu_sum = sync(n1_send, r_a2_dn, r_bm_gu, sh_pair, sh_next, z_gu_sum)
+    n1_send, r_a2_dn, r_bp_dn, z_gu_sum = sync(n1_send, r_a2_dn, r_bp_dn, z_gu_sum)
     n1_got = recv_t(n1_send, c=1)
+    r_z_gu = recv_d(z_gu_sum, z=1)
     n1_keep = normed1_part(half_at(cc), query_grad, expanded_grad, rope_grad, w_query_t, w_expand)
-    r_z_gu = recv_d(z_gu_sum, z=1)
-    n1_got, n1_keep, query_grad, expanded_grad, ap_gu_sum, g_am_gu, sh_pair, sh_next = sync(
-        n1_got, n1_keep, query_grad, expanded_grad, ap_gu_sum, g_am_gu, sh_pair, sh_next
+    n1_got, n1_keep, query_grad, expanded_grad, g_am_gu, mixed, pay_half = sync(
+        n1_got, n1_keep, query_grad, expanded_grad, g_am_gu, mixed, pay_half
     )
     n1_b = split_sum(n1_keep, n1_got, starts4)
     n1_y1, n1_y3 = recv_t(n1_b[1], y=-1), recv_t(n1_b[3], y=1)
-    r_ap_gu = recv_d(ap_gu_sum, x=-1)
 
     w_query_g = dot(query_grad, normed1, TN).astype(BF)
     w_expand_g = dot(compressed, expanded_grad, TN).astype(BF)
     w_expand_g = jnp.concatenate([w_expand_g[64 * i : 64 * (i + 1)] for i in range(8)], axis=1)
+    w_out_g, w_router_g = output_grads(starts8, pay_half, pay_other, mixed, normed2)
     rest = cat(w_query_g, w_out_g, w_expand_g, w_router_g)
     rest_half, rest_send = halves(rest, x // 2)
     rest_got = recv_d(rest_send, x=2)
-    n1_y1, n1_y3, n1_b2, rest_half, g_am_gu, g_ap_dn, sh_pair = sync(
-        n1_y1, n1_y3, n1_b[2], rest_half, g_am_gu, g_ap_dn, sh_pair
+    n1_y1, n1_y3, n1_b2, rest_half, g_am_gu, g_ap_dn, sh_keep, sh_got, g_bm_dn = sync(
+        n1_y1, n1_y3, n1_b[2], rest_half, g_am_gu, g_ap_dn, sh_keep, sh_got, g_bm_dn
     )
     n1_y2 = recv_t(n1_b2, y=2)
+    r_bm_dn = recv_d(g_bm_dn, z=1)
     am_gu_sum, ap_dn_sum = add(g_am_gu, r_bm_gu), add(g_ap_dn, r_bp_dn)
-    r_am_gu = recv_d(am_gu_sum, x=1)
-    sh_near = jnp.concatenate([sh_pair, sh_next], axis=1)
-    n1_y1, n1_y3, n1_y2, rest_half, rest_got, r_z_gu, r_ap_gu, ap_dn_sum, sh_near = sync(
-        n1_y1, n1_y3, n1_y2, rest_half, rest_got, r_z_gu, r_ap_gu, ap_dn_sum, sh_near
+    sh_keep, sh_send = halves(add(sh_keep, sh_got), x % 2)
+    sh_got = swap_x(sh_send)
+    n1_y1, n1_y3, n1_y2, rest_half, rest_got, r_bm_dn, r_z_gu, am_gu_sum, ap_dn_sum, sh_keep, sh_got = sync(
+        n1_y1, n1_y3, n1_y2, rest_half, rest_got, r_bm_dn, r_z_gu, am_gu_sum, ap_dn_sum, sh_keep, sh_got
     )
     n1_sum = add(n1_b[0], n1_y1, n1_y2, n1_y3)
     n1_other = recv_t(n1_sum, zh=1)
     rest_keep, rest_send = halves(add(rest_half, rest_got), x % 2)
     rest_got = swap_x(rest_send)
-    n1_sum, n1_other, rest_keep, rest_got, sh_near = sync(n1_sum, n1_other, rest_keep, rest_got, sh_near)
-    sh_far = recv_d(sh_near, x=2)
+    sh_own = add(sh_keep, sh_got)
+    sh_next = swap_x(sh_own)
+    am_dn_sum = add(g_am_dn, r_bm_dn)
+    n1_sum, n1_other, rest_keep, rest_got, sh_own, sh_next, am_gu_sum, ap_gu_sum, ap_dn_sum, am_dn_sum, z_dn_sum = sync(
+        n1_sum, n1_other, rest_keep, rest_got, sh_own, sh_next, am_gu_sum, ap_gu_sum, ap_dn_sum, am_dn_sum, z_dn_sum
+    )
     tok_rows = rows_one(
         (n1_sum, n1_other),
         w_lat,
@@ -912,23 +925,28 @@
         gain2,
     )
     t1, t3 = recv_t(tok_rows, y=1), recv_t(tok_rows, y=-1)
+    r_ap_gu, r_am_gu = recv_d(ap_gu_sum, x=-1), recv_d(am_gu_sum, x=1)
     rest_keep, rest_send = halves(add(rest_keep, rest_got), z)
     rest_got = recv_d(rest_send, z=1)
-    tok_rows, t1, t3, rest_keep, rest_got, r_am_gu, g_bm_dn, ap_dn_sum = sync(
-        tok_rows, t1, t3, rest_keep, rest_got, r_am_gu, g_bm_dn, ap_dn_sum
+    sh_pair = jnp.concatenate([sh_own, sh_next], axis=1)
+    tok_rows, t1, t3, rest_keep, rest_got, sh_pair, z_dn_sum = sync(
+        tok_rows, t1, t3, rest_keep, rest_got, sh_pair, z_dn_sum
     )
     t2 = recv_t(tok_rows, y=2)
     rest_own = add(rest_keep, rest_got)
     rest_pair = recv_d(rest_own, z=1)
-    r_bm_dn, r_ap_dn = recv_d(g_bm_dn, z=1), recv_d(ap_dn_sum, x=-1)
-    tok_rows, t1, t2, t3, rest_own, rest_pair, sh_far, r_ap_dn = sync(
-        tok_rows, t1, t2, t3, rest_own, rest_pair, sh_far, r_ap_dn
-    )
-    tok_half = cat(tok_rows, t1, t2, t3)
+    tok_rows, t1, t2, t3, rest_own, rest_pair, sh_pair, ap_dn_sum, am_dn_sum, z_dn_sum, r_ap_gu, r_am_gu = sync(
+        tok_rows, t1, t2, t3, rest_own, rest_pair, sh_pair, ap_dn_sum, am_dn_sum, z_dn_sum, r_ap_gu, r_am_gu
+    )
+    sh_far = recv_d(sh_pair, x=2)
+    tok_half = stack(tok_rows, t1, t2, t3)
     tok_other = recv_t(tok_half, c=1)
+    r_z_dn = recv_d(z_dn_sum, z=1)
     pair = jnp.concatenate([rest_own, rest_pair], axis=1)
+    tok_half, tok_other, pair, sh_pair, sh_far = sync(tok_half, tok_other, pair, sh_pair, sh_far)
     blocks = [pair] + [recv_d(pair, x=i) for i in (1, 2, 3)]
-    tok_half, tok_other, r_bm_dn, g_am_dn, z_dn_sum = sync(tok_half, tok_other, r_bm_dn, g_am_dn, z_dn_sum)
+    sh_half = jnp.concatenate([sh_pair, sh_far], axis=1)
+    sh_across = recv_d(sh_half, z=1)
     pick = (
         (jnp.arange(LX, dtype=jnp.int32)[None, :] == tr * LW + column[:LW48, None]) & (column[:LW48, None] < LW)
     ).astype(BF)
@@ -936,24 +954,28 @@
     w_lat_g, gains = latent_w_grad(starts8, tok_half, tok_other, normed1, pick)
     gains = jnp.pad(gains[: GAINS // FREE, 128 - FREE :].reshape(-1), (0, 16 * D - GAINS)).reshape(16, D)
     small = cat(w_lat_g, gains.astype(BF))
-    small, z_dn_sum, g_am_dn, r_bm_dn, tok_half = sync(small, z_dn_sum, g_am_dn, r_bm_dn, tok_half)
+    own_cols = lax.dynamic_slice_in_dim(tokens, tr * 128, 128, 1).astype(F32)
+    small = sum_d(small, 1)
+    tokens_grad = spread(starts8, tok_half, tok_other)
+    small, tokens_grad, r_z_dn, ap_dn_sum, am_dn_sum, *blocks = sync(
+        small, tokens_grad, r_z_dn, ap_dn_sum, am_dn_sum, *blocks
+    )
+    small = sum_d(small, 2)
+    r_ap_dn, r_am_dn = recv_d(ap_dn_sum, x=-1), recv_d(am_dn_sum, x=1)
+    wq_grad, wo_grad, we_grad, wr_grad = finish_rest(offsets, blocks)
+    output = (own_cols + branch_sum.astype(F32)).astype(BF)
+    small, wq_grad, wo_grad, we_grad, wr_grad, output, sh_across = sync(
+        small, wq_grad, wo_grad, we_grad, wr_grad, output, sh_across
+    )
     small = sum_d(small, 0)
-    tokens_grad = spread(starts8, tok_half, tok_other)
-    small, tokens_grad, z_dn_sum, g_am_dn, *blocks = sync(small, tokens_grad, z_dn_sum, g_am_dn, *blocks)
-    small = sum_d(small, 1)
-    r_z_dn, r_am_dn = recv_d(z_dn_sum, z=1), recv_d(add(g_am_dn, r_bm_dn), x=1)
-    wq_grad, wo_grad, we_grad, wr_grad = finish_rest(offsets, blocks)
-    sh_offsets = jnp.stack([((x ^ i) * 2 + (z + j) % 2) * 256 for i in range(4) for j in range(2)])
-    sg_grad, su_grad, sd_grad = finish_shared(sh_offsets, sh_near, sh_far)
-    small, sg_grad, su_grad, sd_grad = sync(small, sg_grad, su_grad, sd_grad)
-    small = sum_d(small, 2).astype(F32)
+    sh_offsets = jnp.stack([((z + j) % 2 * 4 + (x ^ i)) * 256 for j in range(2) for i in range(4)])
+    sg_grad, su_grad, sd_grad = finish_shared(sh_offsets, sh_half, sh_across)
     eg_grad, eu_grad, ed_grad = finish_experts(
         (g_own_gu, r_a2_gu, r_ap_gu, r_am_gu, r_z_gu), (g_own_dn, r_a2_dn, r_ap_dn, r_am_dn, r_z_dn)
     )
+    small = small.astype(F32)
     gains = small[LW48:].reshape(-1)
 
-    own_cols = lax.dynamic_slice_in_dim(tokens, tr * 128, 128, 1)
-    output = (own_cols.astype(F32) + branch_sum.astype(F32)).astype(BF)
     return (
         output,
         tokens_grad,

time: 652 us -> 610 us (0.936)
  waiting for transfers between devices: 285 us -> 220 us
  local copies, waits for them, and re-layouts: 49.6 us -> 62.9 us
  starting transfers between devices: 105 us -> 113 us
    ppermute x32, waiting for transfers between devices: 107 us -> 80.5 us  [recv_t(): return lax.ppermute(a, 'tensor', pairs)]
    ppermute x40, waiting for transfers between devices: 152 us -> 128 us  [recv_d(): return lax.ppermute(a, 'dp', pairs)]
    unnamed x222 -> x294, local copies, waits for them, and re-layouts: 32.3 us -> 47.4 us
    ppermute x4, waiting for transfers between devices: 26.1 us -> 11.7 us  [swap_x(): lax.ppermute(a, 'dp', [(i, (i // 2 ^ 1) * 2 + i % 2) for i in range(8)])]
    pallas_call x13 -> x17, Pallas kernels: 51.9 us -> 53.5 us  [whole(): pl.pallas_call(kernel, out_shape=outs, in_specs=specs, out_specs=[VM] * l...]
  transfers between devices with their start and end apart: 78 -> 78, of which waited for: 44 -> 37; matrix products, arithmetic and copies ran while one was open for 11% -> 10% of each run, Pallas kernels for 21% -> 24%
where the time goes in v3:
time: 610 us; the launch traced here: 601 us
  waiting for transfers between devices  220 us (36%)
  Pallas kernels  145 us (24%)
  starting transfers between devices  113 us (19%)
  local copies, waits for them, and re-layouts  62.9 us (10%)
  other arithmetic  41.4 us (7%)
  between operations  16 us (3%)
    ppermute x40, waiting for transfers between devices, recv_d(): return lax.ppermute(a, 'dp', pairs)  128 us
    ppermute x32, waiting for transfers between devices, recv_t(): return lax.ppermute(a, 'tensor', pairs)  80.5 us
    ppermute x32, starting transfers between devices, recv_t(): return lax.ppermute(a, 'tensor', pairs)  65.3 us
    pallas_call x17, Pallas kernels, whole(): pl.pallas_call(kernel, out_shape=outs, in_specs=specs, out_specs=[VM] * l...  53.5 us
    pallas_call x2, Pallas kernels, experts(): pl.pallas_call(kernel, out_shape=[sds(a.shape, BF) for _, _, a in pieces]...  48.9 us
    unnamed x294, local copies, waits for them, and re-layouts  47.4 us
    ppermute x40, starting transfers between devices, recv_d(): return lax.ppermute(a, 'dp', pairs)  44.3 us
    convert_element_type x15, other arithmetic, add(): return sum((t.astype(F32) for t in terms)).astype(BF)  15.6 us
  transfers between devices with their start and end apart: 78, of which 37 were waited for; matrix products, arithmetic and copies ran while one was open for 10% of the time, Pallas kernels for 24%

profile of v3, /device:TPU:1, one launch (start us, length us, event | category | flops | bytes accessed | tf_op | source)
XLA Modules:
  0.0 600.6 jit_solution(13579246227882957009)
XLA Ops:
  56.7 9.6 %shard_map.307 = (bf16[640,2048]{1,0:T(8,128)(2,1)S(1)}, bf16[1024,640]{1,0:T(8,128)(2,1)S(1)}, f32[1024,1]{1,0:T(8,128)S(1)}, bf16[1024,512]{1,0:T(8,128)(2,1)S...) custom-call(bf16[1024,2048]{1,0:T(8,128)(2,1)S(1)} %copy-done.1, ...), custom_call_target="tpu_custom_call" | custom-call | flops 1 | bytes 1 | tf_op jit(solution)/shard_map/pallas_call | solution.py:276
  67.5 6.2 %shard_map.308.m = bf16[1024,128]{1,0:T(8,128)(2,1)S(1)} custom-call(s32[1,2]{1,0:T(1,128)S(1)} %copy-done.93, bf16[1024,128]{1,0:T(8,128)(2,1)S(1)} %copy-done.25, bf16[1024,64]{1,0:T(8,128)(2,1)S(1)} %copy-done.23, bf16[1024,128]{1,0:T(8,128)(2,1)S(1)} %get-tuple-element.326.kn, bf16[1024,64]{1,0:T(8,128)(2,1)S(1)} %get-tuple-element.327.kr, ...), custom_call_target="tpu_custom_call" | custom-call | flops 1 | bytes 1 | tf_op jit(solution)/shard_map/pallas_call | solution.py:193
  79.9 6.8 %collective-permute-start.10 = (bf16[512,2048]{1,0:T(8,128)(2,1)S(1)}, bf16[512,2048]{1,0:T(8,128)(2,1)}, u32[]{:S(2)}, u32[]{:S(2)}) collective-permute-start(bf16[512,2048]{1,0:T(8,128)(2,1)S(1)} %shard_map.309), channel_id=1, source_target_pairs={{1,0},{0,1},{3,2},{2,3},{5,4},{4,5},{7,6},{6,7},{9,8},{8,9},{11,10... | collective-permute-start | bytes 6291464 | tf_op jit(solution)/shard_map/ppermute | solution.py:76
  95.5 12.4 %collective-permute-done.13.refs_7_ = bf16[176,2048]{1,0:T(8,128)(2,1)} collective-permute-done((bf16[176,2048]{1,0:T(8,128)(2,1)}, bf16[176,2048]{1,0:T(8,128)(2,1)}, u32[]{:S(2)}, u32[]{:S(2)}) %collective-permute-start.13) | collective-permute-done | bytes 720928 | tf_op jit(solution)/shard_map/ppermute | solution.py:83
  108.9 16.5 %collective-permute-done.15.refs_8_ = bf16[352,2048]{1,0:T(8,128)(2,1)} collective-permute-done((bf16[352,2048]{1,0:T(8,128)(2,1)}, bf16[352,2048]{1,0:T(8,128)(2,1)}, u32[]{:S(2)}, u32[]{:S(2)}) %collective-permute-start.15) | collective-permute-done | bytes 1441824 | tf_op jit(solution)/shard_map/ppermute | solution.py:83
  128.3 12.1 %collective-permute-done.16.b = bf16[128,2048]{1,0:T(8,128)(2,1)S(1)} collective-permute-done((bf16[128,2048]{1,0:T(8,128)(2,1)S(1)}, bf16[128,2048]{1,0:T(8,128)(2,1)S(1)}, u32[]{:S(2)}, u32[]{:S(2)}) %collective-permute-start.16) | collective-permute-done | bytes 524320 | tf_op jit(solution)/shard_map/ppermute | solution.py:76
  146.8 10.7 %collective-permute-done.18.refs_3_ = bf16[128,2048]{1,0:T(8,128)(2,1)S(1)} collective-permute-done((bf16[128,2048]{1,0:T(8,128)(2,1)S(1)}, bf16[128,2048]{1,0:T(8,128)(2,1)S(1)}, u32[]{:S(2)}, u32[]{:S(2)}) %collective-permute-start.18) | collective-permute-done | bytes 524320 | tf_op jit(solution)/shard_map/ppermute | solution.py:76
  162.8 8.4 %collective-permute-done.20.refs_2_ = bf16[128,2048]{1,0:T(8,128)(2,1)S(1)} collective-permute-done((bf16[128,2048]{1,0:T(8,128)(2,1)S(1)}, bf16[128,2048]{1,0:T(8,128)(2,1)S(1)}, u32[]{:S(2)}, u32[]{:S(2)}) %collective-permute-start.20) | collective-permute-done | bytes 524320 | tf_op jit(solution)/shard_map/ppermute | solution.py:76
  184.1 21.5 %shard_map.314 = (bf16[1024,2048]{1,0:T(8,128)(2,1)}, f32[1024,1]{1,0:T(8,128)}, bf16[480,2048]{1,0:T(8,128)(2,1)}, bf16[480,2048]{1,0:T(8,128)(2,1)}, bf16[480,...) custom-call(s32[8]{0:T(128)} %stack.115.s, ...), custom_call_target="tpu_custom_call" | custom-call | flops 1 | bytes 1 | tf_op jit(solution)/shard_map/pallas_call | solution.py:54
  205.6 23.4 %shard_map.315 = (bf16[352,2048]{1,0:T(8,128)(2,1)}, bf16[176,2048]{1,0:T(8,128)(2,1)S(1)}, bf16[352,2048]{1,0:T(8,128)(2,1)}, bf16[176,2048]{1,0:T(8,128)(2,1)S...) custom-call(bf16[480,2048]{1,0:T(8,128)(2,1)} %get-tuple-element.379, ...), custom_call_target="tpu_custom_call" | custom-call | flops 1 | bytes 1 | tf_op jit(solution)/shard_map/pallas_call | solution.py:446
  231.5 25.4 %shard_map.316 = (bf16[352,2048]{1,0:T(8,128)(2,1)}, bf16[176,2048]{1,0:T(8,128)(2,1)S(1)}, bf16[352,2048]{1,0:T(8,128)(2,1)}, bf16[176,2048]{1,0:T(8,128)(2,1)S...) custom-call(s32[1]{0:T(128)} %bitcast.26.me.refs_0_, ...), custom_call_target="tpu_custom_call" | custom-call | flops 1 | bytes 1 | tf_op jit(solution)/shard_map/pallas_call | solution.py:446
  277.9 4.7 shard_map.320
  290.3 8.3 %collective-permute-done.33 = bf16[352,2048]{1,0:T(8,128)(2,1)} collective-permute-done((bf16[352,2048]{1,0:T(8,128)(2,1)}, bf16[352,2048]{1,0:T(8,128)(2,1)}, u32[]{:S(2)}, u32[]{:S(2)}) %collective-permute-start.33) | collective-permute-done | bytes 1441824 | tf_op jit(solution)/shard_map/ppermute | solution.py:83
  307.4 6.5 %collective-permute-done.36 = bf16[176,2048]{1,0:T(8,128)(2,1)S(1)} collective-permute-done((bf16[176,2048]{1,0:T(8,128)(2,1)S(1)}, bf16[176,2048]{1,0:T(8,128)(2,1)S(1)}, u32[]{:S(2)}, u32[]{:S(2)}) %collective-permute-start.36) | collective-permute-done | bytes 720928 | tf_op jit(solution)/shard_map/ppermute | solution.py:83
  332.6 12.5 %collective-permute-done.40 = bf16[352,2048]{1,0:T(8,128)(2,1)S(1)} collective-permute-done((bf16[352,2048]{1,0:T(8,128)(2,1)S(1)}, bf16[352,2048]{1,0:T(8,128)(2,1)S(1)}, u32[]{:S(2)}, u32[]{:S(2)}) %collective-permute-start.40) | collective-permute-done | bytes 1441824 | tf_op jit(solution)/shard_map/ppermute | solution.py:83
  346.9 5.1 collective-permute-start.42
  359.2 9.9 %shard_map.324 = (bf16[1024,192]{1,0:T(8,128)(2,1)S(1)}, bf16[1024,256]{1,0:T(8,128)(2,1)S(1)}, bf16[1024,64]{1,0:T(8,128)(2,1)S(1)}) custom-call(s32[1,2]{1,0:T(1,128)S(1)} %copy-done.94, bf16[1024,128]{1,0:T(8,128)(2,1)S(1)} %copy-done.26, bf16[1024,64]{1,0:T(8,128)(2,1)S(1)} %copy-done.24, bf16[1024,128]{1,0:T(8,128)(2,1)S(1)} %copy-done.45, ...), custom_call_target="tpu_custom_call" | custom-call | flops 1 | bytes 1 | tf_op jit(solution)/shard_map/pallas_call | solution.py:239
  395.1 9.5 %collective-permute-done.46 = bf16[128,2688]{1,0:T(8,128)(2,1)S(1)} collective-permute-done((bf16[128,2688]{1,0:T(8,128)(2,1)S(1)}, bf16[128,2688]{1,0:T(8,128)(2,1)S(1)}, u32[]{:S(2)}, u32[]{:S(2)}) %collective-permute-start.46) | collective-permute-done | bytes 688160 | tf_op jit(solution)/shard_map/ppermute | solution.py:76
  411.8 5.7 collective-permute-done.52.refs_4_
  419.2 7.4 %collective-permute-done.49 = bf16[128,2688]{1,0:T(8,128)(2,1)S(1)} collective-permute-done((bf16[128,2688]{1,0:T(8,128)(2,1)S(1)}, bf16[128,2688]{1,0:T(8,128)(2,1)S(1)}, u32[]{:S(2)}, u32[]{:S(2)}) %collective-permute-start.49) | collective-permute-done | bytes 688160 | tf_op jit(solution)/shard_map/ppermute | solution.py:76
  426.6 15.3 %collective-permute-done.51 = bf16[176,2048]{1,0:T(8,128)(2,1)S(1)} collective-permute-done((bf16[176,2048]{1,0:T(8,128)(2,1)S(1)}, bf16[176,2048]{1,0:T(8,128)(2,1)S(1)}, u32[]{:S(2)}, u32[]{:S(2)}) %collective-permute-start.51) | collective-permute-done | bytes 720928 | tf_op jit(solution)/shard_map/ppermute | solution.py:83
  449.0 8.9 %collective-permute-done.55 = bf16[400,512]{1,0:T(8,128)(2,1)S(1)} collective-permute-done((bf16[400,512]{1,0:T(8,128)(2,1)S(1)}, bf16[400,512]{1,0:T(8,128)(2,1)S(1)}, u32[]{:S(2)}, u32[]{:S(2)}) %collective-permute-start.55) | collective-permute-done | bytes 409632 | tf_op jit(solution)/shard_map/ppermute | solution.py:129
  457.9 5.6 collective-permute-done.54.b
  478.1 6.4 %collective-permute-done.58.refs_3_ = bf16[128,2688]{1,0:T(8,128)(2,1)S(1)} collective-permute-done((bf16[128,2688]{1,0:T(8,128)(2,1)S(1)}, bf16[128,2688]{1,0:T(8,128)(2,1)S(1)}, u32[]{:S(2)}, u32[]{:S(2)}) %collective-permute-start.58) | collective-permute-done | bytes 688160 | tf_op jit(solution)/shard_map/ppermute | solution.py:76
  487.1 4.8 collective-permute-done.61
  491.9 8.4 %collective-permute-done.60.refs_2_ = bf16[128,2688]{1,0:T(8,128)(2,1)S(1)} collective-permute-done((bf16[128,2688]{1,0:T(8,128)(2,1)S(1)}, bf16[128,2688]{1,0:T(8,128)(2,1)S(1)}, u32[]{:S(2)}, u32[]{:S(2)}) %collective-permute-start.60) | collective-permute-done | bytes 688160 | tf_op jit(solution)/shard_map/ppermute | solution.py:76
  511.1 12.8 %collective-permute-done.65 = bf16[528,512]{1,0:T(8,128)(2,1)S(1)} collective-permute-done((bf16[528,512]{1,0:T(8,128)(2,1)}, bf16[528,512]{1,0:T(8,128)(2,1)S(1)}, u32[]{:S(2)}, u32[]{:S(2)}) %collective-permute-start.65) | collective-permute-done | bytes 540704 | tf_op jit(solution)/shard_map/ppermute | solution.py:83
  534.6 5.7 shard_map.332
  541.7 5.7 collective-permute-done.67.refs_9_
  549.0 6.0 collective-permute-done.69.refs_2_
  574.7 6.0 %collective-permute-done.74.refs_7_ = bf16[176,2048]{1,0:T(8,128)(2,1)} collective-permute-done((bf16[176,2048]{1,0:T(8,128)(2,1)}, bf16[176,2048]{1,0:T(8,128)(2,1)}, u32[]{:S(2)}, u32[]{:S(2)}) %collective-permute-start.74) | collective-permute-done | bytes 720928 | tf_op jit(solution)/shard_map/ppermute | solution.py:83
  586.9 4.6 shard_map.334
  (533 shorter events, 271.6 us)
Async XLA Ops:
  7.2 177.0 %all-gather.2.cloned.1.call-start = ((), (), s32[]{:S(2)}) async-start(), calls=%async_computation.1 | async-start | bytes 4456448 | tf_op jit(solution)/shard_map/all_gather | solution.py:737
  43.9 32.3 %collective-permute-start.9 = (bf16[352,2048]{1,0:T(8,128)(2,1)}, bf16[352,2048]{1,0:T(8,128)(2,1)}, u32[]{:S(2)}, u32[]{:S(2)}) collective-permute-start(bf16[352,2048]{1,0:T(8,128)(2,1)} %pad_maximum_fusion.1.refs_2_), channel_id=1, source_target_pairs={{96,0},{112,16},{0,32},{16,48},{32,64},{48,80},{64,96},{80,112},{9... | collective-permute-start | bytes 4325384 | tf_op jit(solution)/shard_map/ppermute | solution.py:83
  45.1 31.1 %collective-permute-start.8 = (bf16[352,2048]{1,0:T(8,128)(2,1)}, bf16[352,2048]{1,0:T(8,128)(2,1)}, u32[]{:S(2)}, u32[]{:S(2)}) collective-permute-start(bf16[352,2048]{1,0:T(8,128)(2,1)} %pad_maximum_fusion.1.refs_2_), channel_id=1, source_target_pairs={{32,0},{48,16},{64,32},{80,48},{96,64},{112,80},{0,96},{16,112},{3... | collective-permute-start | bytes 4325384 | tf_op jit(solution)/shard_map/ppermute | solution.py:83
  46.6 33.3 %collective-permute-start.7 = (bf16[352,2048]{1,0:T(8,128)(2,1)}, bf16[352,2048]{1,0:T(8,128)(2,1)}, u32[]{:S(2)}, u32[]{:S(2)}) collective-permute-start(bf16[352,2048]{1,0:T(8,128)(2,1)} %pad_maximum_fusion.1.refs_2_), channel_id=1, source_target_pairs={{16,0},{0,16},{48,32},{32,48},{80,64},{64,80},{112,96},{96,112},{1... | collective-permute-start | bytes 4325384 | tf_op jit(solution)/shard_map/ppermute | solution.py:83
  51.7 506.5 %reduce-scatter.2.cloned.1.call-start = ((), (), s32[]{:S(2)}) async-start(), calls=%async_computation.2 | async-start | bytes 4456448 | tf_op jit(solution)/shard_map/reduce_scatter | solution.py:849
  86.7 38.7 %collective-permute-start.15 = (bf16[352,2048]{1,0:T(8,128)(2,1)}, bf16[352,2048]{1,0:T(8,128)(2,1)}, u32[]{:S(2)}, u32[]{:S(2)}) collective-permute-start(bf16[352,2048]{1,0:T(8,128)(2,1)} %collective-permute-done.8.refs_4_), channel_id=1, source_target_pairs={{16,0},{0,16},{48,32},{32,48},{80,64},{64,80},{112,96},{96,112},{1... | collective-permute-start | bytes 4325384 | tf_op jit(solution)/shard_map/ppermute | solution.py:83
  108.9 37.9 %collective-permute-start.19 = (bf16[352,2048]{1,0:T(8,128)(2,1)}, bf16[352,2048]{1,0:T(8,128)(2,1)}, u32[]{:S(2)}, u32[]{:S(2)}) collective-permute-start(bf16[352,2048]{1,0:T(8,128)(2,1)} %pad_maximum_fusion.1.refs_2_), channel_id=1, source_target_pairs={{64,0},{80,16},{96,32},{112,48},{0,64},{16,80},{32,96},{48,112},{6... | collective-permute-start | bytes 4325384 | tf_op jit(solution)/shard_map/ppermute | solution.py:83
  178.6 52.2 %collective-permute-start.24 = (bf16[352,2048]{1,0:T(8,128)(2,1)}, bf16[352,2048]{1,0:T(8,128)(2,1)}, u32[]{:S(2)}, u32[]{:S(2)}) collective-permute-start(bf16[352,2048]{1,0:T(8,128)(2,1)} %collective-permute-done.9.refs_6_), channel_id=1, source_target_pairs={{16,0},{0,16},{48,32},{32,48},{80,64},{64,80},{112,96},{96,112},{1... | collective-permute-start | bytes 4325384 | tf_op jit(solution)/shard_map/ppermute | solution.py:83
  178.7 52.2 %collective-permute-start.26 = (bf16[352,2048]{1,0:T(8,128)(2,1)}, bf16[352,2048]{1,0:T(8,128)(2,1)}, u32[]{:S(2)}, u32[]{:S(2)}) collective-permute-start(bf16[352,2048]{1,0:T(8,128)(2,1)} %collective-permute-done.7.refs_8_), channel_id=1, source_target_pairs={{64,0},{80,16},{96,32},{112,48},{0,64},{16,80},{32,96},{48,112},{6... | collective-permute-start | bytes 4325384 | tf_op jit(solution)/shard_map/ppermute | solution.py:83
  180.0 50.9 %collective-permute-start.25 = (bf16[176,2048]{1,0:T(8,128)(2,1)}, bf16[176,2048]{1,0:T(8,128)(2,1)}, u32[]{:S(2)}, u32[]{:S(2)}) collective-permute-start(bf16[176,2048]{1,0:T(8,128)(2,1)} %collective-permute-done.13.refs_7_), channel_id=1, source_target_pairs={{16,0},{0,16},{48,32},{32,48},{80,64},{64,80},{112,96},{96,112},{1... | collective-permute-start | bytes 2162696 | tf_op jit(solution)/shard_map/ppermute | solution.py:83
  181.8 49.0 %collective-permute-start.27 = (bf16[176,2048]{1,0:T(8,128)(2,1)}, bf16[176,2048]{1,0:T(8,128)(2,1)}, u32[]{:S(2)}, u32[]{:S(2)}) collective-permute-start(bf16[176,2048]{1,0:T(8,128)(2,1)} %collective-permute-done.5.refs_9_), channel_id=1, source_target_pairs={{64,0},{80,16},{96,32},{112,48},{0,64},{16,80},{32,96},{48,112},{6... | collective-permute-start | bytes 2162696 | tf_op jit(solution)/shard_map/ppermute | solution.py:83
  230.9 27.8 %collective-permute-start.28 = (bf16[528,1024]{1,0:T(8,128)(2,1)}, bf16[528,1024]{1,0:T(8,128)(2,1)S(1)}, u32[]{:S(2)}, u32[]{:S(2)}) collective-permute-start(bf16[528,1024]{1,0:T(8,128)(2,1)} %get-tuple-element.401), channel_id=1, source_target_pairs={{16,0},{0,16},{48,32},{32,48},{80,64},{64,80},{112,96},{96,112},{1... | collective-permute-start | bytes 3244040 | tf_op jit(solution)/shard_map/ppermute | solution.py:83
  263.6 35.0 %collective-permute-start.33 = (bf16[352,2048]{1,0:T(8,128)(2,1)}, bf16[352,2048]{1,0:T(8,128)(2,1)}, u32[]{:S(2)}, u32[]{:S(2)}) collective-permute-start(bf16[352,2048]{1,0:T(8,128)(2,1)} %get-tuple-element.429), channel_id=1, source_target_pairs={{64,0},{80,16},{96,32},{112,48},{0,64},{16,80},{32,96},{48,112},{6... | collective-permute-start | bytes 4325384 | tf_op jit(solution)/shard_map/ppermute | solution.py:83
  265.1 33.5 %collective-permute-start.34 = (bf16[352,2048]{1,0:T(8,128)(2,1)}, bf16[352,2048]{1,0:T(8,128)(2,1)}, u32[]{:S(2)}, u32[]{:S(2)}) collective-permute-start(bf16[352,2048]{1,0:T(8,128)(2,1)} %get-tuple-element.430), channel_id=1, source_target_pairs={{16,0},{0,16},{48,32},{32,48},{80,64},{64,80},{112,96},{96,112},{1... | collective-permute-start | bytes 4325384 | tf_op jit(solution)/shard_map/ppermute | solution.py:83
  288.6 25.3 %collective-permute-start.36 = (bf16[176,2048]{1,0:T(8,128)(2,1)S(1)}, bf16[176,2048]{1,0:T(8,128)(2,1)S(1)}, u32[]{:S(2)}, u32[]{:S(2)}) collective-permute-start(bf16[176,2048]{1,0:T(8,128)(2,1)S(1)} %copy-done.139), channel_id=1, source_target_pairs={{64,0},{80,16},{96,32},{112,48},{0,64},{16,80},{32,96},{48,112},{6... | collective-permute-start | bytes 2162696 | tf_op jit(solution)/shard_map/ppermute | solution.py:83
  304.4 40.7 %collective-permute-start.40 = (bf16[352,2048]{1,0:T(8,128)(2,1)S(1)}, bf16[352,2048]{1,0:T(8,128)(2,1)S(1)}, u32[]{:S(2)}, u32[]{:S(2)}) collective-permute-start(bf16[352,2048]{1,0:T(8,128)(2,1)S(1)} %copy-done.137), channel_id=1, source_target_pairs={{16,0},{0,16},{48,32},{32,48},{80,64},{64,80},{112,96},{96,112},{1... | collective-permute-start | bytes 4325384 | tf_op jit(solution)/shard_map/ppermute | solution.py:83
  305.5 39.6 %collective-permute-start.41 = (bf16[352,2048]{1,0:T(8,128)(2,1)S(1)}, bf16[352,2048]{1,0:T(8,128)(2,1)S(1)}, u32[]{:S(2)}, u32[]{:S(2)}) collective-permute-start(bf16[352,2048]{1,0:T(8,128)(2,1)S(1)} %copy-done.136), channel_id=1, source_target_pairs={{64,0},{80,16},{96,32},{112,48},{0,64},{16,80},{32,96},{48,112},{6... | collective-permute-start | bytes 4325384 | tf_op jit(solution)/shard_map/ppermute | solution.py:83
  352.0 19.3 %collective-permute-start.43 = (bf16[176,2048]{1,0:T(8,128)(2,1)S(1)}, bf16[176,2048]{1,0:T(8,128)(2,1)S(1)}, u32[]{:S(2)}, u32[]{:S(2)}) collective-permute-start(bf16[176,2048]{1,0:T(8,128)(2,1)S(1)} %copy-done.100), channel_id=1, source_target_pairs={{64,0},{80,16},{96,32},{112,48},{0,64},{16,80},{32,96},{48,112},{6... | collective-permute-start | bytes 2162696 | tf_op jit(solution)/shard_map/ppermute | solution.py:83
  382.2 35.3 %collective-permute-start.52 = (bf16[352,2048]{1,0:T(8,128)(2,1)S(1)}, bf16[352,2048]{1,0:T(8,128)(2,1)S(1)}, u32[]{:S(2)}, u32[]{:S(2)}) collective-permute-start(bf16[352,2048]{1,0:T(8,128)(2,1)S(1)} %copy-done.113), channel_id=1, source_target_pairs={{16,0},{0,16},{48,32},{32,48},{80,64},{64,80},{112,96},{96,112},{1... | collective-permute-start | bytes 4325384 | tf_op jit(solution)/shard_map/ppermute | solution.py:83
  393.2 24.3 %collective-permute-start.50 = (bf16[400,1024]{1,0:T(8,128)(2,1)S(1)}, bf16[400,1024]{1,0:T(8,128)(2,1)S(1)}, u32[]{:S(2)}, u32[]{:S(2)}) collective-permute-start(bf16[400,1024]{1,0:T(8,128)(2,1)S(1)} %get-tuple-element.600), channel_id=1, source_target_pairs={{64,0},{80,16},{96,32},{112,48},{0,64},{16,80},{32,96},{48,112},{6... | collective-permute-start | bytes 2457608 | tf_op jit(solution)/shard_map/ppermute | solution.py:83
  405.8 20.8 %collective-permute-start.49 = (bf16[128,2688]{1,0:T(8,128)(2,1)S(1)}, bf16[128,2688]{1,0:T(8,128)(2,1)S(1)}, u32[]{:S(2)}, u32[]{:S(2)}) collective-permute-start(bf16[128,2688]{1,0:T(8,128)(2,1)S(1)} %get-tuple-element.501), channel_id=1, source_target_pairs={{4,0},{5,1},{6,2},{7,3},{0,4},{1,5},{2,6},{3,7},{12,8},{13,9},{14,... | collective-permute-start | bytes 2064392 | tf_op jit(solution)/shard_map/ppermute | solution.py:76
  407.8 34.0 %collective-permute-start.51 = (bf16[176,2048]{1,0:T(8,128)(2,1)S(1)}, bf16[176,2048]{1,0:T(8,128)(2,1)S(1)}, u32[]{:S(2)}, u32[]{:S(2)}) collective-permute-start(bf16[176,2048]{1,0:T(8,128)(2,1)S(1)} %copy-done.138), channel_id=1, source_target_pairs={{16,0},{0,16},{48,32},{32,48},{80,64},{64,80},{112,96},{96,112},{1... | collective-permute-start | bytes 2162696 | tf_op jit(solution)/shard_map/ppermute | solution.py:83
  443.3 20.3 %collective-permute-start.54 = (bf16[128,2688]{1,0:T(8,128)(2,1)S(1)}, bf16[128,2688]{1,0:T(8,128)(2,1)S(1)}, u32[]{:S(2)}, u32[]{:S(2)}) collective-permute-start(bf16[128,2688]{1,0:T(8,128)(2,1)S(1)} %add_convert_fusion.8.a), channel_id=1, source_target_pairs={{8,0},{9,1},{10,2},{11,3},{12,4},{13,5},{14,6},{15,7},{0,8},{1,9},... | collective-permute-start | bytes 2064392 | tf_op jit(solution)/shard_map/ppermute | solution.py:76
  463.5 36.8 %collective-permute-start.62 = (bf16[352,2048]{1,0:T(8,128)(2,1)}, bf16[352,2048]{1,0:T(8,128)(2,1)S(1)}, u32[]{:S(2)}, u32[]{:S(2)}) collective-permute-start(bf16[352,2048]{1,0:T(8,128)(2,1)} %add_convert_fusion.1), channel_id=1, source_target_pairs={{96,0},{112,16},{0,32},{16,48},{32,64},{48,80},{64,96},{80,112},{9... | collective-permute-start | bytes 4325384 | tf_op jit(solution)/shard_map/ppermute | solution.py:83
  464.2 37.3 %collective-permute-start.63 = (bf16[352,2048]{1,0:T(8,128)(2,1)}, bf16[352,2048]{1,0:T(8,128)(2,1)}, u32[]{:S(2)}, u32[]{:S(2)}) collective-permute-start(bf16[352,2048]{1,0:T(8,128)(2,1)} %add_convert_fusion), channel_id=1, source_target_pairs={{32,0},{48,16},{64,32},{80,48},{96,64},{112,80},{0,96},{16,112},{3... | collective-permute-start | bytes 4325384 | tf_op jit(solution)/shard_map/ppermute | solution.py:83
  503.8 20.9 %collective-permute-start.64 = (bf16[512,2688]{1,0:T(8,128)(2,1)S(1)}, bf16[512,2688]{1,0:T(8,128)(2,1)}, u32[]{:S(2)}, u32[]{:S(2)}) collective-permute-start(bf16[512,2688]{1,0:T(8,128)(2,1)S(1)} %shard_map.330.a), channel_id=1, source_target_pairs={{1,0},{0,1},{3,2},{2,3},{5,4},{4,5},{7,6},{6,7},{9,8},{8,9},{11,10... | collective-permute-start | bytes 8257544 | tf_op jit(solution)/shard_map/ppermute | solution.py:76
  532.0 23.0 %collective-permute-start.69 = (bf16[400,512]{1,0:T(8,128)(2,1)S(1)}, bf16[400,512]{1,0:T(8,128)(2,1)S(1)}, u32[]{:S(2)}, u32[]{:S(2)}) collective-permute-start(bf16[400,512]{1,0:T(8,128)(2,1)S(1)} %pad_maximum_fusion.6.refs_0_), channel_id=1, source_target_pairs={{64,0},{80,16},{96,32},{112,48},{0,64},{16,80},{32,96},{48,112},{6... | collective-permute-start | bytes 1228808 | tf_op jit(solution)/shard_map/ppermute | solution.py:83
  533.4 22.4 %collective-permute-start.68 = (bf16[400,512]{1,0:T(8,128)(2,1)S(1)}, bf16[400,512]{1,0:T(8,128)(2,1)S(1)}, u32[]{:S(2)}, u32[]{:S(2)}) collective-permute-start(bf16[400,512]{1,0:T(8,128)(2,1)S(1)} %pad_maximum_fusion.6.refs_0_), channel_id=1, source_target_pairs={{32,0},{48,16},{64,32},{80,48},{96,64},{112,80},{0,96},{16,112},{3... | collective-permute-start | bytes 1228808 | tf_op jit(solution)/shard_map/ppermute | solution.py:83
  540.5 30.2 %collective-permute-start.72 = (bf16[528,1024]{1,0:T(8,128)(2,1)S(1)}, bf16[528,1024]{1,0:T(8,128)(2,1)}, u32[]{:S(2)}, u32[]{:S(2)}) collective-permute-start(bf16[528,1024]{1,0:T(8,128)(2,1)S(1)} %constant_dynamic-update-slice_fusion.2.a), channel_id=1, source_target_pairs={{16,0},{0,16},{48,32},{32,48},{80,64},{64,80},{112,96},{96,112},{1... | collective-permute-start | bytes 3244040 | tf_op jit(solution)/shard_map/ppermute | solution.py:83
  560.1 20.7 %collective-permute-start.74 = (bf16[176,2048]{1,0:T(8,128)(2,1)}, bf16[176,2048]{1,0:T(8,128)(2,1)}, u32[]{:S(2)}, u32[]{:S(2)}) collective-permute-start(bf16[176,2048]{1,0:T(8,128)(2,1)} %add_convert_fusion.6), channel_id=1, source_target_pairs={{96,0},{112,16},{0,32},{16,48},{32,64},{48,80},{64,96},{80,112},{9... | collective-permute-start | bytes 2162696 | tf_op jit(solution)/shard_map/ppermute | solution.py:83
  560.1 20.7 %collective-permute-start.75 = (bf16[176,2048]{1,0:T(8,128)(2,1)}, bf16[176,2048]{1,0:T(8,128)(2,1)}, u32[]{:S(2)}, u32[]{:S(2)}) collective-permute-start(bf16[176,2048]{1,0:T(8,128)(2,1)} %add_convert_fusion.5), channel_id=1, source_target_pairs={{32,0},{48,16},{64,32},{80,48},{96,64},{112,80},{0,96},{16,112},{3... | collective-permute-start | bytes 2162696 | tf_op jit(solution)/shard_map/ppermute | solution.py:83
  570.7 20.8 %collective-permute-start.73 = (bf16[64,2048]{1,0:T(8,128)(2,1)S(1)}, bf16[64,2048]{1,0:T(8,128)(2,1)S(1)}, u32[]{:S(2)}, u32[]{:S(2)}) collective-permute-start(bf16[64,2048]{1,0:T(8,128)(2,1)S(1)} %add_convert_fusion.16), channel_id=1, source_target_pairs={{16,0},{0,16},{48,32},{32,48},{80,64},{64,80},{112,96},{96,112},{1... | collective-permute-start | bytes 786440 | tf_op jit(solution)/shard_map/ppermute | solution.py:83
  (186 other events, 1659.5 us)
Sparse Core Ops, SparseCore 0:
  51.8 76.4 all-gather.1
  377.0 92.1 reduce-scatter.1

commit v4 on v3

--- a/solution.py
+++ b/solution.py
@@ -795,10 +795,14 @@
     at_sum = add(at_b[0], *at_y)
     at_other = recv_t(at_sum, zh=1)
     at_sum, at_other, ap_dn, am_gu, own_dn = sync(at_sum, at_other, ap_dn, am_gu, own_dn)
-    hidden, rows2, inv2, probs = rows_mid((at_sum, at_other), own_rows(tokens), norm2_gain[None, :], w_router)
+    own_tokens = own_rows(tokens)
+    hidden, rows2, inv2, probs = rows_mid((at_sum, at_other), own_tokens, norm2_gain[None, :], w_router)
     n2_y1, n2_y3 = recv_t(rows2, y=1), recv_t(rows2, y=-1)
     bp_dn = recv_d(ap_dn, z=1)
-    rows2, n2_y1, n2_y3, a2_gu, own_dn = sync(rows2, n2_y1, n2_y3, a2_gu, own_dn)
+    own_inv1, own_lat, own_inv_lat = own_rows(inv1), own_rows(latent), own_rows(inv_lat)
+    rows2, n2_y1, n2_y3, a2_gu, own_dn, own_inv1, own_lat, own_inv_lat = sync(
+        rows2, n2_y1, n2_y3, a2_gu, own_dn, own_inv1, own_lat, own_inv_lat
+    )
     n2_y2 = recv_t(rows2, y=2)
     a2_dn = recv_d(own_dn, x=2)
     rows2, n2_y1, n2_y2, n2_y3, bp_dn, am_gu, am_dn, zz_gu, zz_dn, a2_dn = sync(
@@ -857,7 +861,6 @@
     n2_sum, n2_other, r_b2_dn, g_bp_dn, sh_keep, sh_send, r_b2_gu, r_bp_gu, g_z_gu, g_ap_gu, g_z_dn = sync(
         n2_sum, n2_other, r_b2_dn, g_bp_dn, sh_keep, sh_send, r_b2_gu, r_bp_gu, g_z_gu, g_ap_gu, g_z_dn
     )
-
     hid_grad, payload, gain2 = rows_two(
         (n2_sum, n2_other), hidden, inv2, probs, own_rows(out_grad), norm2_gain[None, :], w_router_t
     )
@@ -891,16 +894,15 @@
     rest = cat(w_query_g, w_out_g, w_expand_g, w_router_g)
     rest_half, rest_send = halves(rest, x // 2)
     rest_got = recv_d(rest_send, x=2)
-    n1_y1, n1_y3, n1_b2, rest_half, g_am_gu, g_ap_dn, sh_keep, sh_got, g_bm_dn = sync(
-        n1_y1, n1_y3, n1_b[2], rest_half, g_am_gu, g_ap_dn, sh_keep, sh_got, g_bm_dn
+    n1_y1, n1_y3, n1_b2, rest_half, g_am_gu, g_ap_dn, sh_keep, sh_got = sync(
+        n1_y1, n1_y3, n1_b[2], rest_half, g_am_gu, g_ap_dn, sh_keep, sh_got
     )
     n1_y2 = recv_t(n1_b2, y=2)
-    r_bm_dn = recv_d(g_bm_dn, z=1)
     am_gu_sum, ap_dn_sum = add(g_am_gu, r_bm_gu), add(g_ap_dn, r_bp_dn)
     sh_keep, sh_send = halves(add(sh_keep, sh_got), x % 2)
     sh_got = swap_x(sh_send)
-    n1_y1, n1_y3, n1_y2, rest_half, rest_got, r_bm_dn, r_z_gu, am_gu_sum, ap_dn_sum, sh_keep, sh_got = sync(
-        n1_y1, n1_y3, n1_y2, rest_half, rest_got, r_bm_dn, r_z_gu, am_gu_sum, ap_dn_sum, sh_keep, sh_got
+    n1_y1, n1_y3, n1_y2, rest_half, rest_got, r_z_gu, am_gu_sum, ap_dn_sum, sh_keep, sh_got = sync(
+        n1_y1, n1_y3, n1_y2, rest_half, rest_got, r_z_gu, am_gu_sum, ap_dn_sum, sh_keep, sh_got
     )
     n1_sum = add(n1_b[0], n1_y1, n1_y2, n1_y3)
     n1_other = recv_t(n1_sum, zh=1)
@@ -908,45 +910,47 @@
     rest_got = swap_x(rest_send)
     sh_own = add(sh_keep, sh_got)
     sh_next = swap_x(sh_own)
-    am_dn_sum = add(g_am_dn, r_bm_dn)
-    n1_sum, n1_other, rest_keep, rest_got, sh_own, sh_next, am_gu_sum, ap_gu_sum, ap_dn_sum, am_dn_sum, z_dn_sum = sync(
-        n1_sum, n1_other, rest_keep, rest_got, sh_own, sh_next, am_gu_sum, ap_gu_sum, ap_dn_sum, am_dn_sum, z_dn_sum
+    n1_sum, n1_other, rest_keep, rest_got, sh_own, sh_next, am_gu_sum, ap_gu_sum, g_bm_dn = sync(
+        n1_sum, n1_other, rest_keep, rest_got, sh_own, sh_next, am_gu_sum, ap_gu_sum, g_bm_dn
     )
     tok_rows = rows_one(
         (n1_sum, n1_other),
         w_lat,
-        own_rows(tokens),
-        own_rows(inv1),
+        own_tokens,
+        own_inv1,
         hid_grad,
         norm1_gain[None, :],
-        own_rows(latent),
-        own_rows(inv_lat),
+        own_lat,
+        own_inv_lat,
         latent_gain[None, :],
         gain2,
     )
     t1, t3 = recv_t(tok_rows, y=1), recv_t(tok_rows, y=-1)
     r_ap_gu, r_am_gu = recv_d(ap_gu_sum, x=-1), recv_d(am_gu_sum, x=1)
+    r_bm_dn = recv_d(g_bm_dn, z=1)
+    sh_pair = jnp.concatenate([sh_own, sh_next], axis=1)
     rest_keep, rest_send = halves(add(rest_keep, rest_got), z)
+    tok_rows, t1, t3, rest_keep, rest_send, sh_pair, r_bm_dn, g_am_dn, z_dn_sum = sync(
+        tok_rows, t1, t3, rest_keep, rest_send, sh_pair, r_bm_dn, g_am_dn, z_dn_sum
+    )
+    t2 = recv_t(tok_rows, y=2)
     rest_got = recv_d(rest_send, z=1)
-    sh_pair = jnp.concatenate([sh_own, sh_next], axis=1)
-    tok_rows, t1, t3, rest_keep, rest_got, sh_pair, z_dn_sum = sync(
-        tok_rows, t1, t3, rest_keep, rest_got, sh_pair, z_dn_sum
-    )
-    t2 = recv_t(tok_rows, y=2)
+    r_z_dn = recv_d(z_dn_sum, z=1)
+    am_dn_sum = add(g_am_dn, r_bm_dn)
+    tok_rows, t1, t2, t3, rest_keep, rest_got, sh_pair, ap_dn_sum, am_dn_sum, r_z_dn, r_ap_gu, r_am_gu = sync(
+        tok_rows, t1, t2, t3, rest_keep, rest_got, sh_pair, ap_dn_sum, am_dn_sum, r_z_dn, r_ap_gu, r_am_gu
+    )
     rest_own = add(rest_keep, rest_got)
     rest_pair = recv_d(rest_own, z=1)
-    tok_rows, t1, t2, t3, rest_own, rest_pair, sh_pair, ap_dn_sum, am_dn_sum, z_dn_sum, r_ap_gu, r_am_gu = sync(
-        tok_rows, t1, t2, t3, rest_own, rest_pair, sh_pair, ap_dn_sum, am_dn_sum, z_dn_sum, r_ap_gu, r_am_gu
-    )
     sh_far = recv_d(sh_pair, x=2)
+    r_ap_dn, r_am_dn = recv_d(ap_dn_sum, x=-1), recv_d(am_dn_sum, x=1)
     tok_half = stack(tok_rows, t1, t2, t3)
     tok_other = recv_t(tok_half, c=1)
-    r_z_dn = recv_d(z_dn_sum, z=1)
+    tok_half, tok_other, rest_own, rest_pair, sh_pair, sh_far, branch_sum = sync(
+        tok_half, tok_other, rest_own, rest_pair, sh_pair, sh_far, branch_sum
+    )
     pair = jnp.concatenate([rest_own, rest_pair], axis=1)
-    tok_half, tok_other, pair, sh_pair, sh_far = sync(tok_half, tok_other, pair, sh_pair, sh_far)
     blocks = [pair] + [recv_d(pair, x=i) for i in (1, 2, 3)]
-    sh_half = jnp.concatenate([sh_pair, sh_far], axis=1)
-    sh_across = recv_d(sh_half, z=1)
     pick = (
         (jnp.arange(LX, dtype=jnp.int32)[None, :] == tr * LW + column[:LW48, None]) & (column[:LW48, None] < LW)
     ).astype(BF)
@@ -955,19 +959,19 @@
     gains = jnp.pad(gains[: GAINS // FREE, 128 - FREE :].reshape(-1), (0, 16 * D - GAINS)).reshape(16, D)
     small = cat(w_lat_g, gains.astype(BF))
     own_cols = lax.dynamic_slice_in_dim(tokens, tr * 128, 128, 1).astype(F32)
+    small = sum_d(small, 0)
+    sh_half = jnp.concatenate([sh_pair, sh_far], axis=1)
+    small, sh_half, r_ap_dn, r_am_dn = sync(small, sh_half, r_ap_dn, r_am_dn)
     small = sum_d(small, 1)
+    sh_across = recv_d(sh_half, z=1)
     tokens_grad = spread(starts8, tok_half, tok_other)
-    small, tokens_grad, r_z_dn, ap_dn_sum, am_dn_sum, *blocks = sync(
-        small, tokens_grad, r_z_dn, ap_dn_sum, am_dn_sum, *blocks
-    )
+    wq_grad, wo_grad, we_grad, wr_grad = finish_rest(offsets, blocks)
+    small, tokens_grad, wq_grad = sync(small, tokens_grad, wq_grad)
     small = sum_d(small, 2)
-    r_ap_dn, r_am_dn = recv_d(ap_dn_sum, x=-1), recv_d(am_dn_sum, x=1)
-    wq_grad, wo_grad, we_grad, wr_grad = finish_rest(offsets, blocks)
     output = (own_cols + branch_sum.astype(F32)).astype(BF)
     small, wq_grad, wo_grad, we_grad, wr_grad, output, sh_across = sync(
         small, wq_grad, wo_grad, we_grad, wr_grad, output, sh_across
     )
-    small = sum_d(small, 0)
     sh_offsets = jnp.stack([((z + j) % 2 * 4 + (x ^ i)) * 256 for j in range(2) for i in range(4)])
     sg_grad, su_grad, sd_grad = finish_shared(sh_offsets, sh_half, sh_across)
     eg_grad, eu_grad, ed_grad = finish_experts(

time: 610 us -> 588 us (0.964)
  waiting for transfers between devices: 220 us -> 182 us
  starting transfers between devices: 113 us -> 121 us
    ppermute x40, waiting for transfers between devices: 128 us -> 107 us  [recv_d(): return lax.ppermute(a, 'dp', pairs)]
    ppermute x32, waiting for transfers between devices: 80.5 us -> 60.6 us  [recv_t(): return lax.ppermute(a, 'tensor', pairs)]
    ppermute x32, starting transfers between devices: 65.3 us -> 72.5 us  [recv_t(): return lax.ppermute(a, 'tensor', pairs)]
    unnamed x294 -> x272, local copies, waits for them, and re-layouts: 47.4 us -> 46.6 us
  transfers between devices with their start and end apart: 78 -> 78, of which waited for: 37 -> 34; matrix products, arithmetic and copies ran while one was open for 10% -> 11% of each run, Pallas kernels for 24% -> 24%
where the time goes in v4:
time: 588 us; the launch traced here: 579 us
  waiting for transfers between devices  182 us (31%)
  Pallas kernels  145 us (25%)
  starting transfers between devices  121 us (21%)
  local copies, waits for them, and re-layouts  64.8 us (11%)
  other arithmetic  46.1 us (8%)
  between operations  15.9 us (3%)
    ppermute x40, waiting for transfers between devices, recv_d(): return lax.ppermute(a, 'dp', pairs)  107 us
    ppermute x32, starting transfers between devices, recv_t(): return lax.ppermute(a, 'tensor', pairs)  72.5 us
    ppermute x32, waiting for transfers between devices, recv_t(): return lax.ppermute(a, 'tensor', pairs)  60.6 us
    pallas_call x17, Pallas kernels, whole(): pl.pallas_call(kernel, out_shape=outs, in_specs=specs, out_specs=[VM] * l...  54.4 us
    pallas_call x2, Pallas kernels, experts(): pl.pallas_call(kernel, out_shape=[sds(a.shape, BF) for _, _, a in pieces]...  48.9 us
    unnamed x272, local copies, waits for them, and re-layouts  46.6 us
    ppermute x40, starting transfers between devices, recv_d(): return lax.ppermute(a, 'dp', pairs)  45 us
    convert_element_type x15, other arithmetic, add(): return sum((t.astype(F32) for t in terms)).astype(BF)  18 us
  transfers between devices with their start and end apart: 78, of which 34 were waited for; matrix products, arithmetic and copies ran while one was open for 11% of the time, Pallas kernels for 24%

profile of v4, /device:TPU:1, one launch (start us, length us, event | category | flops | bytes accessed | tf_op | source)
XLA Modules:
  0.0 578.7 jit_solution(4601927325376655293)
XLA Ops:
  7.2 4.5 collective-permute-start
  56.9 9.7 %shard_map.307 = (bf16[640,2048]{1,0:T(8,128)(2,1)S(1)}, bf16[1024,640]{1,0:T(8,128)(2,1)S(1)}, f32[1024,1]{1,0:T(8,128)S(1)}, bf16[1024,512]{1,0:T(8,128)(2,1)S...) custom-call(bf16[1024,2048]{1,0:T(8,128)(2,1)S(1)} %copy-done.1, ...), custom_call_target="tpu_custom_call" | custom-call | flops 1 | bytes 1 | tf_op jit(solution)/shard_map/pallas_call | solution.py:276
  68.7 6.2 %shard_map.308.m = bf16[1024,128]{1,0:T(8,128)(2,1)S(1)} custom-call(s32[1,2]{1,0:T(1,128)S(1)} %copy-done.89, bf16[1024,128]{1,0:T(8,128)(2,1)S(1)} %copy-done.25, bf16[1024,64]{1,0:T(8,128)(2,1)S(1)} %copy-done.23, bf16[1024,128]{1,0:T(8,128)(2,1)S(1)} %get-tuple-element.327.kn, bf16[1024,64]{1,0:T(8,128)(2,1)S(1)} %get-tuple-element.328.kr, ...), custom_call_target="tpu_custom_call" | custom-call | flops 1 | bytes 1 | tf_op jit(solution)/shard_map/pallas_call | solution.py:193
  76.4 3.7 collective-permute-done.7.refs_8_
  80.1 6.8 %collective-permute-start.10 = (bf16[512,2048]{1,0:T(8,128)(2,1)S(1)}, bf16[512,2048]{1,0:T(8,128)(2,1)}, u32[]{:S(2)}, u32[]{:S(2)}) collective-permute-start(bf16[512,2048]{1,0:T(8,128)(2,1)S(1)} %shard_map.309), channel_id=1, source_target_pairs={{1,0},{0,1},{3,2},{2,3},{5,4},{4,5},{7,6},{6,7},{9,8},{8,9},{11,10... | collective-permute-start | bytes 6291464 | tf_op jit(solution)/shard_map/ppermute | solution.py:76
  95.7 12.4 %collective-permute-done.13.refs_7_ = bf16[176,2048]{1,0:T(8,128)(2,1)} collective-permute-done((bf16[176,2048]{1,0:T(8,128)(2,1)}, bf16[176,2048]{1,0:T(8,128)(2,1)}, u32[]{:S(2)}, u32[]{:S(2)}) %collective-permute-start.13) | collective-permute-done | bytes 720928 | tf_op jit(solution)/shard_map/ppermute | solution.py:83
  109.1 16.5 %collective-permute-done.15.refs_8_ = bf16[352,2048]{1,0:T(8,128)(2,1)} collective-permute-done((bf16[352,2048]{1,0:T(8,128)(2,1)}, bf16[352,2048]{1,0:T(8,128)(2,1)}, u32[]{:S(2)}, u32[]{:S(2)}) %collective-permute-start.15) | collective-permute-done | bytes 1441824 | tf_op jit(solution)/shard_map/ppermute | solution.py:83
  128.5 12.1 %collective-permute-done.16.b = bf16[128,2048]{1,0:T(8,128)(2,1)S(1)} collective-permute-done((bf16[128,2048]{1,0:T(8,128)(2,1)S(1)}, bf16[128,2048]{1,0:T(8,128)(2,1)S(1)}, u32[]{:S(2)}, u32[]{:S(2)}) %collective-permute-start.16) | collective-permute-done | bytes 524320 | tf_op jit(solution)/shard_map/ppermute | solution.py:76
  151.3 6.4 %collective-permute-done.18.refs_3_ = bf16[128,2048]{1,0:T(8,128)(2,1)S(1)} collective-permute-done((bf16[128,2048]{1,0:T(8,128)(2,1)S(1)}, bf16[128,2048]{1,0:T(8,128)(2,1)S(1)}, u32[]{:S(2)}, u32[]{:S(2)}) %collective-permute-start.18) | collective-permute-done | bytes 524320 | tf_op jit(solution)/shard_map/ppermute | solution.py:76
  160.5 6.9 %collective-permute-done.21.refs_9_ = bf16[176,2048]{1,0:T(8,128)(2,1)S(1)} collective-permute-done((bf16[176,2048]{1,0:T(8,128)(2,1)}, bf16[176,2048]{1,0:T(8,128)(2,1)S(1)}, u32[]{:S(2)}, u32[]{:S(2)}) %collective-permute-start.21) | collective-permute-done | bytes 720928 | tf_op jit(solution)/shard_map/ppermute | solution.py:83
  167.4 4.1 collective-permute-done.20.refs_2_
  184.3 21.4 %shard_map.314 = (bf16[1024,2048]{1,0:T(8,128)(2,1)}, f32[1024,1]{1,0:T(8,128)}, bf16[480,2048]{1,0:T(8,128)(2,1)}, bf16[480,2048]{1,0:T(8,128)(2,1)}, bf16[480,...) custom-call(s32[8]{0:T(128)} %stack.115.s, ...), custom_call_target="tpu_custom_call" | custom-call | flops 1 | bytes 1 | tf_op jit(solution)/shard_map/pallas_call | solution.py:54
  205.8 23.5 %shard_map.315 = (bf16[352,2048]{1,0:T(8,128)(2,1)}, bf16[176,2048]{1,0:T(8,128)(2,1)S(1)}, bf16[352,2048]{1,0:T(8,128)(2,1)}, bf16[176,2048]{1,0:T(8,128)(2,1)S...) custom-call(bf16[480,2048]{1,0:T(8,128)(2,1)} %get-tuple-element.382, ...), custom_call_target="tpu_custom_call" | custom-call | flops 1 | bytes 1 | tf_op jit(solution)/shard_map/pallas_call | solution.py:446
  231.7 25.4 %shard_map.316 = (bf16[352,2048]{1,0:T(8,128)(2,1)}, bf16[176,2048]{1,0:T(8,128)(2,1)S(1)}, bf16[352,2048]{1,0:T(8,128)(2,1)}, bf16[176,2048]{1,0:T(8,128)(2,1)S...) custom-call(s32[1]{0:T(128)} %bitcast.26.me.refs_0_, ...), custom_call_target="tpu_custom_call" | custom-call | flops 1 | bytes 1 | tf_op jit(solution)/shard_map/pallas_call | solution.py:446
  278.0 4.7 shard_map.320
  290.4 8.3 %collective-permute-done.33 = bf16[352,2048]{1,0:T(8,128)(2,1)} collective-permute-done((bf16[352,2048]{1,0:T(8,128)(2,1)}, bf16[352,2048]{1,0:T(8,128)(2,1)}, u32[]{:S(2)}, u32[]{:S(2)}) %collective-permute-start.33) | collective-permute-done | bytes 1441824 | tf_op jit(solution)/shard_map/ppermute | solution.py:83
  307.6 6.5 %collective-permute-done.36 = bf16[176,2048]{1,0:T(8,128)(2,1)S(1)} collective-permute-done((bf16[176,2048]{1,0:T(8,128)(2,1)S(1)}, bf16[176,2048]{1,0:T(8,128)(2,1)S(1)}, u32[]{:S(2)}, u32[]{:S(2)}) %collective-permute-start.36) | collective-permute-done | bytes 720928 | tf_op jit(solution)/shard_map/ppermute | solution.py:83
  332.8 12.5 %collective-permute-done.40 = bf16[352,2048]{1,0:T(8,128)(2,1)S(1)} collective-permute-done((bf16[352,2048]{1,0:T(8,128)(2,1)S(1)}, bf16[352,2048]{1,0:T(8,128)(2,1)S(1)}, u32[]{:S(2)}, u32[]{:S(2)}) %collective-permute-start.40) | collective-permute-done | bytes 1441824 | tf_op jit(solution)/shard_map/ppermute | solution.py:83
  347.1 5.1 collective-permute-start.42
  359.4 9.9 %shard_map.324 = (bf16[1024,192]{1,0:T(8,128)(2,1)S(1)}, bf16[1024,256]{1,0:T(8,128)(2,1)S(1)}, bf16[1024,64]{1,0:T(8,128)(2,1)S(1)}) custom-call(s32[1,2]{1,0:T(1,128)S(1)} %copy-done.90, bf16[1024,128]{1,0:T(8,128)(2,1)S(1)} %copy-done.26, bf16[1024,64]{1,0:T(8,128)(2,1)S(1)} %copy-done.24, bf16[1024,128]{1,0:T(8,128)(2,1)S(1)} %copy-done.45, ...), custom_call_target="tpu_custom_call" | custom-call | flops 1 | bytes 1 | tf_op jit(solution)/shard_map/pallas_call | solution.py:239
  392.1 9.5 %collective-permute-done.46 = bf16[128,2688]{1,0:T(8,128)(2,1)S(1)} collective-permute-done((bf16[128,2688]{1,0:T(8,128)(2,1)S(1)}, bf16[128,2688]{1,0:T(8,128)(2,1)S(1)}, u32[]{:S(2)}, u32[]{:S(2)}) %collective-permute-start.46) | collective-permute-done | bytes 688160 | tf_op jit(solution)/shard_map/ppermute | solution.py:76
  407.8 6.8 %collective-permute-done.51.refs_4_ = bf16[352,2048]{1,0:T(8,128)(2,1)S(1)} collective-permute-done((bf16[352,2048]{1,0:T(8,128)(2,1)S(1)}, bf16[352,2048]{1,0:T(8,128)(2,1)S(1)}, u32[]{:S(2)}, u32[]{:S(2)}) %collective-permute-start.51) | collective-permute-done | bytes 1441824 | tf_op jit(solution)/shard_map/ppermute | solution.py:83
  416.2 8.4 %collective-permute-done.49 = bf16[128,2688]{1,0:T(8,128)(2,1)S(1)} collective-permute-done((bf16[128,2688]{1,0:T(8,128)(2,1)S(1)}, bf16[128,2688]{1,0:T(8,128)(2,1)S(1)}, u32[]{:S(2)}, u32[]{:S(2)}) %collective-permute-start.49) | collective-permute-done | bytes 688160 | tf_op jit(solution)/shard_map/ppermute | solution.py:76
  429.3 12.0 %collective-permute-done.55 = bf16[528,256]{1,0:T(8,128)(2,1)S(1)} collective-permute-done((bf16[528,256]{1,0:T(8,128)(2,1)S(1)}, bf16[528,256]{1,0:T(8,128)(2,1)S(1)}, u32[]{:S(2)}, u32[]{:S(2)}) %collective-permute-start.55) | collective-permute-done | bytes 270368 | tf_op jit(solution)/shard_map/ppermute | solution.py:129
  458.6 7.3 %collective-permute-done.57.refs_3_ = bf16[128,2688]{1,0:T(8,128)(2,1)S(1)} collective-permute-done((bf16[128,2688]{1,0:T(8,128)(2,1)S(1)}, bf16[128,2688]{1,0:T(8,128)(2,1)S(1)}, u32[]{:S(2)}, u32[]{:S(2)}) %collective-permute-start.57) | collective-permute-done | bytes 688160 | tf_op jit(solution)/shard_map/ppermute | solution.py:76
  470.4 8.2 %collective-permute-done.60 = bf16[400,256]{1,0:T(8,128)(2,1)S(1)} collective-permute-done((bf16[400,256]{1,0:T(8,128)(2,1)S(1)}, bf16[400,256]{1,0:T(8,128)(2,1)S(1)}, u32[]{:S(2)}, u32[]{:S(2)}) %collective-permute-start.60) | collective-permute-done | bytes 204832 | tf_op jit(solution)/shard_map/ppermute | solution.py:83
  483.0 13.4 %collective-permute-start.64 = (bf16[512,2688]{1,0:T(8,128)(2,1)S(1)}, bf16[512,2688]{1,0:T(8,128)(2,1)}, u32[]{:S(2)}, u32[]{:S(2)}) collective-permute-start(bf16[512,2688]{1,0:T(8,128)(2,1)S(1)} %shard_map.330.a), channel_id=1, source_target_pairs={{1,0},{0,1},{3,2},{2,3},{5,4},{4,5},{7,6},{6,7},{9,8},{8,9},{11,10... | collective-permute-start | bytes 8257544 | tf_op jit(solution)/shard_map/ppermute | solution.py:76
  504.9 7.3 %collective-permute-done.66 = bf16[528,512]{1,0:T(8,128)(2,1)} collective-permute-done((bf16[528,512]{1,0:T(8,128)(2,1)}, bf16[528,512]{1,0:T(8,128)(2,1)}, u32[]{:S(2)}, u32[]{:S(2)}) %collective-permute-start.66) | collective-permute-done | bytes 540704 | tf_op jit(solution)/shard_map/ppermute | solution.py:83
  528.7 5.7 shard_map.332
  537.1 8.1 %collective-permute-done.72.refs_2_ = bf16[400,512]{1,0:T(8,128)(2,1)} collective-permute-done((bf16[400,512]{1,0:T(8,128)(2,1)S(1)}, bf16[400,512]{1,0:T(8,128)(2,1)}, u32[]{:S(2)}, u32[]{:S(2)}) %collective-permute-start.72) | collective-permute-done | bytes 409632 | tf_op jit(solution)/shard_map/ppermute | solution.py:83
  560.9 4.6 shard_map.334
  567.7 3.9 shard_map.335
  (512 shorter events, 260.8 us)
Async XLA Ops:
  7.2 177.1 %all-gather.2.cloned.1.call-start = ((), (), s32[]{:S(2)}) async-start(), calls=%async_computation.1 | async-start | bytes 4456448 | tf_op jit(solution)/shard_map/all_gather | solution.py:737
  44.1 32.3 %collective-permute-start.9 = (bf16[352,2048]{1,0:T(8,128)(2,1)}, bf16[352,2048]{1,0:T(8,128)(2,1)}, u32[]{:S(2)}, u32[]{:S(2)}) collective-permute-start(bf16[352,2048]{1,0:T(8,128)(2,1)} %pad_maximum_fusion.1.refs_2_), channel_id=1, source_target_pairs={{96,0},{112,16},{0,32},{16,48},{32,64},{48,80},{64,96},{80,112},{9... | collective-permute-start | bytes 4325384 | tf_op jit(solution)/shard_map/ppermute | solution.py:83
  45.3 31.1 %collective-permute-start.8 = (bf16[352,2048]{1,0:T(8,128)(2,1)}, bf16[352,2048]{1,0:T(8,128)(2,1)}, u32[]{:S(2)}, u32[]{:S(2)}) collective-permute-start(bf16[352,2048]{1,0:T(8,128)(2,1)} %pad_maximum_fusion.1.refs_2_), channel_id=1, source_target_pairs={{32,0},{48,16},{64,32},{80,48},{96,64},{112,80},{0,96},{16,112},{3... | collective-permute-start | bytes 4325384 | tf_op jit(solution)/shard_map/ppermute | solution.py:83
  46.8 33.3 %collective-permute-start.7 = (bf16[352,2048]{1,0:T(8,128)(2,1)}, bf16[352,2048]{1,0:T(8,128)(2,1)}, u32[]{:S(2)}, u32[]{:S(2)}) collective-permute-start(bf16[352,2048]{1,0:T(8,128)(2,1)} %pad_maximum_fusion.1.refs_2_), channel_id=1, source_target_pairs={{16,0},{0,16},{48,32},{32,48},{80,64},{64,80},{112,96},{96,112},{1... | collective-permute-start | bytes 4325384 | tf_op jit(solution)/shard_map/ppermute | solution.py:83
  51.9 450.5 %reduce-scatter.2.cloned.1.call-start = ((), (), s32[]{:S(2)}) async-start(), calls=%async_computation.2 | async-start | bytes 4456448 | tf_op jit(solution)/shard_map/reduce_scatter | solution.py:853
  86.9 38.7 %collective-permute-start.15 = (bf16[352,2048]{1,0:T(8,128)(2,1)}, bf16[352,2048]{1,0:T(8,128)(2,1)}, u32[]{:S(2)}, u32[]{:S(2)}) collective-permute-start(bf16[352,2048]{1,0:T(8,128)(2,1)} %collective-permute-done.8.refs_4_), channel_id=1, source_target_pairs={{16,0},{0,16},{48,32},{32,48},{80,64},{64,80},{112,96},{96,112},{1... | collective-permute-start | bytes 4325384 | tf_op jit(solution)/shard_map/ppermute | solution.py:83
  89.1 19.0 %collective-permute-start.13 = (bf16[176,2048]{1,0:T(8,128)(2,1)}, bf16[176,2048]{1,0:T(8,128)(2,1)}, u32[]{:S(2)}, u32[]{:S(2)}) collective-permute-start(bf16[176,2048]{1,0:T(8,128)(2,1)} %bitcast.19.refs_3_), channel_id=1, source_target_pairs={{96,0},{112,16},{0,32},{16,48},{32,64},{48,80},{64,96},{80,112},{9... | collective-permute-start | bytes 2162696 | tf_op jit(solution)/shard_map/ppermute | solution.py:83
  109.1 42.1 %collective-permute-start.19 = (bf16[352,2048]{1,0:T(8,128)(2,1)}, bf16[352,2048]{1,0:T(8,128)(2,1)}, u32[]{:S(2)}, u32[]{:S(2)}) collective-permute-start(bf16[352,2048]{1,0:T(8,128)(2,1)} %pad_maximum_fusion.1.refs_2_), channel_id=1, source_target_pairs={{64,0},{80,16},{96,32},{112,48},{0,64},{16,80},{32,96},{48,112},{6... | collective-permute-start | bytes 4325384 | tf_op jit(solution)/shard_map/ppermute | solution.py:83
  178.8 52.3 %collective-permute-start.24 = (bf16[352,2048]{1,0:T(8,128)(2,1)}, bf16[352,2048]{1,0:T(8,128)(2,1)}, u32[]{:S(2)}, u32[]{:S(2)}) collective-permute-start(bf16[352,2048]{1,0:T(8,128)(2,1)} %collective-permute-done.9.refs_6_), channel_id=1, source_target_pairs={{16,0},{0,16},{48,32},{32,48},{80,64},{64,80},{112,96},{96,112},{1... | collective-permute-start | bytes 4325384 | tf_op jit(solution)/shard_map/ppermute | solution.py:83
  178.8 52.3 %collective-permute-start.26 = (bf16[352,2048]{1,0:T(8,128)(2,1)}, bf16[352,2048]{1,0:T(8,128)(2,1)}, u32[]{:S(2)}, u32[]{:S(2)}) collective-permute-start(bf16[352,2048]{1,0:T(8,128)(2,1)} %collective-permute-done.7.refs_8_), channel_id=1, source_target_pairs={{64,0},{80,16},{96,32},{112,48},{0,64},{16,80},{32,96},{48,112},{6... | collective-permute-start | bytes 4325384 | tf_op jit(solution)/shard_map/ppermute | solution.py:83
  180.1 50.9 %collective-permute-start.25 = (bf16[176,2048]{1,0:T(8,128)(2,1)}, bf16[176,2048]{1,0:T(8,128)(2,1)}, u32[]{:S(2)}, u32[]{:S(2)}) collective-permute-start(bf16[176,2048]{1,0:T(8,128)(2,1)} %collective-permute-done.13.refs_7_), channel_id=1, source_target_pairs={{16,0},{0,16},{48,32},{32,48},{80,64},{64,80},{112,96},{96,112},{1... | collective-permute-start | bytes 2162696 | tf_op jit(solution)/shard_map/ppermute | solution.py:83
  182.0 49.1 %collective-permute-start.27 = (bf16[176,2048]{1,0:T(8,128)(2,1)}, bf16[176,2048]{1,0:T(8,128)(2,1)}, u32[]{:S(2)}, u32[]{:S(2)}) collective-permute-start(bf16[176,2048]{1,0:T(8,128)(2,1)} %collective-permute-done.5.refs_9_), channel_id=1, source_target_pairs={{64,0},{80,16},{96,32},{112,48},{0,64},{16,80},{32,96},{48,112},{6... | collective-permute-start | bytes 2162696 | tf_op jit(solution)/shard_map/ppermute | solution.py:83
  231.1 27.7 %collective-permute-start.28 = (bf16[528,1024]{1,0:T(8,128)(2,1)}, bf16[528,1024]{1,0:T(8,128)(2,1)S(1)}, u32[]{:S(2)}, u32[]{:S(2)}) collective-permute-start(bf16[528,1024]{1,0:T(8,128)(2,1)} %get-tuple-element.404), channel_id=1, source_target_pairs={{16,0},{0,16},{48,32},{32,48},{80,64},{64,80},{112,96},{96,112},{1... | collective-permute-start | bytes 3244040 | tf_op jit(solution)/shard_map/ppermute | solution.py:83
  263.7 35.0 %collective-permute-start.33 = (bf16[352,2048]{1,0:T(8,128)(2,1)}, bf16[352,2048]{1,0:T(8,128)(2,1)}, u32[]{:S(2)}, u32[]{:S(2)}) collective-permute-start(bf16[352,2048]{1,0:T(8,128)(2,1)} %get-tuple-element.432), channel_id=1, source_target_pairs={{64,0},{80,16},{96,32},{112,48},{0,64},{16,80},{32,96},{48,112},{6... | collective-permute-start | bytes 4325384 | tf_op jit(solution)/shard_map/ppermute | solution.py:83
  265.2 33.6 %collective-permute-start.34 = (bf16[352,2048]{1,0:T(8,128)(2,1)}, bf16[352,2048]{1,0:T(8,128)(2,1)}, u32[]{:S(2)}, u32[]{:S(2)}) collective-permute-start(bf16[352,2048]{1,0:T(8,128)(2,1)} %get-tuple-element.433), channel_id=1, source_target_pairs={{16,0},{0,16},{48,32},{32,48},{80,64},{64,80},{112,96},{96,112},{1... | collective-permute-start | bytes 4325384 | tf_op jit(solution)/shard_map/ppermute | solution.py:83
  288.8 25.3 %collective-permute-start.36 = (bf16[176,2048]{1,0:T(8,128)(2,1)S(1)}, bf16[176,2048]{1,0:T(8,128)(2,1)S(1)}, u32[]{:S(2)}, u32[]{:S(2)}) collective-permute-start(bf16[176,2048]{1,0:T(8,128)(2,1)S(1)} %copy-done.128), channel_id=1, source_target_pairs={{64,0},{80,16},{96,32},{112,48},{0,64},{16,80},{32,96},{48,112},{6... | collective-permute-start | bytes 2162696 | tf_op jit(solution)/shard_map/ppermute | solution.py:83
  304.6 40.7 %collective-permute-start.40 = (bf16[352,2048]{1,0:T(8,128)(2,1)S(1)}, bf16[352,2048]{1,0:T(8,128)(2,1)S(1)}, u32[]{:S(2)}, u32[]{:S(2)}) collective-permute-start(bf16[352,2048]{1,0:T(8,128)(2,1)S(1)} %copy-done.127), channel_id=1, source_target_pairs={{16,0},{0,16},{48,32},{32,48},{80,64},{64,80},{112,96},{96,112},{1... | collective-permute-start | bytes 4325384 | tf_op jit(solution)/shard_map/ppermute | solution.py:83
  305.7 39.6 %collective-permute-start.41 = (bf16[352,2048]{1,0:T(8,128)(2,1)S(1)}, bf16[352,2048]{1,0:T(8,128)(2,1)S(1)}, u32[]{:S(2)}, u32[]{:S(2)}) collective-permute-start(bf16[352,2048]{1,0:T(8,128)(2,1)S(1)} %copy-done.126), channel_id=1, source_target_pairs={{64,0},{80,16},{96,32},{112,48},{0,64},{16,80},{32,96},{48,112},{6... | collective-permute-start | bytes 4325384 | tf_op jit(solution)/shard_map/ppermute | solution.py:83
  352.1 19.3 %collective-permute-start.43 = (bf16[176,2048]{1,0:T(8,128)(2,1)S(1)}, bf16[176,2048]{1,0:T(8,128)(2,1)S(1)}, u32[]{:S(2)}, u32[]{:S(2)}) collective-permute-start(bf16[176,2048]{1,0:T(8,128)(2,1)S(1)} %copy-done.96), channel_id=1, source_target_pairs={{64,0},{80,16},{96,32},{112,48},{0,64},{16,80},{32,96},{48,112},{6... | collective-permute-start | bytes 2162696 | tf_op jit(solution)/shard_map/ppermute | solution.py:83
  379.2 35.4 %collective-permute-start.51 = (bf16[352,2048]{1,0:T(8,128)(2,1)S(1)}, bf16[352,2048]{1,0:T(8,128)(2,1)S(1)}, u32[]{:S(2)}, u32[]{:S(2)}) collective-permute-start(bf16[352,2048]{1,0:T(8,128)(2,1)S(1)} %copy-done.108), channel_id=1, source_target_pairs={{16,0},{0,16},{48,32},{32,48},{80,64},{64,80},{112,96},{96,112},{1... | collective-permute-start | bytes 4325384 | tf_op jit(solution)/shard_map/ppermute | solution.py:83
  390.2 24.4 %collective-permute-start.50 = (bf16[400,1024]{1,0:T(8,128)(2,1)S(1)}, bf16[400,1024]{1,0:T(8,128)(2,1)S(1)}, u32[]{:S(2)}, u32[]{:S(2)}) collective-permute-start(bf16[400,1024]{1,0:T(8,128)(2,1)S(1)} %get-tuple-element.602), channel_id=1, source_target_pairs={{64,0},{80,16},{96,32},{112,48},{0,64},{16,80},{32,96},{48,112},{6... | collective-permute-start | bytes 2457608 | tf_op jit(solution)/shard_map/ppermute | solution.py:83
  403.0 21.6 %collective-permute-start.49 = (bf16[128,2688]{1,0:T(8,128)(2,1)S(1)}, bf16[128,2688]{1,0:T(8,128)(2,1)S(1)}, u32[]{:S(2)}, u32[]{:S(2)}) collective-permute-start(bf16[128,2688]{1,0:T(8,128)(2,1)S(1)} %get-tuple-element.503), channel_id=1, source_target_pairs={{4,0},{5,1},{6,2},{7,3},{0,4},{1,5},{2,6},{3,7},{12,8},{13,9},{14,... | collective-permute-start | bytes 2064392 | tf_op jit(solution)/shard_map/ppermute | solution.py:76
  442.3 23.6 %collective-permute-start.58 = (bf16[176,2048]{1,0:T(8,128)(2,1)}, bf16[176,2048]{1,0:T(8,128)(2,1)}, u32[]{:S(2)}, u32[]{:S(2)}) collective-permute-start(bf16[176,2048]{1,0:T(8,128)(2,1)} %get-tuple-element.534), channel_id=1, source_target_pairs={{16,0},{0,16},{48,32},{32,48},{80,64},{64,80},{112,96},{96,112},{1... | collective-permute-start | bytes 2162696 | tf_op jit(solution)/shard_map/ppermute | solution.py:83
  442.4 37.2 %collective-permute-start.62 = (bf16[352,2048]{1,0:T(8,128)(2,1)}, bf16[352,2048]{1,0:T(8,128)(2,1)S(1)}, u32[]{:S(2)}, u32[]{:S(2)}) collective-permute-start(bf16[352,2048]{1,0:T(8,128)(2,1)} %add_convert_fusion.1), channel_id=1, source_target_pairs={{96,0},{112,16},{0,32},{16,48},{32,64},{48,80},{64,96},{80,112},{9... | collective-permute-start | bytes 4325384 | tf_op jit(solution)/shard_map/ppermute | solution.py:83
  443.7 37.0 %collective-permute-start.63 = (bf16[352,2048]{1,0:T(8,128)(2,1)}, bf16[352,2048]{1,0:T(8,128)(2,1)}, u32[]{:S(2)}, u32[]{:S(2)}) collective-permute-start(bf16[352,2048]{1,0:T(8,128)(2,1)} %add_convert_fusion), channel_id=1, source_target_pairs={{32,0},{48,16},{64,32},{80,48},{96,64},{112,80},{0,96},{16,112},{3... | collective-permute-start | bytes 4325384 | tf_op jit(solution)/shard_map/ppermute | solution.py:83
  483.0 29.2 %collective-permute-start.64 = (bf16[512,2688]{1,0:T(8,128)(2,1)S(1)}, bf16[512,2688]{1,0:T(8,128)(2,1)}, u32[]{:S(2)}, u32[]{:S(2)}) collective-permute-start(bf16[512,2688]{1,0:T(8,128)(2,1)S(1)} %shard_map.330.a), channel_id=1, source_target_pairs={{1,0},{0,1},{3,2},{2,3},{5,4},{4,5},{7,6},{6,7},{9,8},{8,9},{11,10... | collective-permute-start | bytes 8257544 | tf_op jit(solution)/shard_map/ppermute | solution.py:76
  499.6 28.4 %collective-permute-start.68 = (bf16[176,2048]{1,0:T(8,128)(2,1)}, bf16[176,2048]{1,0:T(8,128)(2,1)}, u32[]{:S(2)}, u32[]{:S(2)}) collective-permute-start(bf16[176,2048]{1,0:T(8,128)(2,1)} %add_convert_fusion.6), channel_id=1, source_target_pairs={{96,0},{112,16},{0,32},{16,48},{32,64},{48,80},{64,96},{80,112},{9... | collective-permute-start | bytes 2162696 | tf_op jit(solution)/shard_map/ppermute | solution.py:83
  500.0 28.0 %collective-permute-start.69 = (bf16[176,2048]{1,0:T(8,128)(2,1)}, bf16[176,2048]{1,0:T(8,128)(2,1)}, u32[]{:S(2)}, u32[]{:S(2)}) collective-permute-start(bf16[176,2048]{1,0:T(8,128)(2,1)} %add_convert_fusion.5), channel_id=1, source_target_pairs={{32,0},{48,16},{64,32},{80,48},{96,64},{112,80},{0,96},{16,112},{3... | collective-permute-start | bytes 2162696 | tf_op jit(solution)/shard_map/ppermute | solution.py:83
  520.2 25.0 %collective-permute-start.72 = (bf16[400,512]{1,0:T(8,128)(2,1)S(1)}, bf16[400,512]{1,0:T(8,128)(2,1)}, u32[]{:S(2)}, u32[]{:S(2)}) collective-permute-start(bf16[400,512]{1,0:T(8,128)(2,1)S(1)} %constant_dynamic-update-slice_fusion.2.refs_0_), channel_id=1, source_target_pairs={{64,0},{80,16},{96,32},{112,48},{0,64},{16,80},{32,96},{48,112},{6... | collective-permute-start | bytes 1228808 | tf_op jit(solution)/shard_map/ppermute | solution.py:83
  524.4 20.8 %collective-permute-start.71 = (bf16[400,512]{1,0:T(8,128)(2,1)S(1)}, bf16[400,512]{1,0:T(8,128)(2,1)}, u32[]{:S(2)}, u32[]{:S(2)}) collective-permute-start(bf16[400,512]{1,0:T(8,128)(2,1)S(1)} %constant_dynamic-update-slice_fusion.2.refs_0_), channel_id=1, source_target_pairs={{32,0},{48,16},{64,32},{80,48},{96,64},{112,80},{0,96},{16,112},{3... | collective-permute-start | bytes 1228808 | tf_op jit(solution)/shard_map/ppermute | solution.py:83
  528.0 20.8 %collective-permute-start.70 = (bf16[64,2048]{1,0:T(8,128)(2,1)}, bf16[64,2048]{1,0:T(8,128)(2,1)}, u32[]{:S(2)}, u32[]{:S(2)}) collective-permute-start(bf16[64,2048]{1,0:T(8,128)(2,1)} %add_convert_fusion.17), channel_id=1, source_target_pairs={{0,32},{16,48},{32,0},{48,16},{64,96},{80,112},{96,64},{112,80},{1... | collective-permute-start | bytes 786440 | tf_op jit(solution)/shard_map/ppermute | solution.py:129
  534.5 31.2 %collective-permute-start.75 = (bf16[528,1024]{1,0:T(8,128)(2,1)}, bf16[528,1024]{1,0:T(8,128)(2,1)}, u32[]{:S(2)}, u32[]{:S(2)}) collective-permute-start(bf16[528,1024]{1,0:T(8,128)(2,1)} %pad_maximum_fusion.3.a), channel_id=1, source_target_pairs={{16,0},{0,16},{48,32},{32,48},{80,64},{64,80},{112,96},{96,112},{1... | collective-permute-start | bytes 3244040 | tf_op jit(solution)/shard_map/ppermute | solution.py:83
  (175 other events, 1517.9 us)
Sparse Core Ops, SparseCore 0:
  52.0 76.4 all-gather.1
  374.1 82.1 reduce-scatter.1
